TPU v7x, 256 devices: a whole 4x4x8 slice. The times are simulated.
256 devices in a mesh: slot: 16 (over z, core), hid: 16 (over y, x).
Axes of the slice: x: 4, y: 4, z: 8, core: 2. Of those that a mesh axis runs over, the one named last changes fastest.
Arguments:
- cotangent: bfloat16 [32768, 2048], P('slot', 'hid'), may hold values from -6 to 6
- hidden: bfloat16 [32768, 8192], P('slot', 'hid'), may hold values from -6 to 6
- weights: bfloat16 [16, 8192, 2048], P('slot', 'hid'), may hold values from -0.125 to 0.125
- slot_experts: int32 [16, 1], replicated, may hold values from 0 to 3
- next_experts: int32 [16, 1], replicated, may hold values from 0 to 3
- row_counts: int32 [16], replicated, may hold values from 1 to 2048, 20480 in all
- master: float32 [4, 8192, 2048], P(None, 'hid', 'slot'), may hold values from -3 to 3
- momentum: float32 [4, 8192, 2048], P(None, 'hid', 'slot'), may hold values from -96 to 96
Outputs:
- input_grad: bfloat16 [32768, 8192], P('slot', 'hid')
- new_momentum: float32 [4, 8192, 2048], P(None, 'hid', 'slot')
- new_master: float32 [4, 8192, 2048], P(None, 'hid', 'slot')
- placed: bfloat16 [16, 8192, 2048], P('slot', 'hid')
Inputs may be any that keep to these rules, and one draw needn't show every extreme that they name: `slot_experts`: every expert 0 to 3 is held by at least one slot. `next_experts`: every expert 0 to 3 is held by at least one slot. `row_counts`: the counts sum to 20480.
All inputs are finite; a program needn't handle non-finite values.
Results may differ from a plain program's by a relative error of at most 0.015.
Values may be sent and summed in bfloat16 or wider, within the bound.
No kernel may reach another device: no remote copies, remote signals or barrier semaphores. Data moves between devices by JAX's collectives and lax.ppermute only.
A program may use at most 128 MiB of HBM per device.

v0:
```python
import jax
import jax.numpy as jnp
from jax import lax
from jax.sharding import PartitionSpec as P

momentum_decay = 0.9
learn_rate = 0.01


def local(cotangent, hidden, weights, slot_experts, next_experts, row_counts, master, momentum):
    row_span = hidden.shape[0]
    own_slot = lax.axis_index("slot")
    live_count = lax.dynamic_index_in_dim(row_counts, own_slot, 0, keepdims=False)
    live_mask = (jnp.arange(row_span, dtype=jnp.int32) < live_count)[:, None].astype(
        cotangent.dtype
    )
    masked = cotangent * live_mask
    weight_rows = weights[0]
    shard_piece = lax.all_gather(masked, "hid", axis=1, tiled=True)
    hid_grad = lax.dot_general(
        shard_piece, weight_rows, (((1,), (1,)), ((), ())), preferred_element_type=jnp.float32
    )
    w_part = lax.dot_general(
        hidden, shard_piece, (((0,), (0,)), ((), ())), preferred_element_type=jnp.float32
    )
    w_grad = w_part
    hid_grad, w_grad = (hid_grad, w_grad)
    input_grad = hid_grad.astype(jnp.bfloat16)
    expert_count = master.shape[0]
    owners = (
        slot_experts[:, 0][None, :] == jnp.arange(expert_count, dtype=jnp.int32)[:, None]
    ).astype(jnp.float32)
    own_weight = lax.dynamic_index_in_dim(owners, own_slot, 1, keepdims=False)
    stacked = own_weight[:, None, None] * w_grad[None]
    expert_grad = lax.psum_scatter(
        stacked.astype(jnp.bfloat16), "slot", scatter_dimension=2, tiled=True
    ).astype(jnp.float32)
    new_momentum = momentum_decay * momentum + expert_grad
    new_master = master - learn_rate * new_momentum
    rounded = new_master.astype(jnp.bfloat16)
    gathered = lax.all_gather(rounded, "slot", axis=2, tiled=True)
    target = lax.dynamic_index_in_dim(next_experts[:, 0], own_slot, 0, keepdims=False)
    placed = lax.dynamic_index_in_dim(gathered, target, 0, keepdims=True)
    return (input_grad, new_momentum, new_master, placed)


def solution(mesh):
    return jax.shard_map(
        local,
        mesh=mesh,
        in_specs=(
            P("slot", "hid"),
            P("slot", "hid"),
            P("slot", "hid", None),
            P(),
            P(),
            P(),
            P(None, "hid", "slot"),
            P(None, "hid", "slot"),
        ),
        out_specs=(
            P("slot", "hid"),
            P(None, "hid", "slot"),
            P(None, "hid", "slot"),
            P("slot", "hid", None),
        ),
        check_vma=False,
    )
```

profile of v0, /device:TPU:1, one launch (start us, length us, event | category | flops | bytes accessed | tf_op | source)
XLA Modules:
  0.0 297.3 jit_solution(14528464055429409936)
XLA Ops:
  7.2 0.0 copy-start
  7.2 0.0 all-gather.3.cloned.1.call-start
  7.2 1.4 dynamic_slice.15
  8.6 0.6 fusion.1
  9.3 2.2 broadcast_multiply_fusion
  11.4 0.0 all-gather.3.cloned.1.call-update
  11.5 0.0 reduce-scatter.4.cloned.1.call-start
  11.5 1.2 dynamic-slice.1
  12.8 0.6 fusion.2
  13.4 84.5 %all-gather.3.cloned.1.call-done = bf16[2048,2048]{1,0:T(8,128)(2,1)} async-done(((bf16[2048,128]{1,0:T(8,128)(2,1)}), bf16[2048,2048]{1,0:T(8,128)(2,1)}) %all-gather.3.cloned.1.call-update) | async-done | bytes 8388624 | tf_op jit(solution)/shard_map/all_gather | solution.py:19
  97.9 0.0 copy-done
  97.9 9.8 %convolution_bitcast_fusion = f32[512,2048]{0,1:T(8,128)} fusion(bf16[2048,2048]{1,0:T(8,128)(2,1)} %all-gather.3.cloned.1.call-done, bf16[2048,512]{1,0:T(8,128)(2,1)S(1)} %copy-done), kind=kOutput, calls=%fused_computation.1 | convolution fusion | flops 4294967296 | bytes 14680064 | tf_op jit(solution)/shard_map/dot_general | solution.py:23
  107.7 5.5 %copy.13 = f32[512,2048]{1,0:T(8,128)} copy(f32[512,2048]{0,1:T(8,128)} %convolution_bitcast_fusion) | data formatting | bytes 8388608 | tf_op jit(solution)/shard_map/dot_general | solution.py:23
  113.1 8.0 %multiply_convert_fusion = bf16[4,512,2048]{2,1,0:T(8,128)(2,1)} fusion(f32[512,2048]{1,0:T(8,128)} %copy.13, f32[4]{0:T(128)S(1)} %fusion.2), kind=kLoop, calls=%fused_computation | loop fusion | flops 8388608 | bytes 12582928 | tf_op jit(solution)/shard_map/convert_element_type | solution.py:36
  121.1 14.6 %copy.14 = bf16[4,512,2048]{1,0,2:T(4,128)(2,1)} copy(bf16[4,512,2048]{2,1,0:T(8,128)(2,1)} %multiply_convert_fusion) | data formatting | bytes 16777216
  135.7 10.2 %copy.16 = bf16[256,8,4,512]{3,1,2,0:T(8,128)(2,1)} copy(bf16[256,8,4,512]{3,2,1,0:T(4,128)(2,1)} %bitcast.18) | data formatting | bytes 16777216
  146.0 0.0 reduce-scatter.4.cloned.1.call-update
  146.0 0.0 copy-start.1
  146.0 0.2 all-gather.5.cloned.1.call-start
  146.2 68.0 %reduce-scatter.4.cloned.1.call-done = bf16[128,2048]{1,0:T(8,128)(2,1)} async-done(((bf16[2048,2048]{1,0:T(8,128)(2,1)}), bf16[128,2048]{1,0:T(8,128)(2,1)}) %reduce-scatter.4.cloned.1.call-update) | async-done | bytes 524304
  214.3 1.4 reshape.21
  215.7 0.4 copy.15
  216.1 3.2 %fusion.3 = (bf16[4,512,128]{2,1,0:T(8,128)(2,1)}, f32[4,512,128]{2,1,0:T(8,128)}, f32[4,512,128]{2,1,0:T(8,128)}) fusion(f32[4,512,128]{2,1,0:T(8,128)} %param.14, bf16[4,512,128]{2,1,0:T(8,128)(2,1)S(1)} %copy.15, f32[4,512,128]{2,1,0:T(8,128)} %param.15), kind=kLoop, calls=%fused_computation.13 | loop fusion | flops 1572864 | bytes 5242880 | tf_op jit(solution)/shard_map/convert_element_type | solution.py:40
  219.4 0.0 all-gather.5.cloned.1.call-update
  219.4 0.0 copy-done.1
  219.4 0.6 constant_dynamic-slice_fusion
  221.9 9.9 %convolution_convert_fusion = bf16[2048,512]{1,0:T(8,128)(2,1)} fusion(bf16[2048,2048]{1,0:T(8,128)(2,1)} %all-gather.3.cloned.1.call-done, bf16[1,512,2048]{2,1,0:T(8,128)(2,1)} %param.10), kind=kOutput, calls=%fused_computation.2 | convolution fusion | flops 4296015872 | bytes 12582912 | tf_op jit(solution)/shard_map/dot_general | solution.py:20
  231.8 55.9 %all-gather.5.cloned.1.call-done = bf16[4,512,2048]{2,1,0:T(8,128)(2,1)} async-done(((bf16[4,512,128]{2,1,0:T(8,128)(2,1)}), bf16[4,512,2048]{2,1,0:T(8,128)(2,1)}) %all-gather.5.cloned.1.call-update) | async-done | bytes 8388624 | tf_op jit(solution)/shard_map/all_gather | solution.py:41
  287.6 3.2 %constant_dynamic-slice_fusion.1 = bf16[1,512,2048]{2,1,0:T(8,128)(2,1)} fusion(bf16[4,512,2048]{2,1,0:T(8,128)(2,1)} %all-gather.5.cloned.1.call-done, s32[]{:T(128)S(6)} %select_n.12), kind=kLoop, calls=%fused_computation.12 | loop fusion | bytes 4194308 | tf_op jit(solution)/shard_map/jit(dynamic_index_in_dim)/dynamic_slice | solution.py:43
Async XLA Ops:
  7.2 90.8 %copy-start = (bf16[2048,512]{1,0:T(8,128)(2,1)S(1)}, bf16[2048,512]{1,0:T(8,128)(2,1)}, u32[]{:S(2)}) copy-start(bf16[2048,512]{1,0:T(8,128)(2,1)} %param.9) | copy-start | bytes 6291460
  7.2 90.7 %all-gather.3.cloned.1.call-start = ((), (), s32[]{:S(2)}) async-start(), calls=%async_computation.1 | async-start | bytes 8912896 | tf_op jit(solution)/shard_map/all_gather | solution.py:19
  11.5 202.8 %reduce-scatter.4.cloned.1.call-start = ((), (), s32[]{:S(2)}) async-start(), calls=%async_computation.3 | async-start | bytes 8912896
  146.0 73.4 %copy-start.1 = (s32[16,1]{0,1:T(1,128)S(1)}, s32[16,1]{0,1:T(1,128)}, u32[]{:S(2)}) copy-start(s32[16,1]{0,1:T(1,128)} %param.12) | copy-start | bytes 196
  146.0 141.6 %all-gather.5.cloned.1.call-start = ((), (), s32[]{:S(2)}) async-start(), calls=%async_computation.2 | async-start | bytes 8912896 | tf_op jit(solution)/shard_map/all_gather | solution.py:41
Sparse Core Ops, SparseCore 0:
  11.6 86.2 all-gather.2
  146.1 68.1 reduce-scatter.3
  219.5 68.0 all-gather.4
where the time goes:
time: 298 us; the launch traced here: 297 us
  waiting for transfers between devices  208 us (70%)
  local copies, waits for them, and re-layouts  38.5 us (13%)
  matrix products  19.6 us (7%)
  between operations  15.7 us (5%)
  other arithmetic  14.7 us (5%)
    all_gather x1, waiting for transfers between devices, local(): shard_piece = lax.all_gather(masked, 'hid', axis=1, tiled=True)  84.5 us
    unnamed x4, waiting for transfers between devices  68.1 us
    all_gather x1, waiting for transfers between devices, local(): gathered = lax.all_gather(rounded, 'slot', axis=2, tiled=True)  55.9 us
    unnamed x8, local copies, waits for them, and re-layouts  26.7 us
    dot_general x1, matrix products, local(): lax.dot_general(shard_piece, weight_rows, (((1,), (1,)), ((), ())), prefe...  9.86 us
    dot_general x1, matrix products, local(): lax.dot_general(hidden, shard_piece, (((0,), (0,)), ((), ())), preferred_...  9.75 us
    convert_element_type x1, other arithmetic, local(): stacked.astype(jnp.bfloat16)  8 us
  transfers between devices with their start and end apart: 3, of which 3 were waited for; matrix products, arithmetic and copies ran while one was open for 4% of the time, Pallas kernels for 0%

commit v1 on v0

v1 whole, which is shorter than its diff:
```python
import functools

import jax
import jax.numpy as jnp
from jax import lax
from jax.experimental import pallas as pl
from jax.experimental.pallas import tpu as pltpu
from jax.sharding import PartitionSpec as P

momentum_decay = 0.9
learn_rate = 0.01
BOTH = ("slot", "hid")
CHUNKS = ((0, 128),)
VM = pl.BlockSpec(memory_space=pltpu.VMEM)
SM = pl.BlockSpec(memory_space=pltpu.SMEM)
ANY = pl.BlockSpec(memory_space=pl.ANY)
MIB = 1 << 20


def params(mib):
    return pltpu.CompilerParams(vmem_limit_bytes=mib * MIB)


def cost(flops, moved):
    return pl.CostEstimate(flops=flops, bytes_accessed=moved, transcendentals=0)


def position(z, core, y, x):
    return (z * 2 + core) * 16 + y * 4 + x


def line_groups():
    groups = []
    for z in range(8):
        for line in range(4):
            groups.append([position(z, 0, line, k) for k in range(4)])
            groups.append([position(z, 1, k, line) for k in range(4)])
    return groups


def cross_pairs(step):
    pairs = []
    for z in range(8):
        for y in range(4):
            for x in range(4):
                pairs.append((position(z, 0, y, x), position(z, 0, (y + step) % 4, x)))
                pairs.append((position(z, 1, y, x), position(z, 1, y, (x + step) % 4)))
    return pairs


def mask_kernel(live_ref, cot_ref, *out_refs):
    rows = cot_ref.shape[0]
    live = lax.broadcasted_iota(jnp.int32, cot_ref.shape, 0) < live_ref[0]
    turned = jnp.where(live, cot_ref[...], jnp.zeros_like(cot_ref)).T
    for (start, size), out_ref in zip(CHUNKS, out_refs):
        for k in range(4):
            out_ref[k] = turned[start : start + size, :rows]


def masked_chunks(live, cotangent):
    rows = cotangent.shape[0]
    return pl.pallas_call(
        mask_kernel,
        out_shape=[jax.ShapeDtypeStruct((4, size, rows), jnp.bfloat16) for _, size in CHUNKS],
        in_specs=[SM, VM],
        out_specs=[VM] * len(CHUNKS),
        compiler_params=params(32),
        cost_estimate=cost(0, 3 * MIB),
        name="mask_turn",
    )(live, cotangent)


def block_of(place_ref, group, k):
    at = lax.rem(place_ref[1] + group, 4)
    return jnp.where(place_ref[0] == 0, 4 * at + k, 4 * k + at)


def slot_grad_kernel(layout, place_ref, hidden_ref, *refs):
    piece_refs, out_ref = refs[: len(layout)], refs[-1]
    for i, (group, first) in enumerate(layout):
        count, size, rows = piece_refs[i].shape
        grad = jnp.dot(
            piece_refs[i][...].reshape(count * size, rows),
            hidden_ref[...],
            preferred_element_type=jnp.float32,
        ).astype(jnp.bfloat16)
        for k in range(count):
            out_ref[block_of(place_ref, group, first + k)] = grad[k * size : (k + 1) * size]


def slot_grad(place, hidden, pieces, layout):
    size = pieces[0].shape[1]
    width = hidden.shape[1]
    return pl.pallas_call(
        functools.partial(slot_grad_kernel, layout),
        out_shape=jax.ShapeDtypeStruct((16, size, width), jnp.bfloat16),
        in_specs=[SM, VM] + [VM] * len(pieces),
        out_specs=VM,
        compiler_params=params(48),
        cost_estimate=cost(2 * 16 * size * width * hidden.shape[0], 12 * MIB),
        name="slot_grad",
    )(place, hidden, *pieces)


def update_kernel(now_ref, next_ref, got_ref, mom_ref, mas_ref, new_mom_ref, new_mas_ref, send_ref, rounded):
    experts = mom_ref.shape[0]
    size = mom_ref.shape[1]
    step = 32

    def rows_of(i, carry):
        at = pl.ds(pl.multiple_of(i * step, step), step)
        for e in range(experts):
            total = jnp.zeros((step, mom_ref.shape[2]), jnp.float32)
            for s in range(got_ref.shape[0]):
                held = (now_ref[s] == e).astype(jnp.float32)
                total += held * got_ref[s, at].astype(jnp.float32)
            new_mom = momentum_decay * mom_ref[e, at] + total
            new_mas = mas_ref[e, at] - learn_rate * new_mom
            new_mom_ref[e, at] = new_mom
            new_mas_ref[e, at] = new_mas
            rounded[e, at] = new_mas.astype(jnp.bfloat16)
        return carry

    lax.fori_loop(0, size // step, rows_of, 0)
    for s in range(send_ref.shape[0]):
        send_ref[s] = rounded[next_ref[s]]


def update(now, following, got, mom, mas):
    return pl.pallas_call(
        update_kernel,
        out_shape=[
            jax.ShapeDtypeStruct(mom.shape, jnp.float32),
            jax.ShapeDtypeStruct(mom.shape, jnp.float32),
            jax.ShapeDtypeStruct(got.shape, jnp.bfloat16),
        ],
        in_specs=[SM, SM, VM, VM, VM],
        out_specs=[VM] * 3,
        scratch_shapes=[pltpu.VMEM(mom.shape, jnp.bfloat16)],
        compiler_params=params(32),
        cost_estimate=cost(0, 8 * MIB),
        name="momentum_step",
    )(now, following, got, mom, mas)


def input_grad_kernel(layouts, place_ref, weight_ref, *refs):
    out_ref = refs[-1]
    total = None
    for group in range(4):
        rows_of_group, columns = [], []
        for k in range(4):
            for chunk_layout, base in layouts:
                for i, (at, first, count) in enumerate(chunk_layout):
                    if at == group and first <= k < first + count:
                        rows_of_group.append(refs[base + i][k - first])
            start = pl.multiple_of(block_of(place_ref, group, k) * 128, 128)
            columns.append(weight_ref[:, pl.ds(start, 128)])
        left = jnp.concatenate(rows_of_group, axis=0).T
        right = jnp.concatenate(columns, axis=1)
        part = lax.dot_general(
            left, right, (((1,), (1,)), ((), ())), preferred_element_type=jnp.float32
        )
        total = part if total is None else total + part
    out_ref[...] = total.astype(jnp.bfloat16)


def input_gradient(place, weights, chunk_pieces, layout):
    tile = 512
    width = weights.shape[0]
    rows = chunk_pieces[0][0].shape[2]
    flat, layouts = [], []
    for pieces in chunk_pieces:
        layouts.append(
            (tuple((g, f, p.shape[0]) for (g, f), p in zip(layout, pieces)), len(flat))
        )
        flat.extend(pieces)
    return pl.pallas_call(
        functools.partial(input_grad_kernel, layouts),
        grid=(rows // tile,),
        out_shape=jax.ShapeDtypeStruct((rows, width), jnp.bfloat16),
        in_specs=[SM, VM]
        + [pl.BlockSpec((p.shape[0], p.shape[1], tile), lambda i: (0, 0, i)) for p in flat],
        out_specs=pl.BlockSpec((tile, width), lambda i: (i, 0)),
        compiler_params=params(48),
        cost_estimate=cost(2 * rows * width * weights.shape[1], 12 * MIB),
        name="input_grad",
    )(place, weights, *flat)


def placed_kernel(*refs):
    out_ref = refs[-1]
    for j in range(16):
        block = jnp.concatenate([ref[j] for ref in refs[:-1]], axis=0)
        out_ref[:, j * 128 : (j + 1) * 128] = block.T


def place_weights(parts):
    width = parts[0].shape[2]
    return pl.pallas_call(
        placed_kernel,
        out_shape=jax.ShapeDtypeStruct((width, 2048), jnp.bfloat16),
        in_specs=[VM] * len(parts),
        out_specs=VM,
        compiler_params=params(32),
        cost_estimate=cost(0, 4 * MIB),
        name="placed_turn",
    )(*parts)


LAYOUT = ((0, 0), (3, 0), (3, 2), (1, 0), (1, 2), (2, 0), (2, 2))


def gather_hid(replicated):
    own = lax.all_to_all(
        replicated, BOTH, 0, 0, tiled=True, axis_index_groups=line_groups()
    )
    low, high = own[:2], own[2:]
    up, down = cross_pairs(1), cross_pairs(3)
    below_low = lax.ppermute(low, BOTH, up)
    above_high = lax.ppermute(high, BOTH, down)
    below_high = lax.ppermute(high, BOTH, up)
    above_low = lax.ppermute(low, BOTH, down)
    far_low = lax.ppermute(below_low, BOTH, up)
    far_high = lax.ppermute(above_high, BOTH, down)
    return (own, below_low, below_high, above_low, above_high, far_low, far_high)


def local(cotangent, hidden, weights, slot_experts, next_experts, row_counts, master, momentum):
    slot = lax.axis_index("slot")
    hid = lax.axis_index("hid")
    core = slot % 2
    place = jnp.stack([core, jnp.where(core == 0, hid // 4, hid % 4)]).astype(jnp.int32)
    live = lax.dynamic_slice_in_dim(row_counts, slot, 1)
    now, following = slot_experts[:, 0], next_experts[:, 0]
    mom = jnp.swapaxes(momentum, 1, 2)
    mas = jnp.swapaxes(master, 1, 2)

    new_mom, new_mas, parts, chunk_pieces = [], [], [], []
    for (start, size), replicated in zip(CHUNKS, masked_chunks(live, cotangent)):
        pieces = gather_hid(replicated)
        grads = slot_grad(place, hidden, pieces, LAYOUT)
        got = lax.all_to_all(grads, "slot", 0, 0, tiled=True)
        a, b, send = update(
            now, following, got, mom[:, start : start + size], mas[:, start : start + size]
        )
        parts.append(lax.all_to_all(send, "slot", 0, 0, tiled=True))
        new_mom.append(a)
        new_mas.append(b)
        chunk_pieces.append(pieces)

    input_grad = input_gradient(place, weights[0], chunk_pieces, LAYOUT)
    placed = place_weights(parts)[None]
    new_momentum = jnp.swapaxes(jnp.concatenate(new_mom, axis=1), 1, 2)
    new_master = jnp.swapaxes(jnp.concatenate(new_mas, axis=1), 1, 2)
    return (input_grad, new_momentum, new_master, placed)


def solution(mesh):
    return jax.shard_map(
        local,
        mesh=mesh,
        in_specs=(
            P("slot", "hid"),
            P("slot", "hid"),
            P("slot", "hid", None),
            P(),
            P(),
            P(),
            P(None, "hid", "slot"),
            P(None, "hid", "slot"),
        ),
        out_specs=(
            P("slot", "hid"),
            P(None, "hid", "slot"),
            P(None, "hid", "slot"),
            P("slot", "hid", None),
        ),
        check_vma=False,
    )
```

time: 298 us -> 197 us (0.66)
  waiting for transfers between devices: 208 us -> 109 us
  starting transfers between devices: 0.3 us -> 24.5 us
  Pallas kernels: 0 us -> 22.8 us
  blocking collectives: 0 us -> 20.4 us
  matrix products: 19.6 us -> 0 us
  local copies, waits for them, and re-layouts: 38.5 us -> 19.5 us
  between operations: 15.7 us -> 0.73 us
  other arithmetic: 14.7 us -> 0.07 us
    all_gather x2 -> x0, waiting for transfers between devices: 140 us -> none  [the longest x1 84.5 us: local(): shard_piece = lax.all_gather(masked, 'hid', axis=1, tiled=True)]
    all_to_all x0 -> x2, waiting for transfers between devices: none -> 79 us  [the longest x1 44.8 us: local(): got = lax.all_to_all(grads, 'slot', 0, 0, tiled=True)]
    unnamed x4 -> x0, waiting for transfers between devices: 68.1 us -> none
    ppermute x0 -> x6, waiting for transfers between devices: none -> 29.8 us  [the longest x1 11.3 us: gather_hid(): far_low = lax.ppermute(below_low, BOTH, up)]
    pallas_call x0 -> x5, Pallas kernels: none -> 22.8 us  [the longest x1 8.91 us: slot_grad(): pl.pallas_call(functools.partial(slot_grad_kernel, layout), out_shape=jax...]
    all_to_all x0 -> x1, blocking collectives: none -> 20.4 us  [gather_hid(): lax.all_to_all(replicated, BOTH, 0, 0, tiled=True, axis_index_groups=line...]
    dot_general x2 -> x0, matrix products: 19.6 us -> none  [the longest x1 9.86 us: local(): lax.dot_general(shard_piece, weight_rows, (((1,), (1,)), ((), ())), prefe...]
    all_to_all x0 -> x2, starting transfers between devices: none -> 16.5 us  [the longest x1 11.4 us: local(): got = lax.all_to_all(grads, 'slot', 0, 0, tiled=True)]
  transfers between devices with their start and end apart: 3 -> 8, of which waited for: 3 -> 5; matrix products, arithmetic and copies ran while one was open for 4% -> 4% of each run, Pallas kernels for 0% -> 4%
where the time goes in v1:
time: 197 us
  waiting for transfers between devices  109 us (55%)
  starting transfers between devices  24.5 us (12%)
  Pallas kernels  22.8 us (12%)
  blocking collectives  20.4 us (10%)
  local copies, waits for them, and re-layouts  19.5 us (10%)
    all_to_all x1, waiting for transfers between devices, local(): got = lax.all_to_all(grads, 'slot', 0, 0, tiled=True)  44.8 us
    all_to_all x1, waiting for transfers between devices, local(): parts.append(lax.all_to_all(send, 'slot', 0, 0, tiled=True))  34.2 us
    all_to_all x1, blocking collectives, gather_hid(): lax.all_to_all(replicated, BOTH, 0, 0, tiled=True, axis_index_groups=line...  20.4 us
    unnamed x34, local copies, waits for them, and re-layouts  16.7 us
    all_to_all x1, starting transfers between devices, local(): got = lax.all_to_all(grads, 'slot', 0, 0, tiled=True)  11.4 us
    ppermute x1, waiting for transfers between devices, gather_hid(): far_low = lax.ppermute(below_low, BOTH, up)  11.3 us
    ppermute x1, waiting for transfers between devices, gather_hid(): below_low = lax.ppermute(low, BOTH, up)  10 us
    pallas_call x1, Pallas kernels, slot_grad(): pl.pallas_call(functools.partial(slot_grad_kernel, layout), out_shape=jax...  8.91 us
  transfers between devices with their start and end apart: 8, of which 5 were waited for; matrix products, arithmetic and copies ran while one was open for 4% of the time, Pallas kernels for 4%

profile of v1, /device:TPU:1, one launch (start us, length us, event | category | flops | bytes accessed | tf_op | source)
XLA Modules:
  0.0 196.8 jit_solution(3942221228709602377)
XLA Ops:
  0.6 1.2 dynamic_slice.3.live_ref
  1.9 1.0 copy-done.5
  2.9 1.0 mask_turn.1
  3.9 20.4 %all_to_all.15.refs_0_ = bf16[4,128,2048]{2,1,0:T(8,128)(2,1)S(1)} all-to-all(bf16[4,128,2048]{2,1,0:T(8,128)(2,1)S(1)} %mask_turn.1), channel_id=1, replica_groups={{0,1,2,3},{16,20,24,28},{4,5,6,7},{17,21,25,29},{8,9,10,11},{18,22,26,3..., dimensions={0} | all-to-all | bytes 4194304 | tf_op jit(solution)/shard_map/all_to_all | solution.py:214
  24.3 1.5 fusion
  25.9 0.5 copy-done.14
  26.3 1.0 collective-permute-start
  27.3 1.7 collective-permute-start.3
  29.0 2.7 %collective-permute-start.2 = (bf16[2,128,2048]{2,1,0:T(8,128)(2,1)}, bf16[2,128,2048]{2,1,0:T(8,128)(2,1)}, u32[]{:S(2)}, u32[]{:S(2)}) collective-permute-start(bf16[2,128,2048]{2,1,0:T(8,128)(2,1)} %get-tuple-element.15), channel_id=1, source_target_pairs={{0,12},{16,19},{1,13},{17,16},{2,14},{18,17},{3,15},{19,18},{4,0},... | collective-permute-start | bytes 3145736 | tf_op jit(solution)/shard_map/ppermute | solution.py:222
  31.7 10.0 %collective-permute-done.refs_1_ = bf16[2,128,2048]{2,1,0:T(8,128)(2,1)S(1)} collective-permute-done((bf16[2,128,2048]{2,1,0:T(8,128)(2,1)}, bf16[2,128,2048]{2,1,0:T(8,128)(2,1)S(1)}, u32[]{:S(2)}, u32[]{:S(2)}) %collective-permute-start) | collective-permute-done | bytes 1048608 | tf_op jit(solution)/shard_map/ppermute | solution.py:219
  41.7 2.7 %collective-permute-start.5 = (bf16[2,128,2048]{2,1,0:T(8,128)(2,1)S(1)}, bf16[2,128,2048]{2,1,0:T(8,128)(2,1)}, u32[]{:S(2)}, u32[]{:S(2)}) collective-permute-start(bf16[2,128,2048]{2,1,0:T(8,128)(2,1)S(1)} %collective-permute-done.3.refs_4_), channel_id=1, source_target_pairs={{0,12},{16,19},{1,13},{17,16},{2,14},{18,17},{3,15},{19,18},{4,0},... | collective-permute-start | bytes 3145736 | tf_op jit(solution)/shard_map/ppermute | solution.py:224
  44.4 0.1 pad_add_fusion.place_ref
  44.5 8.5 %collective-permute-done.1.refs_2_ = bf16[2,128,2048]{2,1,0:T(8,128)(2,1)S(1)} collective-permute-done((bf16[2,128,2048]{2,1,0:T(8,128)(2,1)}, bf16[2,128,2048]{2,1,0:T(8,128)(2,1)S(1)}, u32[]{:S(2)}, u32[]{:S(2)}) %collective-permute-start.1) | collective-permute-done | bytes 1048608 | tf_op jit(solution)/shard_map/ppermute | solution.py:221
  52.9 11.3 %collective-permute-done.4.refs_5_ = bf16[2,128,2048]{2,1,0:T(8,128)(2,1)} collective-permute-done((bf16[2,128,2048]{2,1,0:T(8,128)(2,1)S(1)}, bf16[2,128,2048]{2,1,0:T(8,128)(2,1)}, u32[]{:S(2)}, u32[]{:S(2)}) %collective-permute-start.4) | collective-permute-done | bytes 1048608 | tf_op jit(solution)/shard_map/ppermute | solution.py:223
  64.3 8.9 %slot_grad.1 = bf16[16,128,512]{2,1,0:T(8,128)(2,1)} custom-call(s32[2]{0:T(128)S(1)} %pad_add_fusion.place_ref, bf16[2048,512]{1,0:T(8,128)(2,1)} %hidden_ref.1, bf16[4,128,2048]{2,1,0:T(8,128)(2,1)} %copy-done.14, bf16[2,128,2048]{2,1,0:T(8,128)(2,1)S(1)} %collective-permute-done.refs_1_, bf16[2,128,2048]{2,1,0:T(8,128)(2,1)S(1)} %collective-permute-done.1.refs_2_, ...), custom_call_target="tpu_custom_call" | custom-call | flops 4294967296 | bytes 12582912 | tf_op jit(solution)/shard_map/slot_grad/pallas_call | solution.py:94
  73.2 11.4 %all-to-all-start.1 = ((bf16[16,128,512]{2,1,0:T(8,128)(2,1)}), bf16[16,128,512]{2,1,0:T(8,128)(2,1)S(1)}, u32[]{:S(2)}, u32[]{:S(2)}) async-start(bf16[16,128,512]{2,1,0:T(8,128)(2,1)} %slot_grad.1), calls=%async_computation.1 | async-start | bytes 4194304 | tf_op jit(solution)/shard_map/all_to_all | solution.py:242
  84.6 1.6 copy.12
  86.2 2.5 %copy.13 = f32[4,512,128]{1,2,0:T(8,128)} copy(f32[4,512,128]{2,1,0:T(8,128)} %param.14) | data formatting | bytes 2097152 | tf_op args[6]
  88.7 44.8 %all-to-all-done.1.got_ref = bf16[16,128,512]{2,1,0:T(8,128)(2,1)S(1)} async-done(((bf16[16,128,512]{2,1,0:T(8,128)(2,1)}), bf16[16,128,512]{2,1,0:T(8,128)(2,1)S(1)}, u32[]{:S(2)}, u32[]{:S(2)}) %all-to-all-start.1) | async-done | bytes 2097184 | tf_op jit(solution)/shard_map/all_to_all | solution.py:242
  133.5 1.2 copy-done
  134.8 2.5 %momentum_step.1 = (f32[4,128,512]{2,1,0:T(8,128)S(1)}, f32[4,128,512]{2,1,0:T(8,128)S(1)}, bf16[16,128,512]{2,1,0:T(8,128)(2,1)S(1)}) custom-call(s32[16]{0:T(128)S(1)} %bitcast.14, s32[16]{0:T(128)S(1)} %bitcast.15, bf16[16,128,512]{2,1,0:T(8,128)(2,1)S(1)} %all-to-all-done.1.got_ref, f32[4,128,512]{2,1,0:T(8,128)S(1)} %bitcast.10, f32[4,128,512]{2,1,0:T(8,128)S(1)} %bitcast.11), custom_call_target="tpu_custom_call" | custom-call | bytes 8388608 | tf_op jit(solution)/shard_map/momentum_step/pallas_call | solution.py:130
  137.3 1.3 copy-done.1
  138.6 1.1 copy-done.2
  139.7 1.1 copy-done.4
  140.8 5.1 %all-to-all-start.2 = ((bf16[16,128,512]{2,1,0:T(8,128)(2,1)}), bf16[16,128,512]{2,1,0:T(8,128)(2,1)S(1)}, u32[]{:S(2)}, u32[]{:S(2)}) async-start(bf16[16,128,512]{2,1,0:T(8,128)(2,1)} %copy-done.1), calls=%async_computation.2 | async-start | bytes 4194304 | tf_op jit(solution)/shard_map/all_to_all | solution.py:246
  145.9 1.2 copy-done.11
  147.1 1.2 copy-done.13
  148.3 8.4 %input_grad.1 = bf16[2048,512]{1,0:T(8,128)(2,1)} custom-call(s32[2]{0:T(128)S(1)} %pad_add_fusion.place_ref, bf16[512,2048]{1,0:T(8,128)(2,1)} %bitcast.17, bf16[4,128,2048]{2,1,0:T(8,128)(2,1)} %copy-done.14, bf16[2,128,2048]{2,1,0:T(8,128)(2,1)S(1)} %copy-done.9, bf16[2,128,2048]{2,1,0:T(8,128)(2,1)S(1)} %copy-done.13, ...), custom_call_target="tpu_custom_call" | custom-call | flops 4294967296 | bytes 12582912 | tf_op jit(solution)/shard_map/input_grad/pallas_call | solution.py:177
  156.7 2.6 %copy.14 = f32[4,512,128]{2,1,0:T(8,128)} copy(f32[4,512,128]{1,2,0:T(8,128)} %bitcast.13) | data formatting | bytes 2097152
  159.4 1.3 copy.15
  160.7 34.2 %all-to-all-done.2.refs_0_ = bf16[16,128,512]{2,1,0:T(8,128)(2,1)S(1)} async-done(((bf16[16,128,512]{2,1,0:T(8,128)(2,1)}), bf16[16,128,512]{2,1,0:T(8,128)(2,1)S(1)}, u32[]{:S(2)}, u32[]{:S(2)}) %all-to-all-start.2) | async-done | bytes 2097184 | tf_op jit(solution)/shard_map/all_to_all | solution.py:246
  194.8 2.0 %placed_turn.1 = bf16[512,2048]{1,0:T(8,128)(2,1)} custom-call(bf16[16,128,512]{2,1,0:T(8,128)(2,1)S(1)} %all-to-all-done.2.refs_0_), custom_call_target="tpu_custom_call" | custom-call | bytes 4194304 | tf_op jit(solution)/shard_map/placed_turn/pallas_call | solution.py:199
  (27 shorter events, 0.1 us)
Async XLA Ops:
  1.9 1.0 copy-start.5
  24.3 2.0 %copy-start.14 = (bf16[4,128,2048]{2,1,0:T(8,128)(2,1)}, bf16[4,128,2048]{2,1,0:T(8,128)(2,1)S(1)}, u32[]{:S(2)}) copy-start(bf16[4,128,2048]{2,1,0:T(8,128)(2,1)S(1)} %all_to_all.15.refs_0_) | copy-start | bytes 6291460
  26.3 15.4 %collective-permute-start = (bf16[2,128,2048]{2,1,0:T(8,128)(2,1)}, bf16[2,128,2048]{2,1,0:T(8,128)(2,1)S(1)}, u32[]{:S(2)}, u32[]{:S(2)}) collective-permute-start(bf16[2,128,2048]{2,1,0:T(8,128)(2,1)} %get-tuple-element.15), channel_id=1, source_target_pairs={{0,4},{16,17},{1,5},{17,18},{2,6},{18,19},{3,7},{19,16},{4,8},{20,... | collective-permute-start | bytes 3145736 | tf_op jit(solution)/shard_map/ppermute | solution.py:219
  27.3 14.4 %collective-permute-start.3 = (bf16[2,128,2048]{2,1,0:T(8,128)(2,1)}, bf16[2,128,2048]{2,1,0:T(8,128)(2,1)S(1)}, u32[]{:S(2)}, u32[]{:S(2)}) collective-permute-start(bf16[2,128,2048]{2,1,0:T(8,128)(2,1)} %get-tuple-element.14), channel_id=1, source_target_pairs={{0,12},{16,19},{1,13},{17,16},{2,14},{18,17},{3,15},{19,18},{4,0},... | collective-permute-start | bytes 3145736 | tf_op jit(solution)/shard_map/ppermute | solution.py:220
  29.0 23.9 %collective-permute-start.1 = (bf16[2,128,2048]{2,1,0:T(8,128)(2,1)}, bf16[2,128,2048]{2,1,0:T(8,128)(2,1)S(1)}, u32[]{:S(2)}, u32[]{:S(2)}) collective-permute-start(bf16[2,128,2048]{2,1,0:T(8,128)(2,1)} %get-tuple-element.14), channel_id=1, source_target_pairs={{0,4},{16,17},{1,5},{17,18},{2,6},{18,19},{3,7},{19,16},{4,8},{20,... | collective-permute-start | bytes 3145736 | tf_op jit(solution)/shard_map/ppermute | solution.py:221
  29.0 23.9 %collective-permute-start.2 = (bf16[2,128,2048]{2,1,0:T(8,128)(2,1)}, bf16[2,128,2048]{2,1,0:T(8,128)(2,1)}, u32[]{:S(2)}, u32[]{:S(2)}) collective-permute-start(bf16[2,128,2048]{2,1,0:T(8,128)(2,1)} %get-tuple-element.15), channel_id=1, source_target_pairs={{0,12},{16,19},{1,13},{17,16},{2,14},{18,17},{3,15},{19,18},{4,0},... | collective-permute-start | bytes 3145736 | tf_op jit(solution)/shard_map/ppermute | solution.py:222
  41.7 31.5 %copy-start.8 = (bf16[2,128,2048]{2,1,0:T(8,128)(2,1)}, bf16[2,128,2048]{2,1,0:T(8,128)(2,1)S(1)}, u32[]{:S(2)}) copy-start(bf16[2,128,2048]{2,1,0:T(8,128)(2,1)S(1)} %collective-permute-done.refs_1_) | copy-start | bytes 3145732
  41.7 22.6 %collective-permute-start.4 = (bf16[2,128,2048]{2,1,0:T(8,128)(2,1)S(1)}, bf16[2,128,2048]{2,1,0:T(8,128)(2,1)}, u32[]{:S(2)}, u32[]{:S(2)}) collective-permute-start(bf16[2,128,2048]{2,1,0:T(8,128)(2,1)S(1)} %collective-permute-done.refs_1_), channel_id=1, source_target_pairs={{0,4},{16,17},{1,5},{17,18},{2,6},{18,19},{3,7},{19,16},{4,8},{20,... | collective-permute-start | bytes 3145736 | tf_op jit(solution)/shard_map/ppermute | solution.py:223
  41.7 31.5 %copy-start.10 = (bf16[2,128,2048]{2,1,0:T(8,128)(2,1)}, bf16[2,128,2048]{2,1,0:T(8,128)(2,1)S(1)}, u32[]{:S(2)}) copy-start(bf16[2,128,2048]{2,1,0:T(8,128)(2,1)S(1)} %collective-permute-done.3.refs_4_) | copy-start | bytes 3145732
  41.7 22.6 %collective-permute-start.5 = (bf16[2,128,2048]{2,1,0:T(8,128)(2,1)S(1)}, bf16[2,128,2048]{2,1,0:T(8,128)(2,1)}, u32[]{:S(2)}, u32[]{:S(2)}) collective-permute-start(bf16[2,128,2048]{2,1,0:T(8,128)(2,1)S(1)} %collective-permute-done.3.refs_4_), channel_id=1, source_target_pairs={{0,12},{16,19},{1,13},{17,16},{2,14},{18,17},{3,15},{19,18},{4,0},... | collective-permute-start | bytes 3145736 | tf_op jit(solution)/shard_map/ppermute | solution.py:224
  52.9 20.3 %copy-start.12 = (bf16[2,128,2048]{2,1,0:T(8,128)(2,1)}, bf16[2,128,2048]{2,1,0:T(8,128)(2,1)S(1)}, u32[]{:S(2)}) copy-start(bf16[2,128,2048]{2,1,0:T(8,128)(2,1)S(1)} %collective-permute-done.1.refs_2_) | copy-start | bytes 3145732
  73.2 60.3 %all-to-all-start.1 = ((bf16[16,128,512]{2,1,0:T(8,128)(2,1)}), bf16[16,128,512]{2,1,0:T(8,128)(2,1)S(1)}, u32[]{:S(2)}, u32[]{:S(2)}) async-start(bf16[16,128,512]{2,1,0:T(8,128)(2,1)} %slot_grad.1), calls=%async_computation.1 | async-start | bytes 4194304 | tf_op jit(solution)/shard_map/all_to_all | solution.py:242
  84.6 49.0 %copy-start.6 = (s32[16,1]{0,1:T(1,128)S(1)}, s32[16,1]{0,1:T(1,128)}, u32[]{:S(2)}) copy-start(s32[16,1]{0,1:T(1,128)} %param.11) | copy-start | bytes 196
  84.6 48.9 %copy-start.7 = (s32[16,1]{0,1:T(1,128)S(1)}, s32[16,1]{0,1:T(1,128)}, u32[]{:S(2)}) copy-start(s32[16,1]{0,1:T(1,128)} %param.12) | copy-start | bytes 196
  133.5 1.2 copy-start
  137.3 1.3 copy-start.1
  138.6 1.1 copy-start.2
  139.7 1.1 copy-start.4
  140.8 5.1 %copy-start.9 = (bf16[2,128,2048]{2,1,0:T(8,128)(2,1)S(1)}, bf16[2,128,2048]{2,1,0:T(8,128)(2,1)}, u32[]{:S(2)}) copy-start(bf16[2,128,2048]{2,1,0:T(8,128)(2,1)} %copy-done.8) | copy-start | bytes 3145732
  140.8 54.1 %all-to-all-start.2 = ((bf16[16,128,512]{2,1,0:T(8,128)(2,1)}), bf16[16,128,512]{2,1,0:T(8,128)(2,1)S(1)}, u32[]{:S(2)}, u32[]{:S(2)}) async-start(bf16[16,128,512]{2,1,0:T(8,128)(2,1)} %copy-done.1), calls=%async_computation.2 | async-start | bytes 4194304 | tf_op jit(solution)/shard_map/all_to_all | solution.py:246
  145.9 1.2 copy-start.11
  147.1 1.2 copy-start.13
  156.7 2.6 %copy-start.3 = (f32[4,128,512]{2,1,0:T(8,128)S(1)}, f32[4,128,512]{2,1,0:T(8,128)}, u32[]{:S(2)}) copy-start(f32[4,128,512]{2,1,0:T(8,128)} %copy-done.2) | copy-start | bytes 3145732

commit v2 on v0

v2 whole, which is shorter than its diff:
```python
import functools

import jax
import jax.numpy as jnp
from jax import lax
from jax.experimental import pallas as pl
from jax.experimental.pallas import tpu as pltpu
from jax.sharding import PartitionSpec as P

momentum_decay = 0.9
learn_rate = 0.01
BOTH = ("slot", "hid")
CHUNKS = ((0, 64), (64, 64))
VM = pl.BlockSpec(memory_space=pltpu.VMEM)
SM = pl.BlockSpec(memory_space=pltpu.SMEM)
HBM = pl.BlockSpec(memory_space=pltpu.HBM)
MIB = 1 << 20


def params(mib):
    return pltpu.CompilerParams(vmem_limit_bytes=mib * MIB)


def cost(flops, moved):
    return pl.CostEstimate(flops=flops, bytes_accessed=moved, transcendentals=0)


def position(z, core, y, x):
    return (z * 2 + core) * 16 + y * 4 + x


def line_pairs(step):
    pairs = []
    for z in range(8):
        for y in range(4):
            for x in range(4):
                pairs.append((position(z, 0, y, x), position(z, 0, y, (x + step) % 4)))
                pairs.append((position(z, 1, y, x), position(z, 1, (y + step) % 4, x)))
    return pairs


def cross_pairs(step):
    pairs = []
    for z in range(8):
        for y in range(4):
            for x in range(4):
                pairs.append((position(z, 0, y, x), position(z, 0, (y + step) % 4, x)))
                pairs.append((position(z, 1, y, x), position(z, 1, y, (x + step) % 4)))
    return pairs


def mask_kernel(place_ref, counts_ref, cot_ref, *out_refs):
    live = lax.broadcasted_iota(jnp.int32, cot_ref.shape, 0) < counts_ref[place_ref[3]]
    turned = jnp.where(live, cot_ref[...], jnp.zeros_like(cot_ref)).T
    for (start, size), out_ref in zip(CHUNKS, out_refs):
        out_ref[0] = turned[start : start + size]


def masked_chunks(place, counts, cotangent):
    rows = cotangent.shape[0]
    return pl.pallas_call(
        mask_kernel,
        out_shape=[jax.ShapeDtypeStruct((1, size, rows), jnp.bfloat16) for _, size in CHUNKS],
        in_specs=[SM, SM, VM],
        out_specs=[VM] * len(CHUNKS),
        compiler_params=params(16),
        cost_estimate=cost(0, 1 * MIB),
        name="mask_turn",
    )(place, counts, cotangent)


STEPS = ((0, 3), (1, 2))
NEAR = (0, 3, 1)
FAR = (2,)


def block_of(place_ref, group, k):
    cross = lax.rem(place_ref[1] + group, 4)
    line = lax.rem(place_ref[2] + k, 4)
    return jnp.where(place_ref[0] == 0, 4 * cross + line, 4 * line + cross)


def slot_grad_kernel(groups, place_ref, hidden_ref, *refs):
    piece_refs, (out_ref, stage, sems) = refs[: 2 * len(groups)], refs[-3:]
    copies = []
    for i, group in enumerate(groups):
        pair = piece_refs[2 * i : 2 * i + 2]
        _, size, rows = pair[0].shape
        grad = jnp.dot(
            jnp.concatenate([ref[...].reshape(2 * size, rows) for ref in pair], axis=0),
            hidden_ref[...],
            preferred_element_type=jnp.float32,
        ).astype(jnp.bfloat16)
        for at, k in enumerate(STEPS[0] + STEPS[1]):
            n = len(copies)
            stage[n] = grad[at * size : (at + 1) * size]
            copy = pltpu.make_async_copy(
                stage.at[n], out_ref.at[block_of(place_ref, group, k)], sems.at[n]
            )
            copy.start()
            copies.append(copy)
    for copy in copies:
        copy.wait()


def slot_grad(place, hidden, pieces, groups, into):
    size = pieces[0].shape[1]
    width = hidden.shape[1]
    blocks = 4 * len(groups)
    extra = () if into is None else (into,)
    return pl.pallas_call(
        functools.partial(slot_grad_kernel, groups),
        out_shape=jax.ShapeDtypeStruct((16, size, width), jnp.bfloat16),
        in_specs=[SM, VM] + [VM] * len(pieces) + [HBM] * len(extra),
        out_specs=HBM,
        input_output_aliases={2 + len(pieces): 0} if extra else {},
        scratch_shapes=[
            pltpu.VMEM((blocks, size, width), jnp.bfloat16),
            pltpu.SemaphoreType.DMA((blocks,)),
        ],
        compiler_params=params(32),
        cost_estimate=cost(2 * blocks * size * width * hidden.shape[0], 6 * MIB),
        name="slot_grad_far" if extra else "slot_grad_near",
    )(place, hidden, *pieces, *extra)


def expert_sum(now_ref, got_ref, e, at):
    total = jnp.zeros((at.size, got_ref.shape[2]), jnp.float32)
    for s in range(got_ref.shape[0]):
        total += (now_ref[s] == e).astype(jnp.float32) * got_ref[s, at].astype(jnp.float32)
    return total


def next_weights_kernel(wanted_only, now_ref, next_ref, got_ref, mom_ref, mas_ref, out_ref, rounded, sems):
    experts, size, _ = mom_ref.shape
    step = 16

    def rows_of(i, carry):
        at = pl.ds(pl.multiple_of(i * step, step), step)
        for e in range(experts):
            new_mom = momentum_decay * mom_ref[e, at] + expert_sum(now_ref, got_ref, e, at)
            rounded[e, at] = (mas_ref[e, at] - learn_rate * new_mom).astype(jnp.bfloat16)
        return carry

    lax.fori_loop(0, size // step, rows_of, 0)
    copies = []
    for s in range(out_ref.shape[0]):
        source = next_ref[s] if wanted_only else s
        copies.append(pltpu.make_async_copy(rounded.at[source], out_ref.at[s], sems.at[s]))
    for copy in copies:
        copy.start()
    for copy in copies:
        copy.wait()


def next_weights(wanted_only, now, following, got, mom, mas):
    count = got.shape[0] if wanted_only else mom.shape[0]
    return pl.pallas_call(
        functools.partial(next_weights_kernel, wanted_only),
        out_shape=jax.ShapeDtypeStruct((count,) + mom.shape[1:], jnp.bfloat16),
        in_specs=[SM, SM, VM, VM, VM],
        out_specs=HBM,
        scratch_shapes=[
            pltpu.VMEM(mom.shape, jnp.bfloat16),
            pltpu.SemaphoreType.DMA((count,)),
        ],
        compiler_params=params(16),
        cost_estimate=cost(0, 3 * MIB),
        name="next_weights",
    )(now, following, got, mom, mas)


def update_kernel(now_ref, mom_ref, mas_ref, *refs):
    got_refs, (new_mom_ref, new_mas_ref, total) = refs[:-3], refs[-3:]
    e = pl.program_id(0)
    start = 0
    for got_ref in got_refs:
        for first in range(0, got_ref.shape[1], 16):
            total[start + first : start + first + 16] = expert_sum(
                now_ref, got_ref, e, pl.ds(first, 16)
            )
        start += got_ref.shape[1]
    new_mom = momentum_decay * mom_ref[0] + total[...].T
    new_mom_ref[0] = new_mom
    new_mas_ref[0] = mas_ref[0] - learn_rate * new_mom


def update(now, momentum, master, gots):
    experts, width, columns = momentum.shape
    block = pl.BlockSpec((1, width, columns), lambda e: (e, 0, 0))
    return pl.pallas_call(
        update_kernel,
        grid=(experts,),
        out_shape=[jax.ShapeDtypeStruct(momentum.shape, jnp.float32)] * 2,
        in_specs=[SM, block, block]
        + [pl.BlockSpec(g.shape, lambda e: (0, 0, 0)) for g in gots],
        out_specs=[block, block],
        scratch_shapes=[pltpu.VMEM((columns, width), jnp.float32)],
        compiler_params=params(24),
        cost_estimate=cost(0, 8 * MIB),
        name="momentum_step",
    )(now, momentum, master, *gots)


def input_grad_kernel(place_ref, weight_ref, *refs):
    pieces, out_ref = refs[:-1], refs[-1]
    total = None
    for i, group in enumerate(NEAR + FAR):
        rows_of_group, columns = [], []
        for half, steps in enumerate(STEPS):
            for n, k in enumerate(steps):
                for chunk in range(len(CHUNKS)):
                    rows_of_group.append(pieces[8 * chunk + 2 * i + half][n])
                start = pl.multiple_of(block_of(place_ref, group, k) * 128, 128)
                columns.append(weight_ref[:, pl.ds(start, 128)])
        left = jnp.concatenate(rows_of_group, axis=0).T
        right = jnp.concatenate(columns, axis=1)
        part = lax.dot_general(
            left, right, (((1,), (1,)), ((), ())), preferred_element_type=jnp.float32
        )
        total = part if total is None else total + part
    out_ref[...] = total.astype(jnp.bfloat16)


def input_gradient(place, weights, pieces):
    tile = 512
    width = weights.shape[0]
    rows = pieces[0].shape[2]
    return pl.pallas_call(
        input_grad_kernel,
        grid=(rows // tile,),
        out_shape=jax.ShapeDtypeStruct((rows, width), jnp.bfloat16),
        in_specs=[SM, VM]
        + [pl.BlockSpec((p.shape[0], p.shape[1], tile), lambda i: (0, 0, i)) for p in pieces],
        out_specs=pl.BlockSpec((tile, width), lambda i: (i, 0)),
        compiler_params=params(32),
        cost_estimate=cost(2 * rows * width * weights.shape[1], 12 * MIB),
        name="input_grad",
    )(place, weights, *pieces)


def placed_kernel(wanted_ref, all_ref, own_ref, out_ref):
    for j in range(2):
        block = jnp.concatenate([all_ref[j, 0], own_ref[j]], axis=0)
        out_ref[:, j * 128 : (j + 1) * 128] = block.T


def place_weights(wanted, every, own):
    slots, size, width = own.shape
    return pl.pallas_call(
        placed_kernel,
        grid_spec=pltpu.PrefetchScalarGridSpec(
            num_scalar_prefetch=1,
            grid=(slots // 2,),
            in_specs=[
                pl.BlockSpec((2, 1) + every.shape[2:], lambda i, wanted: (i, wanted[0], 0, 0)),
                pl.BlockSpec((2, size, width), lambda i, wanted: (i, 0, 0)),
            ],
            out_specs=pl.BlockSpec((width, 256), lambda i, wanted: (0, i)),
        ),
        out_shape=jax.ShapeDtypeStruct((width, slots * 128), jnp.bfloat16),
        compiler_params=params(16),
        cost_estimate=cost(0, 4 * MIB),
        name="placed_turn",
    )(wanted, every, own)


def gather_line(own):
    back = lax.ppermute(own, BOTH, line_pairs(1))
    ahead = lax.ppermute(own, BOTH, line_pairs(3))
    across = lax.ppermute(own, BOTH, line_pairs(2))
    return jnp.concatenate([own, back], axis=0), jnp.concatenate([ahead, across], axis=0)


def gather_cross(one, two):
    up, down = cross_pairs(1), cross_pairs(3)
    one_below = lax.ppermute(one, BOTH, up)
    one_above = lax.ppermute(one, BOTH, down)
    two_below = lax.ppermute(two, BOTH, up)
    two_above = lax.ppermute(two, BOTH, down)
    one_far = lax.ppermute(one_below, BOTH, up)
    two_far = lax.ppermute(two_above, BOTH, down)
    return (one, two, one_below, two_below, one_above, two_above, one_far, two_far)


def local(cotangent, hidden, weights, slot_experts, next_experts, row_counts, master, momentum):
    slot = lax.axis_index("slot")
    hid = lax.axis_index("hid")
    core = slot & 1
    y, x = hid >> 2, hid & 3
    place = jnp.stack(
        [core, jnp.where(core == 0, y, x), jnp.where(core == 0, x, y), slot]
    ).astype(jnp.int32)
    now, following = slot_experts[:, 0], next_experts[:, 0]

    first, second = masked_chunks(place, row_counts, cotangent)
    first_one, first_two = gather_line(first)
    second, first_one = lax.optimization_barrier((second, first_one))
    first_pieces = gather_cross(first_one, first_two)
    second_pieces = gather_cross(*gather_line(second))

    hidden, mom, mas = lax.optimization_barrier(
        (hidden, jnp.swapaxes(momentum, 1, 2), jnp.swapaxes(master, 1, 2))
    )
    def grads_of(pieces):
        near = slot_grad(place, hidden, pieces[:6], NEAR, None)
        return slot_grad(place, hidden, pieces[6:], FAR, near)

    got_first = lax.all_to_all(grads_of(first_pieces), "slot", 0, 0, tiled=True)
    got_first, second_grads = lax.optimization_barrier((got_first, grads_of(second_pieces)))
    gots = (got_first, lax.all_to_all(second_grads, "slot", 0, 0, tiled=True))
    (cut, size), (rest, _) = CHUNKS
    every = next_weights(False, now, following, gots[0], mom[:, cut : cut + size], mas[:, cut : cut + size])
    every = lax.all_gather(every, "slot", axis=0)
    wanted = next_weights(True, now, following, gots[1], mom[:, rest:], mas[:, rest:])
    wanted = lax.all_to_all(wanted, "slot", 0, 0, tiled=True)

    new_momentum, new_master = update(now, momentum, master, gots)
    input_grad = input_gradient(place, weights[0], first_pieces + second_pieces)
    placed = place_weights(lax.dynamic_slice_in_dim(following, slot, 1), every, wanted)[None]
    return (input_grad, new_momentum, new_master, placed)


def solution(mesh):
    return jax.shard_map(
        local,
        mesh=mesh,
        in_specs=(
            P("slot", "hid"),
            P("slot", "hid"),
            P("slot", "hid", None),
            P(),
            P(),
            P(),
            P(None, "hid", "slot"),
            P(None, "hid", "slot"),
        ),
        out_specs=(
            P("slot", "hid"),
            P(None, "hid", "slot"),
            P(None, "hid", "slot"),
            P("slot", "hid", None),
        ),
        check_vma=False,
    )
```

time: 298 us -> 193 us (0.65)
  waiting for transfers between devices: 208 us -> 20.2 us
  blocking collectives: 0 us -> 43.9 us
  starting transfers between devices: 0.3 us -> 40.7 us
  Pallas kernels: 0 us -> 36.7 us
  matrix products: 19.6 us -> 0 us
  other arithmetic: 14.7 us -> 0.93 us
  local copies, waits for them, and re-layouts: 38.5 us -> 33.1 us
    all_gather x2 -> x1, waiting for transfers between devices: 140 us -> 0.01 us  [local(): every = lax.all_gather(every, 'slot', axis=0)]
    unnamed x4 -> x1, waiting for transfers between devices: 68.1 us -> 0.02 us
    all_to_all x0 -> x1, blocking collectives: none -> 43.9 us  [local(): gots = (got_first, lax.all_to_all(second_grads, 'slot', 0, 0, tiled=True))]
    pallas_call x0 -> x10, Pallas kernels: none -> 36.7 us  [the longest x4 13 us: slot_grad(): pl.pallas_call(functools.partial(slot_grad_kernel, groups), out_shape=jax...]
    ppermute x0 -> x18, starting transfers between devices: none -> 23.8 us  [the longest x2 5.87 us: gather_cross(): two_far = lax.ppermute(two_above, BOTH, down)]
    dot_general x2 -> x0, matrix products: 19.6 us -> none  [the longest x1 9.86 us: local(): lax.dot_general(shard_piece, weight_rows, (((1,), (1,)), ((), ())), prefe...]
    all_to_all x0 -> x2, starting transfers between devices: none -> 16.9 us  [the longest x1 12.6 us: local(): got_first = lax.all_to_all(grads_of(first_pieces), 'slot', 0, 0, tiled=True)]
    ppermute x0 -> x18, waiting for transfers between devices: none -> 16.2 us  [the longest x2 6.76 us: gather_cross(): one_below = lax.ppermute(one, BOTH, up)]
  transfers between devices with their start and end apart: 3 -> 21, of which waited for: 3 -> 11; matrix products, arithmetic and copies ran while one was open for 4% -> 6% of each run, Pallas kernels for 0% -> 14%
where the time goes in v2:
time: 193 us; the launch traced here: 190 us
  blocking collectives  43.9 us (23%)
  starting transfers between devices  40.7 us (21%)
  Pallas kernels  36.7 us (19%)
  local copies, waits for them, and re-layouts  33.1 us (17%)
  waiting for transfers between devices  20.2 us (10%)
  between operations  14.3 us (7%)
    all_to_all x1, blocking collectives, local(): gots = (got_first, lax.all_to_all(second_grads, 'slot', 0, 0, tiled=True))  43.9 us
    unnamed x73, local copies, waits for them, and re-layouts  27.3 us
    pallas_call x4, Pallas kernels, slot_grad(): pl.pallas_call(functools.partial(slot_grad_kernel, groups), out_shape=jax...  13 us
    all_to_all x1, starting transfers between devices, local(): got_first = lax.all_to_all(grads_of(first_pieces), 'slot', 0, 0, tiled=True)  12.6 us
    pallas_call x1, Pallas kernels, input_gradient(): pl.pallas_call(input_grad_kernel, grid=(rows // tile,), out_shape=jax.Sha...  8.01 us
    ppermute x2, waiting for transfers between devices, gather_cross(): one_below = lax.ppermute(one, BOTH, up)  6.76 us
    pallas_call x1, Pallas kernels, place_weights(): pl.pallas_call(placed_kernel, grid_spec=pltpu.PrefetchScalarGridSpec(num_...  6.39 us
    ppermute x2, starting transfers between devices, gather_cross(): two_far = lax.ppermute(two_above, BOTH, down)  5.87 us
  transfers between devices with their start and end apart: 21, of which 11 were waited for; matrix products, arithmetic and copies ran while one was open for 6% of the time, Pallas kernels for 14%

profile of v2, /device:TPU:1, one launch (start us, length us, event | category | flops | bytes accessed | tf_op | source)
XLA Modules:
  0.0 189.8 jit_solution(15925891172814779354)
XLA Ops:
  9.7 2.2 %collective-permute-start = (bf16[1,64,2048]{2,1,0:T(8,128)(2,1)S(1)}, bf16[1,64,2048]{2,1,0:T(8,128)(2,1)S(1)}, u32[]{:S(2)}, u32[]{:S(2)}) collective-permute-start(bf16[1,64,2048]{2,1,0:T(8,128)(2,1)S(1)} %get-tuple-element.16), channel_id=1, source_target_pairs={{0,1},{16,20},{1,2},{17,21},{2,3},{18,22},{3,0},{19,23},{4,5},{20,... | collective-permute-start | bytes 786440 | tf_op jit(solution)/shard_map/ppermute | solution.py:269
  11.9 1.5 collective-permute-start.1
  13.4 1.6 collective-permute-start.2
  15.0 2.4 %collective-permute-done = bf16[1,64,2048]{2,1,0:T(8,128)(2,1)S(1)} collective-permute-done((bf16[1,64,2048]{2,1,0:T(8,128)(2,1)S(1)}, bf16[1,64,2048]{2,1,0:T(8,128)(2,1)S(1)}, u32[]{:S(2)}, u32[]{:S(2)}) %collective-permute-start) | collective-permute-done | bytes 262176 | tf_op jit(solution)/shard_map/ppermute | solution.py:269
  22.1 2.5 %collective-permute-start.6 = (bf16[2,64,2048]{2,1,0:T(8,128)(2,1)}, bf16[2,64,2048]{2,1,0:T(8,128)(2,1)}, u32[]{:S(2)}, u32[]{:S(2)}) collective-permute-start(bf16[2,64,2048]{2,1,0:T(8,128)(2,1)} %constant_dynamic-update-slice_fusion.refs_1_), channel_id=1, source_target_pairs={{0,12},{16,19},{1,13},{17,16},{2,14},{18,17},{3,15},{19,18},{4,0},... | collective-permute-start | bytes 1572872 | tf_op jit(solution)/shard_map/ppermute | solution.py:280
  26.1 3.4 %collective-permute-done.3.refs_2_ = bf16[2,64,2048]{2,1,0:T(8,128)(2,1)} collective-permute-done((bf16[2,64,2048]{2,1,0:T(8,128)(2,1)}, bf16[2,64,2048]{2,1,0:T(8,128)(2,1)}, u32[]{:S(2)}, u32[]{:S(2)}) %collective-permute-start.3) | collective-permute-done | bytes 524320 | tf_op jit(solution)/shard_map/ppermute | solution.py:277
  29.5 1.6 collective-permute-done.6.refs_5_
  31.0 3.1 %collective-permute-start.8 = (bf16[2,64,2048]{2,1,0:T(8,128)(2,1)}, bf16[2,64,2048]{2,1,0:T(8,128)(2,1)}, u32[]{:S(2)}, u32[]{:S(2)}) collective-permute-start(bf16[2,64,2048]{2,1,0:T(8,128)(2,1)} %collective-permute-done.6.refs_5_), channel_id=1, source_target_pairs={{0,12},{16,19},{1,13},{17,16},{2,14},{18,17},{3,15},{19,18},{4,0},... | collective-permute-start | bytes 1572872 | tf_op jit(solution)/shard_map/ppermute | solution.py:282
  34.2 2.5 %copy.17 = f32[4,512,128]{1,2,0:T(8,128)} copy(f32[4,512,128]{2,1,0:T(8,128)} %mas_ref.1) | data formatting | bytes 2097152 | tf_op args[6]
  38.6 2.6 %collective-permute-start.10 = (bf16[1,64,2048]{2,1,0:T(8,128)(2,1)S(1)}, bf16[1,64,2048]{2,1,0:T(8,128)(2,1)}, u32[]{:S(2)}, u32[]{:S(2)}) collective-permute-start(bf16[1,64,2048]{2,1,0:T(8,128)(2,1)S(1)} %get-tuple-element.18), channel_id=1, source_target_pairs={{0,3},{16,28},{1,0},{17,29},{2,1},{18,30},{3,2},{19,31},{4,7},{20,... | collective-permute-start | bytes 786440 | tf_op jit(solution)/shard_map/ppermute | solution.py:270
  41.3 5.2 %slot_grad_near.2.refs_2_ = bf16[16,64,512]{2,1,0:T(8,128)(2,1)S(1)} custom-call(s32[4]{0:T(128)S(1)} %pad_add_fusion.place_ref, bf16[2048,512]{1,0:T(8,128)(2,1)S(1)} %copy-done, bf16[2,64,2048]{2,1,0:T(8,128)(2,1)} %pad_maximum_fusion.refs_0_, bf16[2,64,2048]{2,1,0:T(8,128)(2,1)} %constant_dynamic-update-slice_fusion.refs_1_, ...), custom_call_target="tpu_custom_call" | custom-call | flops 1610612736 | bytes 6291456 | tf_op jit(solution)/shard_map/slot_grad_near/pallas_call | solution.py:111
  46.5 2.3 %slot_grad_far.2 = bf16[16,64,512]{2,1,0:T(8,128)(2,1)S(1)} custom-call(s32[4]{0:T(128)S(1)} %pad_add_fusion.place_ref, bf16[2048,512]{1,0:T(8,128)(2,1)S(1)} %copy-done, bf16[2,64,2048]{2,1,0:T(8,128)(2,1)} %collective-permute-done.7.refs_6_.refs_0_, bf16[2,64,2048]{2,1,0:T(8,128)(2,1)} %collective-permute-done.8.refs_7_.refs_1_, ...), custom_call_target="tpu_custom_call", output_to_operand_aliasing={{}: (4, {})} | custom-call | flops 536870912 | bytes 6291456 | tf_op jit(solution)/shard_map/slot_grad_far/pallas_call | solution.py:111
  49.8 12.6 %all-to-all-start = ((bf16[16,64,512]{2,1,0:T(8,128)(2,1)}), bf16[16,64,512]{2,1,0:T(8,128)(2,1)S(1)}, u32[]{:S(2)}, u32[]{:S(2)}) async-start(bf16[16,64,512]{2,1,0:T(8,128)(2,1)} %copy-done.1), calls=%async_computation | async-start | bytes 2097152 | tf_op jit(solution)/shard_map/all_to_all | solution.py:309
  66.9 1.6 collective-permute-start.15
  68.6 1.4 collective-permute-start.14
  70.0 3.3 %collective-permute-done.12.refs_10_.refs_2_ = bf16[2,64,2048]{2,1,0:T(8,128)(2,1)S(1)} collective-permute-done((bf16[2,64,2048]{2,1,0:T(8,128)(2,1)S(1)}, bf16[2,64,2048]{2,1,0:T(8,128)(2,1)S(1)}, u32[]{:S(2)}, u32[]{:S(2)}) %collective-permute-start.12) | collective-permute-done | bytes 524320 | tf_op jit(solution)/shard_map/ppermute | solution.py:277
  73.4 2.0 %collective-permute-done.15.refs_13_.refs_5_ = bf16[2,64,2048]{2,1,0:T(8,128)(2,1)S(1)} collective-permute-done((bf16[2,64,2048]{2,1,0:T(8,128)(2,1)S(1)}, bf16[2,64,2048]{2,1,0:T(8,128)(2,1)S(1)}, u32[]{:S(2)}, u32[]{:S(2)}) %collective-permute-start.15) | collective-permute-done | bytes 524320 | tf_op jit(solution)/shard_map/ppermute | solution.py:280
  75.3 2.8 %collective-permute-start.17 = (bf16[2,64,2048]{2,1,0:T(8,128)(2,1)S(1)}, bf16[2,64,2048]{2,1,0:T(8,128)(2,1)S(1)}, u32[]{:S(2)}, u32[]{:S(2)}) collective-permute-start(bf16[2,64,2048]{2,1,0:T(8,128)(2,1)S(1)} %collective-permute-done.15.refs_13_.refs_5_), channel_id=1, source_target_pairs={{0,12},{16,19},{1,13},{17,16},{2,14},{18,17},{3,15},{19,18},{4,0},... | collective-permute-start | bytes 1572872 | tf_op jit(solution)/shard_map/ppermute | solution.py:282
  78.1 2.5 %fusion = (f32[4,64,512]{2,1,0:T(8,128)}, f32[4,64,512]{2,1,0:T(8,128)}, f32[4,64,512]{2,1,0:T(8,128)}, f32[4,64,512]{2,1,0:T(8,128)}) fusion(f32[4,128,512]{2,1,0:T(8,128)S(1)} %bitcast.19, f32[4,128,512]{2,1,0:T(8,128)} %bitcast.20), kind=kLoop, calls=%fused_computation.9 | loop fusion | bytes 4194304 | tf_op jit(solution)/shard_map/slice | solution.py:315
  81.0 3.9 %slot_grad_near.3.refs_2_ = bf16[16,64,512]{2,1,0:T(8,128)(2,1)S(1)} custom-call(s32[4]{0:T(128)S(1)} %pad_add_fusion.place_ref, bf16[2048,512]{1,0:T(8,128)(2,1)S(1)} %copy-done, bf16[2,64,2048]{2,1,0:T(8,128)(2,1)S(1)} %constant_dynamic-update-slice_fusion.2.refs_8_.refs_0_, bf16[2,64,2048]{2,1,0:T(8,128)(2,1)S(1)} %constant_dynamic-update-slice_fusion.4.refs_9_.refs_1_, ...), custom_call_target="tpu_custom_call" | custom-call | flops 1610612736 | bytes 6291456 | tf_op jit(solution)/shard_map/slot_grad_near/pallas_call | solution.py:111
  85.1 1.5 collective-permute-done.17.refs_15_.refs_1_
  86.6 1.6 slot_grad_far.3
  93.1 2.2 %next_weights.2 = bf16[4,64,512]{2,1,0:T(8,128)(2,1)} custom-call(s32[16]{0:T(128)S(1)} %bitcast.13, s32[16]{0:T(128)S(1)} %bitcast.16, bf16[16,64,512]{2,1,0:T(8,128)(2,1)S(1)} %all-to-all-done.refs_0_.got_ref, f32[4,64,512]{2,1,0:T(8,128)S(1)} %copy-done.11, f32[4,64,512]{2,1,0:T(8,128)S(1)} %copy-done.10), custom_call_target="tpu_custom_call" | custom-call | bytes 3145728 | tf_op jit(solution)/shard_map/next_weights/pallas_call | solution.py:158
  95.3 43.9 %all_to_all.15.refs_1_.got_ref = bf16[16,64,512]{2,1,0:T(8,128)(2,1)S(1)} all-to-all(bf16[16,64,512]{2,1,0:T(8,128)(2,1)S(1)} %copy-done.3), channel_id=1, replica_groups=mesh['slot'=16,'hid'=16] {'slot'}, dimensions={0} | all-to-all | bytes 2097152 | tf_op jit(solution)/shard_map/all_to_all | solution.py:311
  141.4 2.6 %next_weights.3 = bf16[16,64,512]{2,1,0:T(8,128)(2,1)} custom-call(s32[16]{0:T(128)S(1)} %bitcast.14, s32[16]{0:T(128)S(1)} %bitcast.17, bf16[16,64,512]{2,1,0:T(8,128)(2,1)S(1)} %all_to_all.15.refs_1_.got_ref, f32[4,64,512]{2,1,0:T(8,128)S(1)} %copy-done.9, f32[4,64,512]{2,1,0:T(8,128)S(1)} %copy-done.8), custom_call_target="tpu_custom_call" | custom-call | bytes 3145728 | tf_op jit(solution)/shard_map/next_weights/pallas_call | solution.py:158
  144.0 4.3 %all-to-all-start.2 = ((bf16[16,64,512]{2,1,0:T(8,128)(2,1)}), bf16[16,64,512]{2,1,0:T(8,128)(2,1)}, u32[]{:S(2)}, u32[]{:S(2)}) async-start(bf16[16,64,512]{2,1,0:T(8,128)(2,1)} %next_weights.3), calls=%async_computation.2 | async-start | bytes 2097152 | tf_op jit(solution)/shard_map/all_to_all | solution.py:316
  157.2 1.6 copy-done.32
  158.8 8.0 %input_grad.1 = bf16[2048,512]{1,0:T(8,128)(2,1)} custom-call(s32[4]{0:T(128)S(1)} %pad_add_fusion.place_ref, bf16[512,2048]{1,0:T(8,128)(2,1)S(1)} %bitcast.18, bf16[2,64,2048]{2,1,0:T(8,128)(2,1)} %pad_maximum_fusion.refs_0_, bf16[2,64,2048]{2,1,0:T(8,128)(2,1)} %constant_dynamic-update-slice_fusion.refs_1_, ...), custom_call_target="tpu_custom_call" | custom-call | flops 4294967296 | bytes 12582912 | tf_op jit(solution)/shard_map/input_grad/pallas_call | solution.py:229
  166.8 3.7 %momentum_step.1 = (f32[4,512,128]{2,1,0:T(8,128)}, f32[4,512,128]{2,1,0:T(8,128)}) custom-call(s32[16]{0:T(128)S(1)} %bitcast.15, f32[4,512,128]{2,1,0:T(8,128)S(1)} %copy-done.5, f32[4,512,128]{2,1,0:T(8,128)S(1)} %copy-done.6, bf16[16,64,512]{2,1,0:T(8,128)(2,1)S(1)} %all-to-all-done.refs_0_.got_ref, bf16[16,64,512]{2,1,0:T(8,128)(2,1)S(1)} %all_to_all.15.refs_1_.got_ref), custom_call_target="tpu_custom_call" | custom-call | bytes 8388608 | tf_op jit(solution)/shard_map/momentum_step/pallas_call | solution.py:191
  170.5 4.0 %all-to-all-done.2.own_ref = bf16[16,64,512]{2,1,0:T(8,128)(2,1)} async-done(((bf16[16,64,512]{2,1,0:T(8,128)(2,1)}), bf16[16,64,512]{2,1,0:T(8,128)(2,1)}, u32[]{:S(2)}, u32[]{:S(2)}) %all-to-all-start.2) | async-done | bytes 1048608 | tf_op jit(solution)/shard_map/all_to_all | solution.py:316
  174.4 2.2 %copy-done.7 = bf16[64,64,512]{2,1,0:T(8,128)(2,1)S(1)} copy-done((bf16[64,64,512]{2,1,0:T(8,128)(2,1)S(1)}, bf16[64,64,512]{2,1,0:T(8,128)(2,1)}, u32[]{:S(2)}) %copy-start.7) | copy-done | bytes 4194328
  176.6 6.4 %placed_turn.1 = bf16[512,2048]{1,0:T(8,128)(2,1)} custom-call(s32[1]{0:T(128)} %bitcast.8.wanted_ref, bf16[16,4,64,512]{3,2,1,0:T(8,128)(2,1)S(1)} %bitcast.12, bf16[16,64,512]{2,1,0:T(8,128)(2,1)} %all-to-all-done.2.own_ref), custom_call_target="tpu_custom_call" | custom-call | bytes 4194304 | tf_op jit(solution)/shard_map/placed_turn/pallas_call | solution.py:250
  (102 shorter events, 32.5 us)
Async XLA Ops:
  9.7 27.0 %copy-start.4 = (f32[4,512,128]{2,1,0:T(8,128)S(1)}, f32[4,512,128]{2,1,0:T(8,128)}, u32[]{:S(2)}) copy-start(f32[4,512,128]{2,1,0:T(8,128)} %mom_ref.1) | copy-start | bytes 3145732
  9.7 7.7 %collective-permute-start = (bf16[1,64,2048]{2,1,0:T(8,128)(2,1)S(1)}, bf16[1,64,2048]{2,1,0:T(8,128)(2,1)S(1)}, u32[]{:S(2)}, u32[]{:S(2)}) collective-permute-start(bf16[1,64,2048]{2,1,0:T(8,128)(2,1)S(1)} %get-tuple-element.16), channel_id=1, source_target_pairs={{0,1},{16,20},{1,2},{17,21},{2,3},{18,22},{3,0},{19,23},{4,5},{20,... | collective-permute-start | bytes 786440 | tf_op jit(solution)/shard_map/ppermute | solution.py:269
  11.9 7.7 %collective-permute-start.1 = (bf16[1,64,2048]{2,1,0:T(8,128)(2,1)S(1)}, bf16[1,64,2048]{2,1,0:T(8,128)(2,1)S(1)}, u32[]{:S(2)}, u32[]{:S(2)}) collective-permute-start(bf16[1,64,2048]{2,1,0:T(8,128)(2,1)S(1)} %get-tuple-element.16), channel_id=1, source_target_pairs={{0,3},{16,28},{1,0},{17,29},{2,1},{18,30},{3,2},{19,31},{4,7},{20,... | collective-permute-start | bytes 786440 | tf_op jit(solution)/shard_map/ppermute | solution.py:270
  13.4 8.0 %collective-permute-start.2 = (bf16[1,64,2048]{2,1,0:T(8,128)(2,1)S(1)}, bf16[1,64,2048]{2,1,0:T(8,128)(2,1)S(1)}, u32[]{:S(2)}, u32[]{:S(2)}) collective-permute-start(bf16[1,64,2048]{2,1,0:T(8,128)(2,1)S(1)} %get-tuple-element.16), channel_id=1, source_target_pairs={{0,2},{16,24},{1,3},{17,25},{2,0},{18,26},{3,1},{19,27},{4,6},{20,... | collective-permute-start | bytes 786440 | tf_op jit(solution)/shard_map/ppermute | solution.py:271
  18.3 11.2 %collective-permute-start.3 = (bf16[2,64,2048]{2,1,0:T(8,128)(2,1)}, bf16[2,64,2048]{2,1,0:T(8,128)(2,1)}, u32[]{:S(2)}, u32[]{:S(2)}) collective-permute-start(bf16[2,64,2048]{2,1,0:T(8,128)(2,1)} %pad_maximum_fusion.refs_0_), channel_id=1, source_target_pairs={{0,4},{16,17},{1,5},{17,18},{2,6},{18,19},{3,7},{19,16},{4,8},{20,... | collective-permute-start | bytes 1572872 | tf_op jit(solution)/shard_map/ppermute | solution.py:277
  22.1 19.2 %copy-start = (bf16[2048,512]{1,0:T(8,128)(2,1)S(1)}, bf16[2048,512]{1,0:T(8,128)(2,1)}, u32[]{:S(2)}) copy-start(bf16[2048,512]{1,0:T(8,128)(2,1)} %hidden_ref.3) | copy-start | bytes 6291460
  22.1 8.9 %collective-permute-start.6 = (bf16[2,64,2048]{2,1,0:T(8,128)(2,1)}, bf16[2,64,2048]{2,1,0:T(8,128)(2,1)}, u32[]{:S(2)}, u32[]{:S(2)}) collective-permute-start(bf16[2,64,2048]{2,1,0:T(8,128)(2,1)} %constant_dynamic-update-slice_fusion.refs_1_), channel_id=1, source_target_pairs={{0,12},{16,19},{1,13},{17,16},{2,14},{18,17},{3,15},{19,18},{4,0},... | collective-permute-start | bytes 1572872 | tf_op jit(solution)/shard_map/ppermute | solution.py:280
  24.6 14.0 %collective-permute-start.5 = (bf16[2,64,2048]{2,1,0:T(8,128)(2,1)}, bf16[2,64,2048]{2,1,0:T(8,128)(2,1)}, u32[]{:S(2)}, u32[]{:S(2)}) collective-permute-start(bf16[2,64,2048]{2,1,0:T(8,128)(2,1)} %pad_maximum_fusion.refs_0_), channel_id=1, source_target_pairs={{0,12},{16,19},{1,13},{17,16},{2,14},{18,17},{3,15},{19,18},{4,0},... | collective-permute-start | bytes 1572872 | tf_op jit(solution)/shard_map/ppermute | solution.py:278
  24.8 16.4 %collective-permute-start.4 = (bf16[2,64,2048]{2,1,0:T(8,128)(2,1)}, bf16[2,64,2048]{2,1,0:T(8,128)(2,1)}, u32[]{:S(2)}, u32[]{:S(2)}) collective-permute-start(bf16[2,64,2048]{2,1,0:T(8,128)(2,1)} %constant_dynamic-update-slice_fusion.refs_1_), channel_id=1, source_target_pairs={{0,4},{16,17},{1,5},{17,18},{2,6},{18,19},{3,7},{19,16},{4,8},{20,... | collective-permute-start | bytes 1572872 | tf_op jit(solution)/shard_map/ppermute | solution.py:279
  29.5 17.0 %collective-permute-start.7 = (bf16[2,64,2048]{2,1,0:T(8,128)(2,1)}, bf16[2,64,2048]{2,1,0:T(8,128)(2,1)}, u32[]{:S(2)}, u32[]{:S(2)}) collective-permute-start(bf16[2,64,2048]{2,1,0:T(8,128)(2,1)} %collective-permute-done.3.refs_2_), channel_id=1, source_target_pairs={{0,4},{16,17},{1,5},{17,18},{2,6},{18,19},{3,7},{19,16},{4,8},{20,... | collective-permute-start | bytes 1572872 | tf_op jit(solution)/shard_map/ppermute | solution.py:281
  31.0 15.5 %collective-permute-start.8 = (bf16[2,64,2048]{2,1,0:T(8,128)(2,1)}, bf16[2,64,2048]{2,1,0:T(8,128)(2,1)}, u32[]{:S(2)}, u32[]{:S(2)}) collective-permute-start(bf16[2,64,2048]{2,1,0:T(8,128)(2,1)} %collective-permute-done.6.refs_5_), channel_id=1, source_target_pairs={{0,12},{16,19},{1,13},{17,16},{2,14},{18,17},{3,15},{19,18},{4,0},... | collective-permute-start | bytes 1572872 | tf_op jit(solution)/shard_map/ppermute | solution.py:282
  38.0 28.0 %collective-permute-start.11 = (bf16[1,64,2048]{2,1,0:T(8,128)(2,1)S(1)}, bf16[1,64,2048]{2,1,0:T(8,128)(2,1)}, u32[]{:S(2)}, u32[]{:S(2)}) collective-permute-start(bf16[1,64,2048]{2,1,0:T(8,128)(2,1)S(1)} %get-tuple-element.18), channel_id=1, source_target_pairs={{0,2},{16,24},{1,3},{17,25},{2,0},{18,26},{3,1},{19,27},{4,6},{20,... | collective-permute-start | bytes 786440 | tf_op jit(solution)/shard_map/ppermute | solution.py:271
  38.6 26.4 %collective-permute-start.10 = (bf16[1,64,2048]{2,1,0:T(8,128)(2,1)S(1)}, bf16[1,64,2048]{2,1,0:T(8,128)(2,1)}, u32[]{:S(2)}, u32[]{:S(2)}) collective-permute-start(bf16[1,64,2048]{2,1,0:T(8,128)(2,1)S(1)} %get-tuple-element.18), channel_id=1, source_target_pairs={{0,3},{16,28},{1,0},{17,29},{2,1},{18,30},{3,2},{19,31},{4,7},{20,... | collective-permute-start | bytes 786440 | tf_op jit(solution)/shard_map/ppermute | solution.py:270
  41.3 21.3 %collective-permute-start.9 = (bf16[1,64,2048]{2,1,0:T(8,128)(2,1)S(1)}, bf16[1,64,2048]{2,1,0:T(8,128)(2,1)}, u32[]{:S(2)}, u32[]{:S(2)}) collective-permute-start(bf16[1,64,2048]{2,1,0:T(8,128)(2,1)S(1)} %get-tuple-element.18), channel_id=1, source_target_pairs={{0,1},{16,20},{1,2},{17,21},{2,3},{18,22},{3,0},{19,23},{4,5},{20,... | collective-permute-start | bytes 786440 | tf_op jit(solution)/shard_map/ppermute | solution.py:269
  49.8 41.1 %all-to-all-start = ((bf16[16,64,512]{2,1,0:T(8,128)(2,1)}), bf16[16,64,512]{2,1,0:T(8,128)(2,1)S(1)}, u32[]{:S(2)}, u32[]{:S(2)}) async-start(bf16[16,64,512]{2,1,0:T(8,128)(2,1)} %copy-done.1), calls=%async_computation | async-start | bytes 2097152 | tf_op jit(solution)/shard_map/all_to_all | solution.py:309
  62.4 112.0 %all-gather.3.cloned.1.call-start = ((), (), s32[]{:S(2)}) async-start(), calls=%async_computation.3 | async-start | bytes 4456448 | tf_op jit(solution)/shard_map/all_gather | solution.py:314
  62.5 15.6 %copy-start.33 = (f32[4,512,128]{1,2,0:T(8,128)S(1)}, f32[4,512,128]{1,2,0:T(8,128)}, u32[]{:S(2)}) copy-start(f32[4,512,128]{1,2,0:T(8,128)} %copy.17) | copy-start | bytes 3145732
  63.6 17.4 %copy-start.14 = (bf16[2,64,2048]{2,1,0:T(8,128)(2,1)}, bf16[2,64,2048]{2,1,0:T(8,128)(2,1)S(1)}, u32[]{:S(2)}) copy-start(bf16[2,64,2048]{2,1,0:T(8,128)(2,1)S(1)} %constant_dynamic-update-slice_fusion.2.refs_8_.refs_0_) | copy-start | bytes 1572868
  63.6 9.8 %collective-permute-start.12 = (bf16[2,64,2048]{2,1,0:T(8,128)(2,1)S(1)}, bf16[2,64,2048]{2,1,0:T(8,128)(2,1)S(1)}, u32[]{:S(2)}, u32[]{:S(2)}) collective-permute-start(bf16[2,64,2048]{2,1,0:T(8,128)(2,1)S(1)} %constant_dynamic-update-slice_fusion.2.refs_8_.refs_0_), channel_id=1, source_target_pairs={{0,4},{16,17},{1,5},{17,18},{2,6},{18,19},{3,7},{19,16},{4,8},{20,... | collective-permute-start | bytes 1572872 | tf_op jit(solution)/shard_map/ppermute | solution.py:277
  66.9 17.9 %copy-start.12 = (bf16[2,64,2048]{2,1,0:T(8,128)(2,1)}, bf16[2,64,2048]{2,1,0:T(8,128)(2,1)S(1)}, u32[]{:S(2)}) copy-start(bf16[2,64,2048]{2,1,0:T(8,128)(2,1)S(1)} %constant_dynamic-update-slice_fusion.4.refs_9_.refs_1_) | copy-start | bytes 1572868
  66.9 8.4 %collective-permute-start.15 = (bf16[2,64,2048]{2,1,0:T(8,128)(2,1)S(1)}, bf16[2,64,2048]{2,1,0:T(8,128)(2,1)S(1)}, u32[]{:S(2)}, u32[]{:S(2)}) collective-permute-start(bf16[2,64,2048]{2,1,0:T(8,128)(2,1)S(1)} %constant_dynamic-update-slice_fusion.4.refs_9_.refs_1_), channel_id=1, source_target_pairs={{0,12},{16,19},{1,13},{17,16},{2,14},{18,17},{3,15},{19,18},{4,0},... | collective-permute-start | bytes 1572872 | tf_op jit(solution)/shard_map/ppermute | solution.py:280
  68.6 12.4 %collective-permute-start.14 = (bf16[2,64,2048]{2,1,0:T(8,128)(2,1)S(1)}, bf16[2,64,2048]{2,1,0:T(8,128)(2,1)S(1)}, u32[]{:S(2)}, u32[]{:S(2)}) collective-permute-start(bf16[2,64,2048]{2,1,0:T(8,128)(2,1)S(1)} %constant_dynamic-update-slice_fusion.2.refs_8_.refs_0_), channel_id=1, source_target_pairs={{0,12},{16,19},{1,13},{17,16},{2,14},{18,17},{3,15},{19,18},{4,0},... | collective-permute-start | bytes 1572872 | tf_op jit(solution)/shard_map/ppermute | solution.py:278
  70.0 11.0 %collective-permute-start.13 = (bf16[2,64,2048]{2,1,0:T(8,128)(2,1)S(1)}, bf16[2,64,2048]{2,1,0:T(8,128)(2,1)S(1)}, u32[]{:S(2)}, u32[]{:S(2)}) collective-permute-start(bf16[2,64,2048]{2,1,0:T(8,128)(2,1)S(1)} %constant_dynamic-update-slice_fusion.4.refs_9_.refs_1_), channel_id=1, source_target_pairs={{0,4},{16,17},{1,5},{17,18},{2,6},{18,19},{3,7},{19,16},{4,8},{20,... | collective-permute-start | bytes 1572872 | tf_op jit(solution)/shard_map/ppermute | solution.py:279
  73.4 11.5 %copy-start.16 = (bf16[2,64,2048]{2,1,0:T(8,128)(2,1)}, bf16[2,64,2048]{2,1,0:T(8,128)(2,1)S(1)}, u32[]{:S(2)}) copy-start(bf16[2,64,2048]{2,1,0:T(8,128)(2,1)S(1)} %collective-permute-done.12.refs_10_.refs_2_) | copy-start | bytes 1572868
  73.4 11.7 %collective-permute-start.16 = (bf16[2,64,2048]{2,1,0:T(8,128)(2,1)S(1)}, bf16[2,64,2048]{2,1,0:T(8,128)(2,1)S(1)}, u32[]{:S(2)}, u32[]{:S(2)}) collective-permute-start(bf16[2,64,2048]{2,1,0:T(8,128)(2,1)S(1)} %collective-permute-done.12.refs_10_.refs_2_), channel_id=1, source_target_pairs={{0,4},{16,17},{1,5},{17,18},{2,6},{18,19},{3,7},{19,16},{4,8},{20,... | collective-permute-start | bytes 1572872 | tf_op jit(solution)/shard_map/ppermute | solution.py:281
  75.3 9.5 %copy-start.18 = (bf16[2,64,2048]{2,1,0:T(8,128)(2,1)}, bf16[2,64,2048]{2,1,0:T(8,128)(2,1)S(1)}, u32[]{:S(2)}) copy-start(bf16[2,64,2048]{2,1,0:T(8,128)(2,1)S(1)} %collective-permute-done.15.refs_13_.refs_5_) | copy-start | bytes 1572868
  75.3 11.2 %collective-permute-start.17 = (bf16[2,64,2048]{2,1,0:T(8,128)(2,1)S(1)}, bf16[2,64,2048]{2,1,0:T(8,128)(2,1)S(1)}, u32[]{:S(2)}, u32[]{:S(2)}) collective-permute-start(bf16[2,64,2048]{2,1,0:T(8,128)(2,1)S(1)} %collective-permute-done.15.refs_13_.refs_5_), channel_id=1, source_target_pairs={{0,12},{16,19},{1,13},{17,16},{2,14},{18,17},{3,15},{19,18},{4,0},... | collective-permute-start | bytes 1572872 | tf_op jit(solution)/shard_map/ppermute | solution.py:282
  84.9 6.0 %copy-start.29 = (s32[16,1]{0,1:T(1,128)S(1)}, s32[16,1]{0,1:T(1,128)}, u32[]{:S(2)}) copy-start(s32[16,1]{0,1:T(1,128)} %param.11) | copy-start | bytes 196
  84.9 6.0 %copy-start.30 = (s32[16,1]{0,1:T(1,128)S(1)}, s32[16,1]{0,1:T(1,128)}, u32[]{:S(2)}) copy-start(s32[16,1]{0,1:T(1,128)} %param.12) | copy-start | bytes 196
  144.0 30.5 %all-to-all-start.2 = ((bf16[16,64,512]{2,1,0:T(8,128)(2,1)}), bf16[16,64,512]{2,1,0:T(8,128)(2,1)}, u32[]{:S(2)}, u32[]{:S(2)}) async-start(bf16[16,64,512]{2,1,0:T(8,128)(2,1)} %next_weights.3), calls=%async_computation.2 | async-start | bytes 2097152 | tf_op jit(solution)/shard_map/all_to_all | solution.py:316
  158.8 8.0 %copy-start.5 = (f32[4,512,128]{2,1,0:T(8,128)S(1)}, f32[4,512,128]{2,1,0:T(8,128)}, u32[]{:S(2)}) copy-start(f32[4,512,128]{2,1,0:T(8,128)} %mom_ref.1) | copy-start | bytes 3145732
  158.8 8.0 %copy-start.6 = (f32[4,512,128]{2,1,0:T(8,128)S(1)}, f32[4,512,128]{2,1,0:T(8,128)}, u32[]{:S(2)}) copy-start(f32[4,512,128]{2,1,0:T(8,128)} %mas_ref.1) | copy-start | bytes 3145732
  (23 other events, 34.0 us)
Sparse Core Ops, SparseCore 0:
  95.4 64.5 all-gather.2

commit v3 on v2

v3 whole, which is shorter than its diff:
```python
import functools

import jax
import jax.numpy as jnp
from jax import lax
from jax.experimental import pallas as pl
from jax.experimental.pallas import tpu as pltpu
from jax.sharding import PartitionSpec as P

momentum_decay = 0.9
learn_rate = 0.01
BOTH = ("slot", "hid")
VM = pl.BlockSpec(memory_space=pltpu.VMEM)
SM = pl.BlockSpec(memory_space=pltpu.SMEM)
HBM = pl.BlockSpec(memory_space=pltpu.HBM)
MIB = 1 << 20


def params(mib):
    return pltpu.CompilerParams(vmem_limit_bytes=mib * MIB)


def cost(flops, moved):
    return pl.CostEstimate(flops=flops, bytes_accessed=moved, transcendentals=0)


def position(z, core, y, x):
    return (z * 2 + core) * 16 + y * 4 + x


def line_pairs(step):
    pairs = []
    for z in range(8):
        for y in range(4):
            for x in range(4):
                pairs.append((position(z, 0, y, x), position(z, 0, y, (x + step) % 4)))
                pairs.append((position(z, 1, y, x), position(z, 1, (y + step) % 4, x)))
    return pairs


def cross_pairs(step):
    pairs = []
    for z in range(8):
        for y in range(4):
            for x in range(4):
                pairs.append((position(z, 0, y, x), position(z, 0, (y + step) % 4, x)))
                pairs.append((position(z, 1, y, x), position(z, 1, y, (x + step) % 4)))
    return pairs


def mask_kernel(place_ref, counts_ref, cot_ref, out_ref):
    live = lax.broadcasted_iota(jnp.int32, cot_ref.shape, 0) < counts_ref[place_ref[3]]
    out_ref[...] = jnp.where(live, cot_ref[...], jnp.zeros_like(cot_ref)).T


def masked_block(place, counts, cotangent):
    return pl.pallas_call(
        mask_kernel,
        out_shape=jax.ShapeDtypeStruct(cotangent.shape[::-1], jnp.bfloat16),
        in_specs=[SM, SM, VM],
        out_specs=VM,
        compiler_params=params(16),
        cost_estimate=cost(0, 1 * MIB),
        name="mask_turn",
    )(place, counts, cotangent)


STEPS = (0, 3, 1, 2)
GROUPS = (0, 3, 1, 2)


def block_of(place_ref, group, k):
    cross = lax.rem(place_ref[1] + group, 4)
    line = lax.rem(place_ref[2] + k, 4)
    return jnp.where(place_ref[0] == 0, 4 * cross + line, 4 * line + cross)


def fetch(refs, held, sems):
    copies = [
        pltpu.make_async_copy(ref, held.at[n], sems.at[n]) for n, ref in enumerate(refs)
    ]
    for copy in copies:
        copy.start()
    return copies


def slot_grad_kernel(groups, place_ref, hidden_ref, *refs):
    piece_refs, (out_ref, held, stage, in_sems, sems) = refs[: 4 * len(groups)], refs[-5:]
    loads = fetch(piece_refs, held, in_sems)
    copies = []
    _, size, rows = held.shape
    for i, group in enumerate(groups):
        for load in loads[4 * i : 4 * i + 4]:
            load.wait()
        grad = jnp.dot(
            held[4 * i : 4 * i + 4].reshape(4 * size, rows),
            hidden_ref[...],
            preferred_element_type=jnp.float32,
        ).astype(jnp.bfloat16)
        for at, k in enumerate(STEPS):
            n = len(copies)
            stage[n] = grad[at * size : (at + 1) * size]
            copy = pltpu.make_async_copy(
                stage.at[n], out_ref.at[block_of(place_ref, group, k)], sems.at[n]
            )
            copy.start()
            copies.append(copy)
    for copy in copies:
        copy.wait()


def slot_grad(place, hidden, pieces, groups, into):
    size, rows = pieces[0].shape
    width = hidden.shape[1]
    extra = () if into is None else (into,)
    return pl.pallas_call(
        functools.partial(slot_grad_kernel, groups),
        out_shape=jax.ShapeDtypeStruct((16, size, width), jnp.bfloat16),
        in_specs=[SM, VM] + [HBM] * (len(pieces) + len(extra)),
        out_specs=HBM,
        input_output_aliases={2 + len(pieces): 0} if extra else {},
        scratch_shapes=[
            pltpu.VMEM((len(pieces), size, rows), jnp.bfloat16),
            pltpu.VMEM((len(pieces), size, width), jnp.bfloat16),
            pltpu.SemaphoreType.DMA((len(pieces),)),
            pltpu.SemaphoreType.DMA((len(pieces),)),
        ],
        compiler_params=params(32),
        cost_estimate=cost(2 * len(pieces) * size * width * rows, 6 * MIB),
        name="slot_grad",
    )(place, hidden, *pieces, *extra)


def expert_sum(now_ref, got_ref, e, at):
    total = None
    for s in range(got_ref.shape[0]):
        part = (now_ref[s] == e).astype(jnp.float32) * got_ref[s, at].astype(jnp.float32)
        total = part if total is None else total + part
    return total


def next_weights_kernel(now_ref, next_ref, got_ref, base_ref, out_ref, rounded):
    experts, size, _ = base_ref.shape
    step = 32

    def rows_of(i, carry):
        at = pl.ds(pl.multiple_of(i * step, step), step)
        for e in range(experts):
            total = expert_sum(now_ref, got_ref, e, at)
            rounded[e, at] = (base_ref[e, at] - learn_rate * total).astype(jnp.bfloat16)
        return carry

    lax.fori_loop(0, size // step, rows_of, 0)
    for s in range(out_ref.shape[0]):
        out_ref[s] = rounded[next_ref[s]]


def next_weights(now, following, got, base):
    return pl.pallas_call(
        next_weights_kernel,
        out_shape=jax.ShapeDtypeStruct(got.shape, jnp.bfloat16),
        in_specs=[SM, SM, VM, VM],
        out_specs=VM,
        scratch_shapes=[pltpu.VMEM(base.shape, jnp.bfloat16)],
        compiler_params=params(16),
        cost_estimate=cost(0, 6 * MIB),
        name="next_weights",
    )(now, following, got, base)


def update_kernel(now_ref, mom_ref, mas_ref, got_ref, new_mom_ref, new_mas_ref, total):
    e = pl.program_id(0)
    for first in range(0, total.shape[0], 16):
        total[first : first + 16] = expert_sum(now_ref, got_ref, e, pl.ds(first, 16))
    new_mom = momentum_decay * mom_ref[0] + total[...].T
    new_mom_ref[0] = new_mom
    new_mas_ref[0] = mas_ref[0] - learn_rate * new_mom


def update(now, momentum, master, got):
    experts, width, columns = momentum.shape
    block = pl.BlockSpec((1, width, columns), lambda e: (e, 0, 0))
    return pl.pallas_call(
        update_kernel,
        grid=(experts,),
        out_shape=[jax.ShapeDtypeStruct(momentum.shape, jnp.float32)] * 2,
        in_specs=[SM, block, block, pl.BlockSpec(got.shape, lambda e: (0, 0, 0))],
        out_specs=[block, block],
        scratch_shapes=[pltpu.VMEM((columns, width), jnp.float32)],
        compiler_params=params(24),
        cost_estimate=cost(0, 8 * MIB),
        name="momentum_step",
    )(now, momentum, master, got)


def input_grad_kernel(place_ref, weight_ref, *refs):
    piece_refs, (out_ref, held, sems) = refs[:-3], refs[-3:]
    tile = out_ref.shape[0]
    tiles = held.shape[-1] // tile
    now = pl.program_id(0)

    def load(n, t):
        part = pl.ds(t * tile, tile)
        return pltpu.make_async_copy(
            piece_refs[n].at[:, part], held.at[n, :, part], sems.at[t, n]
        )

    @pl.when(now == 0)
    def _():
        for t in range(tiles):
            for n in range(len(piece_refs)):
                load(n, t).start()

    here = pl.multiple_of(now * tile, tile)
    for n in range(len(piece_refs)):
        part = pl.ds(here, tile)
        pltpu.make_async_copy(
            piece_refs[n].at[:, part], held.at[n, :, part], sems.at[now, n]
        ).wait()
    total = None
    for i, group in enumerate(GROUPS):
        rows_of_group, columns = [], []
        for n, k in enumerate(STEPS):
            rows_of_group.append(held[4 * i + n, :, pl.ds(here, tile)])
            start = pl.multiple_of(block_of(place_ref, group, k) * 128, 128)
            columns.append(weight_ref[:, pl.ds(start, 128)])
        left = jnp.concatenate(rows_of_group, axis=0).T
        right = jnp.concatenate(columns, axis=1)
        part = lax.dot_general(
            left, right, (((1,), (1,)), ((), ())), preferred_element_type=jnp.float32
        )
        total = part if total is None else total + part
    out_ref[...] = total.astype(jnp.bfloat16)


def input_gradient(place, weights, pieces):
    tile = 512
    width = weights.shape[0]
    rows = pieces[0].shape[1]
    return pl.pallas_call(
        input_grad_kernel,
        grid=(rows // tile,),
        out_shape=jax.ShapeDtypeStruct((rows, width), jnp.bfloat16),
        in_specs=[SM, VM] + [HBM] * len(pieces),
        out_specs=pl.BlockSpec((tile, width), lambda i: (i, 0)),
        scratch_shapes=[
            pltpu.VMEM((len(pieces),) + pieces[0].shape, jnp.bfloat16),
            pltpu.SemaphoreType.DMA((rows // tile, len(pieces))),
        ],
        compiler_params=params(32),
        cost_estimate=cost(2 * rows * width * weights.shape[1], 12 * MIB),
        name="input_grad",
    )(place, weights, *pieces)


def placed_kernel(got_ref, out_ref):
    for j in range(got_ref.shape[0]):
        out_ref[:, j * 128 : (j + 1) * 128] = got_ref[j].T


def place_weights(got):
    slots, size, width = got.shape
    return pl.pallas_call(
        placed_kernel,
        out_shape=jax.ShapeDtypeStruct((width, slots * size), jnp.bfloat16),
        in_specs=[VM],
        out_specs=VM,
        compiler_params=params(16),
        cost_estimate=cost(0, 4 * MIB),
        name="placed_turn",
    )(got)


def gather_hid(own):
    on, back, up, down = line_pairs(1), line_pairs(3), cross_pairs(1), cross_pairs(3)
    behind = lax.ppermute(own, BOTH, on)
    ahead = lax.ppermute(own, BOTH, back)
    below = [lax.ppermute(own, BOTH, up)]
    above = [lax.ppermute(own, BOTH, down)]
    across = lax.ppermute(behind, BOTH, on)
    line = [own, behind, ahead, across]
    below += [lax.ppermute(p, BOTH, up) for p in line[1:]]
    above += [lax.ppermute(p, BOTH, down) for p in line[1:]]
    far = [lax.ppermute(p, BOTH, up) for p in below[:2]]
    far += [lax.ppermute(p, BOTH, down) for p in above[2:]]
    return line, below, above, far


def local(cotangent, hidden, weights, slot_experts, next_experts, row_counts, master, momentum):
    slot = lax.axis_index("slot")
    hid = lax.axis_index("hid")
    core = slot & 1
    y, x = hid >> 2, hid & 3
    place = jnp.stack(
        [core, jnp.where(core == 0, y, x), jnp.where(core == 0, x, y), slot]
    ).astype(jnp.int32)
    now, following = slot_experts[:, 0], next_experts[:, 0]

    line, below, above, far = gather_hid(masked_block(place, row_counts, cotangent))
    grads = slot_grad(place, hidden, line, GROUPS[:1], None)
    grads = slot_grad(place, hidden, below + above, GROUPS[1:3], grads)
    grads = slot_grad(place, hidden, far, GROUPS[3:], grads)
    got = lax.all_to_all(grads, "slot", 0, 0, tiled=True)
    input_grad = input_gradient(place, weights[0], line + below + above + far)
    got, input_grad = lax.optimization_barrier((got, input_grad))
    base = jnp.swapaxes(master - (learn_rate * momentum_decay) * momentum, 1, 2)
    arrived = lax.all_to_all(next_weights(now, following, got, base), "slot", 0, 0, tiled=True)

    new_momentum, new_master = update(now, momentum, master, got)
    placed = place_weights(arrived)[None]
    return (input_grad, new_momentum, new_master, placed)


def solution(mesh):
    return jax.shard_map(
        local,
        mesh=mesh,
        in_specs=(
            P("slot", "hid"),
            P("slot", "hid"),
            P("slot", "hid", None),
            P(),
            P(),
            P(),
            P(None, "hid", "slot"),
            P(None, "hid", "slot"),
        ),
        out_specs=(
            P("slot", "hid"),
            P(None, "hid", "slot"),
            P(None, "hid", "slot"),
            P("slot", "hid", None),
        ),
        check_vma=False,
    )
```

time: 193 us -> 188 us (0.974); the launches traced: 190 us -> 187 us
  waiting for transfers between devices: 20.2 us -> 88 us
  blocking collectives: 43.9 us -> 0 us
  between operations: 14.3 us -> 0.96 us
  Pallas kernels: 36.7 us -> 29 us
  local copies, waits for them, and re-layouts: 33.1 us -> 26.2 us
  other arithmetic: 0.93 us -> 2.97 us
    all_to_all x2, waiting for transfers between devices: 3.96 us -> 65.3 us  [the longest x1 44.2 us: local(): lax.all_to_all(next_weights(now, following, got, base), 'slot', 0, 0, til...]
    all_to_all x1 -> x0, blocking collectives: 43.9 us -> none  [local(): gots = (got_first, lax.all_to_all(second_grads, 'slot', 0, 0, tiled=True))]
    ppermute x18 -> x15, waiting for transfers between devices: 16.2 us -> 22.7 us  [the longest x3 6.26 us: gather_hid(): below += [lax.ppermute(p, BOTH, up) for p in line[1:]]]
    pallas_call x4 -> x3, Pallas kernels: 11.9 us -> 6.75 us  [the longest x1 3.59 us: place_weights(): pl.pallas_call(placed_kernel, out_shape=jax.ShapeDtypeStruct((width, slot...]
    pallas_call x4 -> x3, Pallas kernels: 13 us -> 9.6 us  [slot_grad(): pl.pallas_call(functools.partial(slot_grad_kernel, groups), out_shape=jax...]
    transpose x0 -> x1, other arithmetic: none -> 2.9 us  [local(): base = jnp.swapaxes(master - learn_rate * momentum_decay * momentum, 1, 2)]
    concatenate x3 -> x0, local copies, waits for them, and re-layouts: 2.73 us -> none  [the longest x2 1.68 us: gather_line(): jnp.concatenate([ahead, across], axis=0)]
    ppermute x18 -> x15, starting transfers between devices: 23.8 us -> 21.2 us  [the longest x3 4.37 us: gather_hid(): below += [lax.ppermute(p, BOTH, up) for p in line[1:]]]
  transfers between devices with their start and end apart: 21 -> 17, of which waited for: 11 -> 10; matrix products, arithmetic and copies ran while one was open for 6% -> 4% of each run, Pallas kernels for 14% -> 10%
where the time goes in v3:
time: 188 us; the launch traced here: 187 us
  waiting for transfers between devices  88 us (47%)
  starting transfers between devices  40.2 us (21%)
  Pallas kernels  29 us (15%)
  local copies, waits for them, and re-layouts  26.2 us (14%)
  other arithmetic  2.97 us (2%)
    all_to_all x1, waiting for transfers between devices, local(): lax.all_to_all(next_weights(now, following, got, base), 'slot', 0, 0, til...  44.2 us
    unnamed x88, local copies, waits for them, and re-layouts  26.2 us
    all_to_all x1, waiting for transfers between devices, local(): got = lax.all_to_all(grads, 'slot', 0, 0, tiled=True)  21.1 us
    all_to_all x1, starting transfers between devices, local(): got = lax.all_to_all(grads, 'slot', 0, 0, tiled=True)  14 us
    pallas_call x3, Pallas kernels, slot_grad(): pl.pallas_call(functools.partial(slot_grad_kernel, groups), out_shape=jax...  9.6 us
    pallas_call x1, Pallas kernels, input_gradient(): pl.pallas_call(input_grad_kernel, grid=(rows // tile,), out_shape=jax.Sha...  9.04 us
    ppermute x3, waiting for transfers between devices, gather_hid(): below += [lax.ppermute(p, BOTH, up) for p in line[1:]]  6.26 us
    ppermute x2, waiting for transfers between devices, gather_hid(): far = [lax.ppermute(p, BOTH, up) for p in below[:2]]  5.82 us
  transfers between devices with their start and end apart: 17, of which 10 were waited for; matrix products, arithmetic and copies ran while one was open for 4% of the time, Pallas kernels for 10%

profile of v3, /device:TPU:1, one launch (start us, length us, event | category | flops | bytes accessed | tf_op | source)
XLA Modules:
  0.0 187.3 jit_solution(5502273992847590551)
XLA Ops:
  3.2 2.2 %collective-permute-start.2 = (bf16[128,2048]{1,0:T(8,128)(2,1)S(1)}, bf16[128,2048]{1,0:T(8,128)(2,1)S(1)}, u32[]{:S(2)}, u32[]{:S(2)}) collective-permute-start(bf16[128,2048]{1,0:T(8,128)(2,1)S(1)} %mask_turn.1.refs_0_), channel_id=1, source_target_pairs={{0,1},{16,20},{1,2},{17,21},{2,3},{18,22},{3,0},{19,23},{4,5},{20,... | collective-permute-start | bytes 1572872 | tf_op jit(solution)/shard_map/ppermute | solution.py:276
  5.4 1.5 collective-permute-start.5
  8.1 1.5 collective-permute-start.13
  9.6 4.1 %collective-permute-done.2.refs_1_ = bf16[128,2048]{1,0:T(8,128)(2,1)S(1)} collective-permute-done((bf16[128,2048]{1,0:T(8,128)(2,1)S(1)}, bf16[128,2048]{1,0:T(8,128)(2,1)S(1)}, u32[]{:S(2)}, u32[]{:S(2)}) %collective-permute-start.2) | collective-permute-done | bytes 524320 | tf_op jit(solution)/shard_map/ppermute | solution.py:276
  14.7 2.6 %collective-permute-start.3 = (bf16[128,2048]{1,0:T(8,128)(2,1)S(1)}, bf16[128,2048]{1,0:T(8,128)(2,1)S(1)}, u32[]{:S(2)}, u32[]{:S(2)}) collective-permute-start(bf16[128,2048]{1,0:T(8,128)(2,1)S(1)} %collective-permute-done.2.refs_1_), channel_id=1, source_target_pairs={{0,4},{16,17},{1,5},{17,18},{2,6},{18,19},{3,7},{19,16},{4,8},{20,... | collective-permute-start | bytes 1572872 | tf_op jit(solution)/shard_map/ppermute | solution.py:282
  17.3 1.4 collective-permute-start.6
  18.7 3.4 %collective-permute-done.refs_0_.refs_4_ = bf16[128,2048]{1,0:T(8,128)(2,1)S(1)} collective-permute-done((bf16[128,2048]{1,0:T(8,128)(2,1)S(1)}, bf16[128,2048]{1,0:T(8,128)(2,1)S(1)}, u32[]{:S(2)}, u32[]{:S(2)}) %collective-permute-start) | collective-permute-done | bytes 524320 | tf_op jit(solution)/shard_map/ppermute | solution.py:278
  22.0 1.5 collective-permute-start.11
  23.5 1.6 collective-permute-done.8.refs_3_
  25.1 2.6 %collective-permute-start.9 = (bf16[128,2048]{1,0:T(8,128)(2,1)S(1)}, bf16[128,2048]{1,0:T(8,128)(2,1)S(1)}, u32[]{:S(2)}, u32[]{:S(2)}) collective-permute-start(bf16[128,2048]{1,0:T(8,128)(2,1)S(1)} %collective-permute-done.8.refs_3_), channel_id=1, source_target_pairs={{0,12},{16,19},{1,13},{17,16},{2,14},{18,17},{3,15},{19,18},{4,0},... | collective-permute-start | bytes 1572872 | tf_op jit(solution)/shard_map/ppermute | solution.py:283
  28.8 2.2 %collective-permute-start.1 = (bf16[128,2048]{1,0:T(8,128)(2,1)S(1)}, bf16[128,2048]{1,0:T(8,128)(2,1)S(1)}, u32[]{:S(2)}, u32[]{:S(2)}) collective-permute-start(bf16[128,2048]{1,0:T(8,128)(2,1)S(1)} %collective-permute-done.refs_0_.refs_4_), channel_id=1, source_target_pairs={{0,4},{16,17},{1,5},{17,18},{2,6},{18,19},{3,7},{19,16},{4,8},{20,... | collective-permute-start | bytes 1572872 | tf_op jit(solution)/shard_map/ppermute | solution.py:284
  31.0 1.6 collective-permute-done.14.refs_5_.refs_9_
  33.1 5.5 %collective-permute-done.11.refs_2_.refs_6_ = bf16[128,2048]{1,0:T(8,128)(2,1)S(1)} collective-permute-done((bf16[128,2048]{1,0:T(8,128)(2,1)S(1)}, bf16[128,2048]{1,0:T(8,128)(2,1)S(1)}, u32[]{:S(2)}, u32[]{:S(2)}) %collective-permute-start.11) | collective-permute-done | bytes 524320 | tf_op jit(solution)/shard_map/ppermute | solution.py:282
  38.6 2.7 %collective-permute-start.10 = (bf16[128,2048]{1,0:T(8,128)(2,1)S(1)}, bf16[128,2048]{1,0:T(8,128)(2,1)S(1)}, u32[]{:S(2)}, u32[]{:S(2)}) collective-permute-start(bf16[128,2048]{1,0:T(8,128)(2,1)S(1)} %collective-permute-done.9.refs_7_.refs_11_), channel_id=1, source_target_pairs={{0,12},{16,19},{1,13},{17,16},{2,14},{18,17},{3,15},{19,18},{4,0},... | collective-permute-start | bytes 1572872 | tf_op jit(solution)/shard_map/ppermute | solution.py:285
  41.3 1.6 copy-done
  42.9 2.7 %slot_grad.3.refs_8_ = bf16[16,128,512]{2,1,0:T(8,128)(2,1)} custom-call(s32[4]{0:T(128)S(1)} %pad_add_fusion.place_ref, bf16[2048,512]{1,0:T(8,128)(2,1)S(1)} %copy-done, bf16[128,2048]{1,0:T(8,128)(2,1)S(1)} %mask_turn.1.refs_0_, bf16[128,2048]{1,0:T(8,128)(2,1)S(1)} %collective-permute-done.2.refs_1_, ...), custom_call_target="tpu_custom_call" | custom-call | flops 1073741824 | bytes 6291456 | tf_op jit(solution)/shard_map/slot_grad/pallas_call | solution.py:116
  45.8 4.2 %slot_grad.4.refs_4_ = bf16[16,128,512]{2,1,0:T(8,128)(2,1)} custom-call(s32[4]{0:T(128)S(1)} %pad_add_fusion.place_ref, bf16[2048,512]{1,0:T(8,128)(2,1)S(1)} %copy-done.1, bf16[128,2048]{1,0:T(8,128)(2,1)S(1)} %collective-permute-done.refs_0_.refs_4_, ...), custom_call_target="tpu_custom_call", output_to_operand_aliasing={{}: (10, {})} | custom-call | flops 2147483648 | bytes 6291456 | tf_op jit(solution)/shard_map/slot_grad/pallas_call | solution.py:116
  50.2 5.6 %collective-permute-done.4.refs_1_.refs_13_ = bf16[128,2048]{1,0:T(8,128)(2,1)S(1)} collective-permute-done((bf16[128,2048]{1,0:T(8,128)(2,1)S(1)}, bf16[128,2048]{1,0:T(8,128)(2,1)S(1)}, u32[]{:S(2)}, u32[]{:S(2)}) %collective-permute-start.4) | collective-permute-done | bytes 524320 | tf_op jit(solution)/shard_map/ppermute | solution.py:284
  55.8 2.7 %slot_grad.5 = bf16[16,128,512]{2,1,0:T(8,128)(2,1)} custom-call(s32[4]{0:T(128)S(1)} %pad_add_fusion.place_ref, bf16[2048,512]{1,0:T(8,128)(2,1)S(1)} %copy-done.1, bf16[128,2048]{1,0:T(8,128)(2,1)S(1)} %collective-permute-done.1.refs_0_.refs_12_, bf16[128,2048]{1,0:T(8,128)(2,1)S(1)} %collective-permute-done.4.refs_1_.refs_13_, ...), custom_call_target="tpu_custom_call", output_to_operand_aliasing={{}: (6, {})} | custom-call | flops 1073741824 | bytes 6291456 | tf_op jit(solution)/shard_map/slot_grad/pallas_call | solution.py:116
  61.8 14.0 %all-to-all-start = ((bf16[16,128,512]{2,1,0:T(8,128)(2,1)}), bf16[16,128,512]{2,1,0:T(8,128)(2,1)S(1)}, u32[]{:S(2)}, u32[]{:S(2)}) async-start(bf16[16,128,512]{2,1,0:T(8,128)(2,1)} %slot_grad.5), calls=%async_computation | async-start | bytes 4194304 | tf_op jit(solution)/shard_map/all_to_all | solution.py:303
  75.8 1.3 copy.14
  77.1 2.5 %copy.15 = f32[4,512,128]{1,2,0:T(8,128)} copy(f32[4,512,128]{2,1,0:T(8,128)} %mas_ref.1) | data formatting | bytes 2097152 | tf_op args[6]
  79.6 2.9 %subtract_bitcast_fusion.base_ref = f32[4,128,512]{2,1,0:T(8,128)} fusion(f32[4,512,128]{1,2,0:T(8,128)} %copy.15, f32[4,512,128]{1,2,0:T(8,128)} %copy.14), kind=kLoop, calls=%fused_computation | loop fusion | flops 524288 | bytes 3145728 | tf_op jit(solution)/shard_map/transpose | solution.py:306
  93.0 1.6 copy-done.42
  94.6 9.0 %input_grad.1 = bf16[2048,512]{1,0:T(8,128)(2,1)} custom-call(s32[4]{0:T(128)S(1)} %pad_add_fusion.place_ref, bf16[512,2048]{1,0:T(8,128)(2,1)S(1)} %bitcast.13, bf16[128,2048]{1,0:T(8,128)(2,1)S(1)} %copy-done.7, bf16[128,2048]{1,0:T(8,128)(2,1)S(1)} %copy-done.9, bf16[128,2048]{1,0:T(8,128)(2,1)S(1)} %copy-done.11, bf16[128,2048]{1,0:T(8,128)(2,1)S(1)} %copy-done.13, ...), custom_call_target="tpu_custom_call" | custom-call | flops 4294967296 | bytes 12582912 | tf_op jit(solution)/shard_map/input_grad/pallas_call | solution.py:240
  103.7 21.1 %all-to-all-done.got_ref = bf16[16,128,512]{2,1,0:T(8,128)(2,1)S(1)} async-done(((bf16[16,128,512]{2,1,0:T(8,128)(2,1)}), bf16[16,128,512]{2,1,0:T(8,128)(2,1)S(1)}, u32[]{:S(2)}, u32[]{:S(2)}) %all-to-all-start) | async-done | bytes 2097184 | tf_op jit(solution)/shard_map/all_to_all | solution.py:303
  126.0 2.4 %next_weights.1 = bf16[16,128,512]{2,1,0:T(8,128)(2,1)S(1)} custom-call(s32[16]{0:T(128)S(1)} %bitcast.10, s32[16]{0:T(128)S(1)} %bitcast.12, bf16[16,128,512]{2,1,0:T(8,128)(2,1)S(1)} %all-to-all-done.got_ref, f32[4,128,512]{2,1,0:T(8,128)S(1)} %copy-done.5), custom_call_target="tpu_custom_call" | custom-call | bytes 6291456 | tf_op jit(solution)/shard_map/next_weights/pallas_call | solution.py:159
  128.4 1.3 copy-done.2
  129.7 5.0 %all-to-all-start.1 = ((bf16[16,128,512]{2,1,0:T(8,128)(2,1)}), bf16[16,128,512]{2,1,0:T(8,128)(2,1)}, u32[]{:S(2)}, u32[]{:S(2)}) async-start(bf16[16,128,512]{2,1,0:T(8,128)(2,1)} %copy-done.2), calls=%async_computation.1 | async-start | bytes 4194304 | tf_op jit(solution)/shard_map/all_to_all | solution.py:307
  135.9 3.6 %momentum_step.1 = (f32[4,512,128]{2,1,0:T(8,128)}, f32[4,512,128]{2,1,0:T(8,128)}) custom-call(s32[16]{0:T(128)S(1)} %bitcast.11, f32[4,512,128]{2,1,0:T(8,128)S(1)} %copy-done.3, f32[4,512,128]{2,1,0:T(8,128)S(1)} %copy-done.4, bf16[16,128,512]{2,1,0:T(8,128)(2,1)S(1)} %all-to-all-done.got_ref), custom_call_target="tpu_custom_call" | custom-call | bytes 8388608 | tf_op jit(solution)/shard_map/momentum_step/pallas_call | solution.py:183
  139.5 44.2 %all-to-all-done.1.got_ref = bf16[16,128,512]{2,1,0:T(8,128)(2,1)} async-done(((bf16[16,128,512]{2,1,0:T(8,128)(2,1)}), bf16[16,128,512]{2,1,0:T(8,128)(2,1)}, u32[]{:S(2)}, u32[]{:S(2)}) %all-to-all-start.1) | async-done | bytes 2097184 | tf_op jit(solution)/shard_map/all_to_all | solution.py:307
  183.7 3.6 %placed_turn.1 = bf16[512,2048]{1,0:T(8,128)(2,1)} custom-call(bf16[16,128,512]{2,1,0:T(8,128)(2,1)} %all-to-all-done.1.got_ref), custom_call_target="tpu_custom_call" | custom-call | bytes 4194304 | tf_op jit(solution)/shard_map/placed_turn/pallas_call | solution.py:263
  (100 shorter events, 22.8 us)
Async XLA Ops:
  3.2 42.4 %copy-start.6 = (bf16[128,2048]{1,0:T(8,128)(2,1)}, bf16[128,2048]{1,0:T(8,128)(2,1)S(1)}, u32[]{:S(2)}) copy-start(bf16[128,2048]{1,0:T(8,128)(2,1)S(1)} %mask_turn.1.refs_0_) | copy-start | bytes 1572868
  3.2 10.5 %collective-permute-start.2 = (bf16[128,2048]{1,0:T(8,128)(2,1)S(1)}, bf16[128,2048]{1,0:T(8,128)(2,1)S(1)}, u32[]{:S(2)}, u32[]{:S(2)}) collective-permute-start(bf16[128,2048]{1,0:T(8,128)(2,1)S(1)} %mask_turn.1.refs_0_), channel_id=1, source_target_pairs={{0,1},{16,20},{1,2},{17,21},{2,3},{18,22},{3,0},{19,23},{4,5},{20,... | collective-permute-start | bytes 1572872 | tf_op jit(solution)/shard_map/ppermute | solution.py:276
  5.4 11.9 %collective-permute-start.5 = (bf16[128,2048]{1,0:T(8,128)(2,1)S(1)}, bf16[128,2048]{1,0:T(8,128)(2,1)S(1)}, u32[]{:S(2)}, u32[]{:S(2)}) collective-permute-start(bf16[128,2048]{1,0:T(8,128)(2,1)S(1)} %mask_turn.1.refs_0_), channel_id=1, source_target_pairs={{0,3},{16,28},{1,0},{17,29},{2,1},{18,30},{3,2},{19,31},{4,7},{20,... | collective-permute-start | bytes 1572872 | tf_op jit(solution)/shard_map/ppermute | solution.py:277
  6.9 15.1 %collective-permute-start = (bf16[128,2048]{1,0:T(8,128)(2,1)S(1)}, bf16[128,2048]{1,0:T(8,128)(2,1)S(1)}, u32[]{:S(2)}, u32[]{:S(2)}) collective-permute-start(bf16[128,2048]{1,0:T(8,128)(2,1)S(1)} %mask_turn.1.refs_0_), channel_id=1, source_target_pairs={{0,4},{16,17},{1,5},{17,18},{2,6},{18,19},{3,7},{19,16},{4,8},{20,... | collective-permute-start | bytes 1572872 | tf_op jit(solution)/shard_map/ppermute | solution.py:278
  8.1 13.9 %collective-permute-start.13 = (bf16[128,2048]{1,0:T(8,128)(2,1)S(1)}, bf16[128,2048]{1,0:T(8,128)(2,1)S(1)}, u32[]{:S(2)}, u32[]{:S(2)}) collective-permute-start(bf16[128,2048]{1,0:T(8,128)(2,1)S(1)} %mask_turn.1.refs_0_), channel_id=1, source_target_pairs={{0,12},{16,19},{1,13},{17,16},{2,14},{18,17},{3,15},{19,18},{4,0},... | collective-permute-start | bytes 1572872 | tf_op jit(solution)/shard_map/ppermute | solution.py:279
  13.7 31.9 %copy-start.8 = (bf16[128,2048]{1,0:T(8,128)(2,1)}, bf16[128,2048]{1,0:T(8,128)(2,1)S(1)}, u32[]{:S(2)}) copy-start(bf16[128,2048]{1,0:T(8,128)(2,1)S(1)} %collective-permute-done.2.refs_1_) | copy-start | bytes 1572868
  13.7 11.4 %collective-permute-start.8 = (bf16[128,2048]{1,0:T(8,128)(2,1)S(1)}, bf16[128,2048]{1,0:T(8,128)(2,1)S(1)}, u32[]{:S(2)}, u32[]{:S(2)}) collective-permute-start(bf16[128,2048]{1,0:T(8,128)(2,1)S(1)} %collective-permute-done.2.refs_1_), channel_id=1, source_target_pairs={{0,1},{16,20},{1,2},{17,21},{2,3},{18,22},{3,0},{19,23},{4,5},{20,... | collective-permute-start | bytes 1572872 | tf_op jit(solution)/shard_map/ppermute | solution.py:280
  14.7 13.7 %collective-permute-start.3 = (bf16[128,2048]{1,0:T(8,128)(2,1)S(1)}, bf16[128,2048]{1,0:T(8,128)(2,1)S(1)}, u32[]{:S(2)}, u32[]{:S(2)}) collective-permute-start(bf16[128,2048]{1,0:T(8,128)(2,1)S(1)} %collective-permute-done.2.refs_1_), channel_id=1, source_target_pairs={{0,4},{16,17},{1,5},{17,18},{2,6},{18,19},{3,7},{19,16},{4,8},{20,... | collective-permute-start | bytes 1572872 | tf_op jit(solution)/shard_map/ppermute | solution.py:282
  17.3 28.3 %copy-start.10 = (bf16[128,2048]{1,0:T(8,128)(2,1)}, bf16[128,2048]{1,0:T(8,128)(2,1)S(1)}, u32[]{:S(2)}) copy-start(bf16[128,2048]{1,0:T(8,128)(2,1)S(1)} %collective-permute-done.5.refs_2_) | copy-start | bytes 1572868
  17.3 11.4 %collective-permute-start.6 = (bf16[128,2048]{1,0:T(8,128)(2,1)S(1)}, bf16[128,2048]{1,0:T(8,128)(2,1)S(1)}, u32[]{:S(2)}, u32[]{:S(2)}) collective-permute-start(bf16[128,2048]{1,0:T(8,128)(2,1)S(1)} %collective-permute-done.5.refs_2_), channel_id=1, source_target_pairs={{0,12},{16,19},{1,13},{17,16},{2,14},{18,17},{3,15},{19,18},{4,0},... | collective-permute-start | bytes 1572872 | tf_op jit(solution)/shard_map/ppermute | solution.py:283
  22.0 23.6 %copy-start.23 = (bf16[128,2048]{1,0:T(8,128)(2,1)}, bf16[128,2048]{1,0:T(8,128)(2,1)S(1)}, u32[]{:S(2)}) copy-start(bf16[128,2048]{1,0:T(8,128)(2,1)S(1)} %collective-permute-done.refs_0_.refs_4_) | copy-start | bytes 1572868
  22.0 10.5 %collective-permute-start.14 = (bf16[128,2048]{1,0:T(8,128)(2,1)S(1)}, bf16[128,2048]{1,0:T(8,128)(2,1)S(1)}, u32[]{:S(2)}, u32[]{:S(2)}) collective-permute-start(bf16[128,2048]{1,0:T(8,128)(2,1)S(1)} %collective-permute-done.2.refs_1_), channel_id=1, source_target_pairs={{0,12},{16,19},{1,13},{17,16},{2,14},{18,17},{3,15},{19,18},{4,0},... | collective-permute-start | bytes 1572872 | tf_op jit(solution)/shard_map/ppermute | solution.py:283
  22.0 23.6 %copy-start.25 = (bf16[128,2048]{1,0:T(8,128)(2,1)}, bf16[128,2048]{1,0:T(8,128)(2,1)S(1)}, u32[]{:S(2)}) copy-start(bf16[128,2048]{1,0:T(8,128)(2,1)S(1)} %collective-permute-done.13.refs_4_.refs_8_) | copy-start | bytes 1572868
  22.0 16.6 %collective-permute-start.11 = (bf16[128,2048]{1,0:T(8,128)(2,1)S(1)}, bf16[128,2048]{1,0:T(8,128)(2,1)S(1)}, u32[]{:S(2)}, u32[]{:S(2)}) collective-permute-start(bf16[128,2048]{1,0:T(8,128)(2,1)S(1)} %collective-permute-done.5.refs_2_), channel_id=1, source_target_pairs={{0,4},{16,17},{1,5},{17,18},{2,6},{18,19},{3,7},{19,16},{4,8},{20,... | collective-permute-start | bytes 1572872 | tf_op jit(solution)/shard_map/ppermute | solution.py:282
  25.1 20.6 %copy-start.12 = (bf16[128,2048]{1,0:T(8,128)(2,1)}, bf16[128,2048]{1,0:T(8,128)(2,1)S(1)}, u32[]{:S(2)}) copy-start(bf16[128,2048]{1,0:T(8,128)(2,1)S(1)} %collective-permute-done.8.refs_3_) | copy-start | bytes 1572868
  25.1 13.6 %collective-permute-start.9 = (bf16[128,2048]{1,0:T(8,128)(2,1)S(1)}, bf16[128,2048]{1,0:T(8,128)(2,1)S(1)}, u32[]{:S(2)}, u32[]{:S(2)}) collective-permute-start(bf16[128,2048]{1,0:T(8,128)(2,1)S(1)} %collective-permute-done.8.refs_3_), channel_id=1, source_target_pairs={{0,12},{16,19},{1,13},{17,16},{2,14},{18,17},{3,15},{19,18},{4,0},... | collective-permute-start | bytes 1572872 | tf_op jit(solution)/shard_map/ppermute | solution.py:283
  28.4 17.3 %copy-start.27 = (bf16[128,2048]{1,0:T(8,128)(2,1)}, bf16[128,2048]{1,0:T(8,128)(2,1)S(1)}, u32[]{:S(2)}) copy-start(bf16[128,2048]{1,0:T(8,128)(2,1)S(1)} %collective-permute-done.3.refs_1_.refs_5_) | copy-start | bytes 1572868
  28.4 17.2 %collective-permute-start.12 = (bf16[128,2048]{1,0:T(8,128)(2,1)S(1)}, bf16[128,2048]{1,0:T(8,128)(2,1)S(1)}, u32[]{:S(2)}, u32[]{:S(2)}) collective-permute-start(bf16[128,2048]{1,0:T(8,128)(2,1)S(1)} %collective-permute-done.8.refs_3_), channel_id=1, source_target_pairs={{0,4},{16,17},{1,5},{17,18},{2,6},{18,19},{3,7},{19,16},{4,8},{20,... | collective-permute-start | bytes 1572872 | tf_op jit(solution)/shard_map/ppermute | solution.py:282
  28.8 16.9 %copy-start.29 = (bf16[128,2048]{1,0:T(8,128)(2,1)}, bf16[128,2048]{1,0:T(8,128)(2,1)S(1)}, u32[]{:S(2)}) copy-start(bf16[128,2048]{1,0:T(8,128)(2,1)S(1)} %collective-permute-done.6.refs_6_.refs_10_) | copy-start | bytes 1572868
  28.8 21.4 %collective-permute-start.1 = (bf16[128,2048]{1,0:T(8,128)(2,1)S(1)}, bf16[128,2048]{1,0:T(8,128)(2,1)S(1)}, u32[]{:S(2)}, u32[]{:S(2)}) collective-permute-start(bf16[128,2048]{1,0:T(8,128)(2,1)S(1)} %collective-permute-done.refs_0_.refs_4_), channel_id=1, source_target_pairs={{0,4},{16,17},{1,5},{17,18},{2,6},{18,19},{3,7},{19,16},{4,8},{20,... | collective-permute-start | bytes 1572872 | tf_op jit(solution)/shard_map/ppermute | solution.py:284
  32.6 13.1 %copy-start.31 = (bf16[128,2048]{1,0:T(8,128)(2,1)}, bf16[128,2048]{1,0:T(8,128)(2,1)S(1)}, u32[]{:S(2)}) copy-start(bf16[128,2048]{1,0:T(8,128)(2,1)S(1)} %collective-permute-done.14.refs_5_.refs_9_) | copy-start | bytes 1572868
  32.6 23.2 %collective-permute-start.4 = (bf16[128,2048]{1,0:T(8,128)(2,1)S(1)}, bf16[128,2048]{1,0:T(8,128)(2,1)S(1)}, u32[]{:S(2)}, u32[]{:S(2)}) collective-permute-start(bf16[128,2048]{1,0:T(8,128)(2,1)S(1)} %collective-permute-done.3.refs_1_.refs_5_), channel_id=1, source_target_pairs={{0,4},{16,17},{1,5},{17,18},{2,6},{18,19},{3,7},{19,16},{4,8},{20,... | collective-permute-start | bytes 1572872 | tf_op jit(solution)/shard_map/ppermute | solution.py:284
  38.6 7.1 %copy-start.33 = (bf16[128,2048]{1,0:T(8,128)(2,1)}, bf16[128,2048]{1,0:T(8,128)(2,1)S(1)}, u32[]{:S(2)}) copy-start(bf16[128,2048]{1,0:T(8,128)(2,1)S(1)} %collective-permute-done.11.refs_2_.refs_6_) | copy-start | bytes 1572868
  38.6 17.1 %collective-permute-start.7 = (bf16[128,2048]{1,0:T(8,128)(2,1)S(1)}, bf16[128,2048]{1,0:T(8,128)(2,1)S(1)}, u32[]{:S(2)}, u32[]{:S(2)}) collective-permute-start(bf16[128,2048]{1,0:T(8,128)(2,1)S(1)} %collective-permute-done.6.refs_6_.refs_10_), channel_id=1, source_target_pairs={{0,12},{16,19},{1,13},{17,16},{2,14},{18,17},{3,15},{19,18},{4,0},... | collective-permute-start | bytes 1572872 | tf_op jit(solution)/shard_map/ppermute | solution.py:285
  38.6 7.1 %copy-start.35 = (bf16[128,2048]{1,0:T(8,128)(2,1)}, bf16[128,2048]{1,0:T(8,128)(2,1)S(1)}, u32[]{:S(2)}) copy-start(bf16[128,2048]{1,0:T(8,128)(2,1)S(1)} %collective-permute-done.9.refs_7_.refs_11_) | copy-start | bytes 1572868
  38.6 17.1 %collective-permute-start.10 = (bf16[128,2048]{1,0:T(8,128)(2,1)S(1)}, bf16[128,2048]{1,0:T(8,128)(2,1)S(1)}, u32[]{:S(2)}, u32[]{:S(2)}) collective-permute-start(bf16[128,2048]{1,0:T(8,128)(2,1)S(1)} %collective-permute-done.9.refs_7_.refs_11_), channel_id=1, source_target_pairs={{0,12},{16,19},{1,13},{17,16},{2,14},{18,17},{3,15},{19,18},{4,0},... | collective-permute-start | bytes 1572872 | tf_op jit(solution)/shard_map/ppermute | solution.py:285
  45.7 4.2 %copy-start.37 = (bf16[128,2048]{1,0:T(8,128)(2,1)}, bf16[128,2048]{1,0:T(8,128)(2,1)S(1)}, u32[]{:S(2)}) copy-start(bf16[128,2048]{1,0:T(8,128)(2,1)S(1)} %collective-permute-done.12.refs_3_.refs_7_) | copy-start | bytes 1572868
  61.8 14.0 %copy-start.3 = (f32[4,512,128]{2,1,0:T(8,128)S(1)}, f32[4,512,128]{2,1,0:T(8,128)}, u32[]{:S(2)}) copy-start(f32[4,512,128]{2,1,0:T(8,128)} %mom_ref.1) | copy-start | bytes 3145732
  61.8 62.9 %all-to-all-start = ((bf16[16,128,512]{2,1,0:T(8,128)(2,1)}), bf16[16,128,512]{2,1,0:T(8,128)(2,1)S(1)}, u32[]{:S(2)}, u32[]{:S(2)}) async-start(bf16[16,128,512]{2,1,0:T(8,128)(2,1)} %slot_grad.5), calls=%async_computation | async-start | bytes 4194304 | tf_op jit(solution)/shard_map/all_to_all | solution.py:303
  94.6 30.1 %copy-start.39 = (s32[16,1]{0,1:T(1,128)S(1)}, s32[16,1]{0,1:T(1,128)}, u32[]{:S(2)}) copy-start(s32[16,1]{0,1:T(1,128)} %param.11) | copy-start | bytes 196
  94.6 30.1 %copy-start.41 = (s32[16,1]{0,1:T(1,128)S(1)}, s32[16,1]{0,1:T(1,128)}, u32[]{:S(2)}) copy-start(s32[16,1]{0,1:T(1,128)} %param.12) | copy-start | bytes 196
  129.7 54.0 %all-to-all-start.1 = ((bf16[16,128,512]{2,1,0:T(8,128)(2,1)}), bf16[16,128,512]{2,1,0:T(8,128)(2,1)}, u32[]{:S(2)}, u32[]{:S(2)}) async-start(bf16[16,128,512]{2,1,0:T(8,128)(2,1)} %copy-done.2), calls=%async_computation.1 | async-start | bytes 4194304 | tf_op jit(solution)/shard_map/all_to_all | solution.py:307
  (28 other events, 42.8 us)

commit v4 on v3

--- a/solution.py
+++ b/solution.py
@@ -84,14 +84,19 @@
     return copies
 
 
-def slot_grad_kernel(groups, place_ref, hidden_ref, *refs):
-    piece_refs, (out_ref, held, stage, in_sems, sems) = refs[: 4 * len(groups)], refs[-5:]
+def slot_grad_kernel(groups, keep, place_ref, hidden_ref, *refs):
+    piece_refs = refs[: 4 * len(groups)]
+    held, stage, in_sems, sems, keep_sems = refs[-5:]
+    out_ref = refs[-7] if keep else refs[-6]
     loads = fetch(piece_refs, held, in_sems)
-    copies = []
+    copies, kept = [], []
     _, size, rows = held.shape
     for i, group in enumerate(groups):
-        for load in loads[4 * i : 4 * i + 4]:
-            load.wait()
+        for n in range(4 * i, 4 * i + 4):
+            loads[n].wait()
+            if keep:
+                kept.append(pltpu.make_async_copy(held.at[n], refs[-6].at[n], keep_sems.at[n]))
+                kept[n].start()
         grad = jnp.dot(
             held[4 * i : 4 * i + 4].reshape(4 * size, rows),
             hidden_ref[...],
@@ -105,23 +110,27 @@
             )
             copy.start()
             copies.append(copy)
-    for copy in copies:
+    for copy in copies + kept:
         copy.wait()
 
 
-def slot_grad(place, hidden, pieces, groups, into):
+def slot_grad(place, hidden, pieces, groups, into, keep=False):
     size, rows = pieces[0].shape
     width = hidden.shape[1]
     extra = () if into is None else (into,)
-    return pl.pallas_call(
-        functools.partial(slot_grad_kernel, groups),
-        out_shape=jax.ShapeDtypeStruct((16, size, width), jnp.bfloat16),
+    shapes = [jax.ShapeDtypeStruct((16, size, width), jnp.bfloat16)]
+    if keep:
+        shapes.append(jax.ShapeDtypeStruct((len(pieces), size, rows), jnp.bfloat16))
+    return pl.pallas_call(
+        functools.partial(slot_grad_kernel, groups, keep),
+        out_shape=shapes,
         in_specs=[SM, VM] + [HBM] * (len(pieces) + len(extra)),
-        out_specs=HBM,
+        out_specs=[HBM] * len(shapes),
         input_output_aliases={2 + len(pieces): 0} if extra else {},
         scratch_shapes=[
             pltpu.VMEM((len(pieces), size, rows), jnp.bfloat16),
             pltpu.VMEM((len(pieces), size, width), jnp.bfloat16),
+            pltpu.SemaphoreType.DMA((len(pieces),)),
             pltpu.SemaphoreType.DMA((len(pieces),)),
             pltpu.SemaphoreType.DMA((len(pieces),)),
         ],
@@ -194,7 +203,8 @@
 
 
 def input_grad_kernel(place_ref, weight_ref, *refs):
-    piece_refs, (out_ref, held, sems) = refs[:-3], refs[-3:]
+    piece_refs, (far_ref, out_ref, held, sems) = refs[:-4], refs[-4:]
+    piece_refs += tuple(far_ref.at[n] for n in range(4))
     tile = out_ref.shape[0]
     tiles = held.shape[-1] // tile
     now = pl.program_id(0)
@@ -233,7 +243,7 @@
     out_ref[...] = total.astype(jnp.bfloat16)
 
 
-def input_gradient(place, weights, pieces):
+def input_gradient(place, weights, pieces, far):
     tile = 512
     width = weights.shape[0]
     rows = pieces[0].shape[1]
@@ -241,21 +251,30 @@
         input_grad_kernel,
         grid=(rows // tile,),
         out_shape=jax.ShapeDtypeStruct((rows, width), jnp.bfloat16),
-        in_specs=[SM, VM] + [HBM] * len(pieces),
+        in_specs=[SM, VM] + [HBM] * (len(pieces) + 1),
         out_specs=pl.BlockSpec((tile, width), lambda i: (i, 0)),
         scratch_shapes=[
-            pltpu.VMEM((len(pieces),) + pieces[0].shape, jnp.bfloat16),
-            pltpu.SemaphoreType.DMA((rows // tile, len(pieces))),
+            pltpu.VMEM((16,) + pieces[0].shape, jnp.bfloat16),
+            pltpu.SemaphoreType.DMA((rows // tile, 16)),
         ],
         compiler_params=params(32),
         cost_estimate=cost(2 * rows * width * weights.shape[1], 12 * MIB),
         name="input_grad",
-    )(place, weights, *pieces)
-
-
-def placed_kernel(got_ref, out_ref):
-    for j in range(got_ref.shape[0]):
-        out_ref[:, j * 128 : (j + 1) * 128] = got_ref[j].T
+    )(place, weights, *pieces, far)
+
+
+def placed_kernel(got_ref, out_ref, held, turned, in_sems, sems):
+    slots = got_ref.shape[0]
+    loads = fetch([got_ref.at[j] for j in range(slots)], held, in_sems)
+    copies = []
+    for j in range(slots):
+        loads[j].wait()
+        turned[j] = held[j].T
+        columns = pl.ds(j * 128, 128)
+        copies.append(pltpu.make_async_copy(turned.at[j], out_ref.at[:, columns], sems.at[j]))
+        copies[j].start()
+    for copy in copies:
+        copy.wait()
 
 
 def place_weights(got):
@@ -263,8 +282,14 @@
     return pl.pallas_call(
         placed_kernel,
         out_shape=jax.ShapeDtypeStruct((width, slots * size), jnp.bfloat16),
-        in_specs=[VM],
-        out_specs=VM,
+        in_specs=[HBM],
+        out_specs=HBM,
+        scratch_shapes=[
+            pltpu.VMEM(got.shape, jnp.bfloat16),
+            pltpu.VMEM((slots, width, size), jnp.bfloat16),
+            pltpu.SemaphoreType.DMA((slots,)),
+            pltpu.SemaphoreType.DMA((slots,)),
+        ],
         compiler_params=params(16),
         cost_estimate=cost(0, 4 * MIB),
         name="placed_turn",
@@ -297,13 +322,13 @@
     now, following = slot_experts[:, 0], next_experts[:, 0]
 
     line, below, above, far = gather_hid(masked_block(place, row_counts, cotangent))
-    grads = slot_grad(place, hidden, line, GROUPS[:1], None)
-    grads = slot_grad(place, hidden, below + above, GROUPS[1:3], grads)
-    grads = slot_grad(place, hidden, far, GROUPS[3:], grads)
+    (grads,) = slot_grad(place, hidden, line, GROUPS[:1], None)
+    (grads,) = slot_grad(place, hidden, below + above, GROUPS[1:3], grads)
+    grads, far = slot_grad(place, hidden, far, GROUPS[3:], grads, keep=True)
     got = lax.all_to_all(grads, "slot", 0, 0, tiled=True)
-    input_grad = input_gradient(place, weights[0], line + below + above + far)
-    got, input_grad = lax.optimization_barrier((got, input_grad))
-    base = jnp.swapaxes(master - (learn_rate * momentum_decay) * momentum, 1, 2)
+    input_grad = input_gradient(place, weights[0], line + below + above, far)
+    old_master, old_momentum, input_grad = lax.optimization_barrier((master, momentum, input_grad))
+    base = jnp.swapaxes(old_master - (learn_rate * momentum_decay) * old_momentum, 1, 2)
     arrived = lax.all_to_all(next_weights(now, following, got, base), "slot", 0, 0, tiled=True)
 
     new_momentum, new_master = update(now, momentum, master, got)

time: 188 us -> 184 us (0.979)
  starting transfers between devices: 40.2 us -> 36.7 us
    ppermute x3, starting transfers between devices: 3.97 us -> 9.58 us  [gather_hid(): above += [lax.ppermute(p, BOTH, down) for p in line[1:]]]
    unnamed x88 -> x66, local copies, waits for them, and re-layouts: 26.2 us -> 22 us
    all_to_all x1, starting transfers between devices: 14 us -> 10 us  [local(): got = lax.all_to_all(grads, 'slot', 0, 0, tiled=True)]
    optimization_barrier x0 -> x2, local copies, waits for them, and re-layouts: none -> 3.93 us  [local(): lax.optimization_barrier((master, momentum, input_grad))]
    ppermute x3, starting transfers between devices: 4.37 us -> 0.5 us  [gather_hid(): below += [lax.ppermute(p, BOTH, up) for p in line[1:]]]
    ppermute x1, waiting for transfers between devices: 3.35 us -> 0.01 us  [gather_hid(): below = [lax.ppermute(own, BOTH, up)]]
    ppermute x3, waiting for transfers between devices: 6.26 us -> 9.38 us  [gather_hid(): below += [lax.ppermute(p, BOTH, up) for p in line[1:]]]
    ppermute x2, starting transfers between devices: 2.74 us -> 0.01 us  [gather_hid(): far = [lax.ppermute(p, BOTH, up) for p in below[:2]]]
  transfers between devices with their start and end apart: 17 -> 17, of which waited for: 10 -> 10; matrix products, arithmetic and copies ran while one was open for 4% -> 4% of each run, Pallas kernels for 10% -> 11%
where the time goes in v4:
time: 184 us; the launch traced here: 183 us
  waiting for transfers between devices  87.5 us (48%)
  starting transfers between devices  36.7 us (20%)
  Pallas kernels  29 us (16%)
  local copies, waits for them, and re-layouts  25.9 us (14%)
  other arithmetic  2.84 us (2%)
    all_to_all x1, waiting for transfers between devices, local(): lax.all_to_all(next_weights(now, following, got, base), 'slot', 0, 0, til...  44.2 us
    unnamed x66, local copies, waits for them, and re-layouts  22 us
    all_to_all x1, waiting for transfers between devices, local(): got = lax.all_to_all(grads, 'slot', 0, 0, tiled=True)  19.6 us
    all_to_all x1, starting transfers between devices, local(): got = lax.all_to_all(grads, 'slot', 0, 0, tiled=True)  10 us
    pallas_call x3, Pallas kernels, slot_grad(): pl.pallas_call(functools.partial(slot_grad_kernel, groups, keep), out_sha...  9.89 us
    ppermute x3, starting transfers between devices, gather_hid(): above += [lax.ppermute(p, BOTH, down) for p in line[1:]]  9.58 us
    ppermute x3, waiting for transfers between devices, gather_hid(): below += [lax.ppermute(p, BOTH, up) for p in line[1:]]  9.38 us
    pallas_call x1, Pallas kernels, input_gradient(): pl.pallas_call(input_grad_kernel, grid=(rows // tile,), out_shape=jax.Sha...  9.01 us
  transfers between devices with their start and end apart: 17, of which 10 were waited for; matrix products, arithmetic and copies ran while one was open for 4% of the time, Pallas kernels for 11%

profile of v4, /device:TPU:1, one launch (start us, length us, event | category | flops | bytes accessed | tf_op | source)
XLA Modules:
  0.0 183.0 jit_solution(517044691884415132)
XLA Ops:
  3.2 2.2 %collective-permute-start = (bf16[128,2048]{1,0:T(8,128)(2,1)S(1)}, bf16[128,2048]{1,0:T(8,128)(2,1)S(1)}, u32[]{:S(2)}, u32[]{:S(2)}) collective-permute-start(bf16[128,2048]{1,0:T(8,128)(2,1)S(1)} %mask_turn.1.refs_0_), channel_id=1, source_target_pairs={{0,1},{16,20},{1,2},{17,21},{2,3},{18,22},{3,0},{19,23},{4,5},{20,... | collective-permute-start | bytes 1572872 | tf_op jit(solution)/shard_map/ppermute | solution.py:301
  5.4 1.5 collective-permute-start.1
  6.9 2.5 %collective-permute-start.7 = (bf16[128,2048]{1,0:T(8,128)(2,1)S(1)}, bf16[128,2048]{1,0:T(8,128)(2,1)S(1)}, u32[]{:S(2)}, u32[]{:S(2)}) collective-permute-start(bf16[128,2048]{1,0:T(8,128)(2,1)S(1)} %mask_turn.1.refs_0_), channel_id=1, source_target_pairs={{0,12},{16,19},{1,13},{17,16},{2,14},{18,17},{3,15},{19,18},{4,0},... | collective-permute-start | bytes 1572872 | tf_op jit(solution)/shard_map/ppermute | solution.py:304
  9.4 4.3 %collective-permute-done.refs_1_ = bf16[128,2048]{1,0:T(8,128)(2,1)S(1)} collective-permute-done((bf16[128,2048]{1,0:T(8,128)(2,1)S(1)}, bf16[128,2048]{1,0:T(8,128)(2,1)S(1)}, u32[]{:S(2)}, u32[]{:S(2)}) %collective-permute-start) | collective-permute-done | bytes 524320 | tf_op jit(solution)/shard_map/ppermute | solution.py:301
  14.4 5.2 %collective-permute-start.9 = (bf16[128,2048]{1,0:T(8,128)(2,1)S(1)}, bf16[128,2048]{1,0:T(8,128)(2,1)S(1)}, u32[]{:S(2)}, u32[]{:S(2)}) collective-permute-start(bf16[128,2048]{1,0:T(8,128)(2,1)S(1)} %collective-permute-done.1.refs_2_), channel_id=1, source_target_pairs={{0,12},{16,19},{1,13},{17,16},{2,14},{18,17},{3,15},{19,18},{4,0},... | collective-permute-start | bytes 1572872 | tf_op jit(solution)/shard_map/ppermute | solution.py:308
  20.7 3.4 %collective-permute-start.8 = (bf16[128,2048]{1,0:T(8,128)(2,1)S(1)}, bf16[128,2048]{1,0:T(8,128)(2,1)S(1)}, u32[]{:S(2)}, u32[]{:S(2)}) collective-permute-start(bf16[128,2048]{1,0:T(8,128)(2,1)S(1)} %collective-permute-done.refs_1_), channel_id=1, source_target_pairs={{0,12},{16,19},{1,13},{17,16},{2,14},{18,17},{3,15},{19,18},{4,0},... | collective-permute-start | bytes 1572872 | tf_op jit(solution)/shard_map/ppermute | solution.py:308
  24.1 2.5 %collective-permute-done.2.refs_3_ = bf16[128,2048]{1,0:T(8,128)(2,1)S(1)} collective-permute-done((bf16[128,2048]{1,0:T(8,128)(2,1)S(1)}, bf16[128,2048]{1,0:T(8,128)(2,1)S(1)}, u32[]{:S(2)}, u32[]{:S(2)}) %collective-permute-start.2) | collective-permute-done | bytes 524320 | tf_op jit(solution)/shard_map/ppermute | solution.py:305
  28.1 6.0 %collective-permute-done.5.refs_2_.refs_6_ = bf16[128,2048]{1,0:T(8,128)(2,1)S(1)} collective-permute-done((bf16[128,2048]{1,0:T(8,128)(2,1)S(1)}, bf16[128,2048]{1,0:T(8,128)(2,1)S(1)}, u32[]{:S(2)}, u32[]{:S(2)}) %collective-permute-start.5) | collective-permute-done | bytes 524320 | tf_op jit(solution)/shard_map/ppermute | solution.py:307
  34.1 2.7 %collective-permute-start.13 = (bf16[128,2048]{1,0:T(8,128)(2,1)S(1)}, bf16[128,2048]{1,0:T(8,128)(2,1)S(1)}, u32[]{:S(2)}, u32[]{:S(2)}) collective-permute-start(bf16[128,2048]{1,0:T(8,128)(2,1)S(1)} %collective-permute-done.9.refs_6_.refs_10_), channel_id=1, source_target_pairs={{0,12},{16,19},{1,13},{17,16},{2,14},{18,17},{3,15},{19,18},{4,0},... | collective-permute-start | bytes 1572872 | tf_op jit(solution)/shard_map/ppermute | solution.py:310
  36.8 3.4 %collective-permute-done.4.refs_1_.refs_5_ = bf16[128,2048]{1,0:T(8,128)(2,1)S(1)} collective-permute-done((bf16[128,2048]{1,0:T(8,128)(2,1)S(1)}, bf16[128,2048]{1,0:T(8,128)(2,1)S(1)}, u32[]{:S(2)}, u32[]{:S(2)}) %collective-permute-start.4) | collective-permute-done | bytes 524320 | tf_op jit(solution)/shard_map/ppermute | solution.py:307
  40.2 2.7 %collective-permute-start.14 = (bf16[128,2048]{1,0:T(8,128)(2,1)S(1)}, bf16[128,2048]{1,0:T(8,128)(2,1)S(1)}, u32[]{:S(2)}, u32[]{:S(2)}) collective-permute-start(bf16[128,2048]{1,0:T(8,128)(2,1)S(1)} %collective-permute-done.10.refs_7_.refs_11_), channel_id=1, source_target_pairs={{0,12},{16,19},{1,13},{17,16},{2,14},{18,17},{3,15},{19,18},{4,0},... | collective-permute-start | bytes 1572872 | tf_op jit(solution)/shard_map/ppermute | solution.py:310
  42.8 1.6 copy-done
  44.4 2.7 %slot_grad.3.refs_8_ = bf16[16,128,512]{2,1,0:T(8,128)(2,1)} custom-call(s32[4]{0:T(128)S(1)} %pad_add_fusion.place_ref, bf16[2048,512]{1,0:T(8,128)(2,1)S(1)} %copy-done, bf16[128,2048]{1,0:T(8,128)(2,1)S(1)} %mask_turn.1.refs_0_, bf16[128,2048]{1,0:T(8,128)(2,1)S(1)} %collective-permute-done.refs_1_, bf16[128,2048]{1,0:T(8,128)(2,1)S(1)} %collective-permute-done.1.refs_2_, ...), custom_call_target="tpu_custom_call" | custom-call | flops 1073741824 | bytes 6291456 | tf_op jit(solution)/shard_map/slot_grad/pallas_call | solution.py:124
  47.3 4.3 %slot_grad.4.refs_4_ = bf16[16,128,512]{2,1,0:T(8,128)(2,1)} custom-call(s32[4]{0:T(128)S(1)} %pad_add_fusion.place_ref, bf16[2048,512]{1,0:T(8,128)(2,1)S(1)} %copy-done.1, bf16[128,2048]{1,0:T(8,128)(2,1)S(1)} %collective-permute-done.3.refs_0_.refs_4_, ...), custom_call_target="tpu_custom_call", output_to_operand_aliasing={{}: (10, {})} | custom-call | flops 2147483648 | bytes 6291456 | tf_op jit(solution)/shard_map/slot_grad/pallas_call | solution.py:124
  51.7 5.6 %collective-permute-done.12.refs_1_ = bf16[128,2048]{1,0:T(8,128)(2,1)S(1)} collective-permute-done((bf16[128,2048]{1,0:T(8,128)(2,1)S(1)}, bf16[128,2048]{1,0:T(8,128)(2,1)S(1)}, u32[]{:S(2)}, u32[]{:S(2)}) %collective-permute-start.12) | collective-permute-done | bytes 524320 | tf_op jit(solution)/shard_map/ppermute | solution.py:309
  57.3 2.9 %slot_grad.5 = (bf16[16,128,512]{2,1,0:T(8,128)(2,1)}, bf16[4,128,2048]{2,1,0:T(8,128)(2,1)S(1)}) custom-call(s32[4]{0:T(128)S(1)} %pad_add_fusion.place_ref, bf16[2048,512]{1,0:T(8,128)(2,1)S(1)} %copy-done.1, bf16[128,2048]{1,0:T(8,128)(2,1)S(1)} %collective-permute-done.11.refs_0_, ...), custom_call_target="tpu_custom_call", output_to_operand_aliasing={{0}: (6, {})} | custom-call | flops 1073741824 | bytes 6291456 | tf_op jit(solution)/shard_map/slot_grad/pallas_call | solution.py:124
  60.2 1.3 copy-done.31
  61.5 10.0 %all-to-all-start = ((bf16[16,128,512]{2,1,0:T(8,128)(2,1)}), bf16[16,128,512]{2,1,0:T(8,128)(2,1)S(1)}, u32[]{:S(2)}, u32[]{:S(2)}) async-start(bf16[16,128,512]{2,1,0:T(8,128)(2,1)} %get-tuple-element.13), calls=%async_computation | async-start | bytes 4194304 | tf_op jit(solution)/shard_map/all_to_all | solution.py:328
  82.0 1.6 copy-done.30
  83.6 1.6 copy-done.32
  85.2 9.0 %input_grad.1 = bf16[2048,512]{1,0:T(8,128)(2,1)} custom-call(s32[4]{0:T(128)S(1)} %pad_add_fusion.place_ref, bf16[512,2048]{1,0:T(8,128)(2,1)S(1)} %bitcast.13, bf16[128,2048]{1,0:T(8,128)(2,1)S(1)} %mask_turn.1.refs_0_, bf16[128,2048]{1,0:T(8,128)(2,1)S(1)} %collective-permute-done.refs_1_, bf16[128,2048]{1,0:T(8,128)(2,1)S(1)} %copy-done.7, ...), custom_call_target="tpu_custom_call" | custom-call | flops 4294967296 | bytes 12582912 | tf_op jit(solution)/shard_map/input_grad/pallas_call | solution.py:250
  94.2 2.6 %copy.15 = f32[4,512,128]{1,2,0:T(8,128)} copy(f32[4,512,128]{2,1,0:T(8,128)} %mas_ref.1) | data formatting | bytes 2097152 | tf_op jit(solution)/shard_map/optimization_barrier | solution.py:330
  96.8 1.3 copy.14
  98.1 2.8 %subtract_bitcast_fusion.base_ref = f32[4,128,512]{2,1,0:T(8,128)} fusion(f32[4,512,128]{1,2,0:T(8,128)} %copy.15, f32[4,512,128]{1,2,0:T(8,128)} %copy.14), kind=kLoop, calls=%fused_computation | loop fusion | flops 524288 | bytes 3145728 | tf_op jit(solution)/shard_map/transpose | solution.py:331
  100.9 19.6 %all-to-all-done.got_ref = bf16[16,128,512]{2,1,0:T(8,128)(2,1)S(1)} async-done(((bf16[16,128,512]{2,1,0:T(8,128)(2,1)}), bf16[16,128,512]{2,1,0:T(8,128)(2,1)S(1)}, u32[]{:S(2)}, u32[]{:S(2)}) %all-to-all-start) | async-done | bytes 2097184 | tf_op jit(solution)/shard_map/all_to_all | solution.py:328
  120.5 1.2 copy-done.5
  121.7 2.4 %next_weights.1 = bf16[16,128,512]{2,1,0:T(8,128)(2,1)S(1)} custom-call(s32[16]{0:T(128)S(1)} %bitcast.10, s32[16]{0:T(128)S(1)} %bitcast.12, bf16[16,128,512]{2,1,0:T(8,128)(2,1)S(1)} %all-to-all-done.got_ref, f32[4,128,512]{2,1,0:T(8,128)S(1)} %copy-done.5), custom_call_target="tpu_custom_call" | custom-call | bytes 6291456 | tf_op jit(solution)/shard_map/next_weights/pallas_call | solution.py:168
  124.2 1.3 copy-done.2
  125.5 5.0 %all-to-all-start.1 = ((bf16[16,128,512]{2,1,0:T(8,128)(2,1)}), bf16[16,128,512]{2,1,0:T(8,128)(2,1)}, u32[]{:S(2)}, u32[]{:S(2)}) async-start(bf16[16,128,512]{2,1,0:T(8,128)(2,1)} %copy-done.2), calls=%async_computation.1 | async-start | bytes 4194304 | tf_op jit(solution)/shard_map/all_to_all | solution.py:332
  131.7 3.6 %momentum_step.1 = (f32[4,512,128]{2,1,0:T(8,128)}, f32[4,512,128]{2,1,0:T(8,128)}) custom-call(s32[16]{0:T(128)S(1)} %bitcast.11, f32[4,512,128]{2,1,0:T(8,128)S(1)} %copy-done.3, f32[4,512,128]{2,1,0:T(8,128)S(1)} %copy-done.4, bf16[16,128,512]{2,1,0:T(8,128)(2,1)S(1)} %all-to-all-done.got_ref), custom_call_target="tpu_custom_call" | custom-call | bytes 8388608 | tf_op jit(solution)/shard_map/momentum_step/pallas_call | solution.py:192
  135.3 44.2 %all-to-all-done.1.got_ref = bf16[16,128,512]{2,1,0:T(8,128)(2,1)} async-done(((bf16[16,128,512]{2,1,0:T(8,128)(2,1)}), bf16[16,128,512]{2,1,0:T(8,128)(2,1)}, u32[]{:S(2)}, u32[]{:S(2)}) %all-to-all-start.1) | async-done | bytes 2097184 | tf_op jit(solution)/shard_map/all_to_all | solution.py:332
  179.5 3.3 %placed_turn.1 = bf16[512,2048]{1,0:T(8,128)(2,1)} custom-call(bf16[16,128,512]{2,1,0:T(8,128)(2,1)} %all-to-all-done.1.got_ref), custom_call_target="tpu_custom_call" | custom-call | bytes 4194304 | tf_op jit(solution)/shard_map/placed_turn/pallas_call | solution.py:282
  (80 shorter events, 17.6 us)
Async XLA Ops:
  3.2 10.5 %collective-permute-start = (bf16[128,2048]{1,0:T(8,128)(2,1)S(1)}, bf16[128,2048]{1,0:T(8,128)(2,1)S(1)}, u32[]{:S(2)}, u32[]{:S(2)}) collective-permute-start(bf16[128,2048]{1,0:T(8,128)(2,1)S(1)} %mask_turn.1.refs_0_), channel_id=1, source_target_pairs={{0,1},{16,20},{1,2},{17,21},{2,3},{18,22},{3,0},{19,23},{4,5},{20,... | collective-permute-start | bytes 1572872 | tf_op jit(solution)/shard_map/ppermute | solution.py:301
  5.4 9.1 %collective-permute-start.1 = (bf16[128,2048]{1,0:T(8,128)(2,1)S(1)}, bf16[128,2048]{1,0:T(8,128)(2,1)S(1)}, u32[]{:S(2)}, u32[]{:S(2)}) collective-permute-start(bf16[128,2048]{1,0:T(8,128)(2,1)S(1)} %mask_turn.1.refs_0_), channel_id=1, source_target_pairs={{0,3},{16,28},{1,0},{17,29},{2,1},{18,30},{3,2},{19,31},{4,7},{20,... | collective-permute-start | bytes 1572872 | tf_op jit(solution)/shard_map/ppermute | solution.py:302
  6.9 13.8 %collective-permute-start.7 = (bf16[128,2048]{1,0:T(8,128)(2,1)S(1)}, bf16[128,2048]{1,0:T(8,128)(2,1)S(1)}, u32[]{:S(2)}, u32[]{:S(2)}) collective-permute-start(bf16[128,2048]{1,0:T(8,128)(2,1)S(1)} %mask_turn.1.refs_0_), channel_id=1, source_target_pairs={{0,12},{16,19},{1,13},{17,16},{2,14},{18,17},{3,15},{19,18},{4,0},... | collective-permute-start | bytes 1572872 | tf_op jit(solution)/shard_map/ppermute | solution.py:304
  9.4 14.7 %collective-permute-start.3 = (bf16[128,2048]{1,0:T(8,128)(2,1)S(1)}, bf16[128,2048]{1,0:T(8,128)(2,1)S(1)}, u32[]{:S(2)}, u32[]{:S(2)}) collective-permute-start(bf16[128,2048]{1,0:T(8,128)(2,1)S(1)} %mask_turn.1.refs_0_), channel_id=1, source_target_pairs={{0,4},{16,17},{1,5},{17,18},{2,6},{18,19},{3,7},{19,16},{4,8},{20,... | collective-permute-start | bytes 1572872 | tf_op jit(solution)/shard_map/ppermute | solution.py:303
  13.7 12.9 %collective-permute-start.2 = (bf16[128,2048]{1,0:T(8,128)(2,1)S(1)}, bf16[128,2048]{1,0:T(8,128)(2,1)S(1)}, u32[]{:S(2)}, u32[]{:S(2)}) collective-permute-start(bf16[128,2048]{1,0:T(8,128)(2,1)S(1)} %collective-permute-done.refs_1_), channel_id=1, source_target_pairs={{0,1},{16,20},{1,2},{17,21},{2,3},{18,22},{3,0},{19,23},{4,5},{20,... | collective-permute-start | bytes 1572872 | tf_op jit(solution)/shard_map/ppermute | solution.py:305
  14.4 32.7 %copy-start.6 = (bf16[128,2048]{1,0:T(8,128)(2,1)}, bf16[128,2048]{1,0:T(8,128)(2,1)S(1)}, u32[]{:S(2)}) copy-start(bf16[128,2048]{1,0:T(8,128)(2,1)S(1)} %collective-permute-done.1.refs_2_) | copy-start | bytes 1572868
  14.4 13.2 %collective-permute-start.9 = (bf16[128,2048]{1,0:T(8,128)(2,1)S(1)}, bf16[128,2048]{1,0:T(8,128)(2,1)S(1)}, u32[]{:S(2)}, u32[]{:S(2)}) collective-permute-start(bf16[128,2048]{1,0:T(8,128)(2,1)S(1)} %collective-permute-done.1.refs_2_), channel_id=1, source_target_pairs={{0,12},{16,19},{1,13},{17,16},{2,14},{18,17},{3,15},{19,18},{4,0},... | collective-permute-start | bytes 1572872 | tf_op jit(solution)/shard_map/ppermute | solution.py:308
  19.7 14.4 %collective-permute-start.5 = (bf16[128,2048]{1,0:T(8,128)(2,1)S(1)}, bf16[128,2048]{1,0:T(8,128)(2,1)S(1)}, u32[]{:S(2)}, u32[]{:S(2)}) collective-permute-start(bf16[128,2048]{1,0:T(8,128)(2,1)S(1)} %collective-permute-done.1.refs_2_), channel_id=1, source_target_pairs={{0,4},{16,17},{1,5},{17,18},{2,6},{18,19},{3,7},{19,16},{4,8},{20,... | collective-permute-start | bytes 1572872 | tf_op jit(solution)/shard_map/ppermute | solution.py:307
  20.7 26.5 %copy-start.11 = (bf16[128,2048]{1,0:T(8,128)(2,1)}, bf16[128,2048]{1,0:T(8,128)(2,1)S(1)}, u32[]{:S(2)}) copy-start(bf16[128,2048]{1,0:T(8,128)(2,1)S(1)} %collective-permute-done.7.refs_4_.refs_8_) | copy-start | bytes 1572868
  20.7 13.4 %collective-permute-start.8 = (bf16[128,2048]{1,0:T(8,128)(2,1)S(1)}, bf16[128,2048]{1,0:T(8,128)(2,1)S(1)}, u32[]{:S(2)}, u32[]{:S(2)}) collective-permute-start(bf16[128,2048]{1,0:T(8,128)(2,1)S(1)} %collective-permute-done.refs_1_), channel_id=1, source_target_pairs={{0,12},{16,19},{1,13},{17,16},{2,14},{18,17},{3,15},{19,18},{4,0},... | collective-permute-start | bytes 1572872 | tf_op jit(solution)/shard_map/ppermute | solution.py:308
  24.1 23.1 %copy-start.13 = (bf16[128,2048]{1,0:T(8,128)(2,1)}, bf16[128,2048]{1,0:T(8,128)(2,1)S(1)}, u32[]{:S(2)}) copy-start(bf16[128,2048]{1,0:T(8,128)(2,1)S(1)} %collective-permute-done.3.refs_0_.refs_4_) | copy-start | bytes 1572868
  24.1 16.1 %collective-permute-start.4 = (bf16[128,2048]{1,0:T(8,128)(2,1)S(1)}, bf16[128,2048]{1,0:T(8,128)(2,1)S(1)}, u32[]{:S(2)}, u32[]{:S(2)}) collective-permute-start(bf16[128,2048]{1,0:T(8,128)(2,1)S(1)} %collective-permute-done.refs_1_), channel_id=1, source_target_pairs={{0,4},{16,17},{1,5},{17,18},{2,6},{18,19},{3,7},{19,16},{4,8},{20,... | collective-permute-start | bytes 1572872 | tf_op jit(solution)/shard_map/ppermute | solution.py:307
  26.6 20.6 %copy-start.8 = (bf16[128,2048]{1,0:T(8,128)(2,1)}, bf16[128,2048]{1,0:T(8,128)(2,1)S(1)}, u32[]{:S(2)}) copy-start(bf16[128,2048]{1,0:T(8,128)(2,1)S(1)} %collective-permute-done.2.refs_3_) | copy-start | bytes 1572868
  26.6 13.5 %collective-permute-start.10 = (bf16[128,2048]{1,0:T(8,128)(2,1)S(1)}, bf16[128,2048]{1,0:T(8,128)(2,1)S(1)}, u32[]{:S(2)}, u32[]{:S(2)}) collective-permute-start(bf16[128,2048]{1,0:T(8,128)(2,1)S(1)} %collective-permute-done.2.refs_3_), channel_id=1, source_target_pairs={{0,12},{16,19},{1,13},{17,16},{2,14},{18,17},{3,15},{19,18},{4,0},... | collective-permute-start | bytes 1572872 | tf_op jit(solution)/shard_map/ppermute | solution.py:308
  27.6 19.6 %copy-start.15 = (bf16[128,2048]{1,0:T(8,128)(2,1)}, bf16[128,2048]{1,0:T(8,128)(2,1)S(1)}, u32[]{:S(2)}) copy-start(bf16[128,2048]{1,0:T(8,128)(2,1)S(1)} %collective-permute-done.9.refs_6_.refs_10_) | copy-start | bytes 1572868
  27.6 19.6 %collective-permute-start.6 = (bf16[128,2048]{1,0:T(8,128)(2,1)S(1)}, bf16[128,2048]{1,0:T(8,128)(2,1)S(1)}, u32[]{:S(2)}, u32[]{:S(2)}) collective-permute-start(bf16[128,2048]{1,0:T(8,128)(2,1)S(1)} %collective-permute-done.2.refs_3_), channel_id=1, source_target_pairs={{0,4},{16,17},{1,5},{17,18},{2,6},{18,19},{3,7},{19,16},{4,8},{20,... | collective-permute-start | bytes 1572872 | tf_op jit(solution)/shard_map/ppermute | solution.py:307
  34.1 13.2 %copy-start.17 = (bf16[128,2048]{1,0:T(8,128)(2,1)}, bf16[128,2048]{1,0:T(8,128)(2,1)S(1)}, u32[]{:S(2)}) copy-start(bf16[128,2048]{1,0:T(8,128)(2,1)S(1)} %collective-permute-done.5.refs_2_.refs_6_) | copy-start | bytes 1572868
  34.1 17.6 %collective-permute-start.11 = (bf16[128,2048]{1,0:T(8,128)(2,1)S(1)}, bf16[128,2048]{1,0:T(8,128)(2,1)S(1)}, u32[]{:S(2)}, u32[]{:S(2)}) collective-permute-start(bf16[128,2048]{1,0:T(8,128)(2,1)S(1)} %collective-permute-done.3.refs_0_.refs_4_), channel_id=1, source_target_pairs={{0,4},{16,17},{1,5},{17,18},{2,6},{18,19},{3,7},{19,16},{4,8},{20,... | collective-permute-start | bytes 1572872 | tf_op jit(solution)/shard_map/ppermute | solution.py:309
  34.1 13.2 %copy-start.19 = (bf16[128,2048]{1,0:T(8,128)(2,1)}, bf16[128,2048]{1,0:T(8,128)(2,1)S(1)}, u32[]{:S(2)}) copy-start(bf16[128,2048]{1,0:T(8,128)(2,1)S(1)} %collective-permute-done.8.refs_5_.refs_9_) | copy-start | bytes 1572868
  34.1 17.6 %collective-permute-start.13 = (bf16[128,2048]{1,0:T(8,128)(2,1)S(1)}, bf16[128,2048]{1,0:T(8,128)(2,1)S(1)}, u32[]{:S(2)}, u32[]{:S(2)}) collective-permute-start(bf16[128,2048]{1,0:T(8,128)(2,1)S(1)} %collective-permute-done.9.refs_6_.refs_10_), channel_id=1, source_target_pairs={{0,12},{16,19},{1,13},{17,16},{2,14},{18,17},{3,15},{19,18},{4,0},... | collective-permute-start | bytes 1572872 | tf_op jit(solution)/shard_map/ppermute | solution.py:310
  40.2 7.1 %copy-start.21 = (bf16[128,2048]{1,0:T(8,128)(2,1)}, bf16[128,2048]{1,0:T(8,128)(2,1)S(1)}, u32[]{:S(2)}) copy-start(bf16[128,2048]{1,0:T(8,128)(2,1)S(1)} %collective-permute-done.4.refs_1_.refs_5_) | copy-start | bytes 1572868
  40.2 17.1 %collective-permute-start.12 = (bf16[128,2048]{1,0:T(8,128)(2,1)S(1)}, bf16[128,2048]{1,0:T(8,128)(2,1)S(1)}, u32[]{:S(2)}, u32[]{:S(2)}) collective-permute-start(bf16[128,2048]{1,0:T(8,128)(2,1)S(1)} %collective-permute-done.4.refs_1_.refs_5_), channel_id=1, source_target_pairs={{0,4},{16,17},{1,5},{17,18},{2,6},{18,19},{3,7},{19,16},{4,8},{20,... | collective-permute-start | bytes 1572872 | tf_op jit(solution)/shard_map/ppermute | solution.py:309
  40.2 7.1 %copy-start.23 = (bf16[128,2048]{1,0:T(8,128)(2,1)}, bf16[128,2048]{1,0:T(8,128)(2,1)S(1)}, u32[]{:S(2)}) copy-start(bf16[128,2048]{1,0:T(8,128)(2,1)S(1)} %collective-permute-done.10.refs_7_.refs_11_) | copy-start | bytes 1572868
  40.2 17.1 %collective-permute-start.14 = (bf16[128,2048]{1,0:T(8,128)(2,1)S(1)}, bf16[128,2048]{1,0:T(8,128)(2,1)S(1)}, u32[]{:S(2)}, u32[]{:S(2)}) collective-permute-start(bf16[128,2048]{1,0:T(8,128)(2,1)S(1)} %collective-permute-done.10.refs_7_.refs_11_), channel_id=1, source_target_pairs={{0,12},{16,19},{1,13},{17,16},{2,14},{18,17},{3,15},{19,18},{4,0},... | collective-permute-start | bytes 1572872 | tf_op jit(solution)/shard_map/ppermute | solution.py:310
  42.8 1.6 copy-start
  44.4 2.9 %copy-start.1 = (bf16[2048,512]{1,0:T(8,128)(2,1)S(1)}, bf16[2048,512]{1,0:T(8,128)(2,1)}, u32[]{:S(2)}) copy-start(bf16[2048,512]{1,0:T(8,128)(2,1)} %hidden_ref.5) | copy-start | bytes 6291460
  47.3 4.3 %copy-start.25 = (bf16[128,2048]{1,0:T(8,128)(2,1)}, bf16[128,2048]{1,0:T(8,128)(2,1)S(1)}, u32[]{:S(2)}) copy-start(bf16[128,2048]{1,0:T(8,128)(2,1)S(1)} %collective-permute-done.6.refs_3_.refs_7_) | copy-start | bytes 1572868
  61.5 59.0 %all-to-all-start = ((bf16[16,128,512]{2,1,0:T(8,128)(2,1)}), bf16[16,128,512]{2,1,0:T(8,128)(2,1)S(1)}, u32[]{:S(2)}, u32[]{:S(2)}) async-start(bf16[16,128,512]{2,1,0:T(8,128)(2,1)} %get-tuple-element.13), calls=%async_computation | async-start | bytes 4194304 | tf_op jit(solution)/shard_map/all_to_all | solution.py:328
  94.2 2.6 %copy-start.3 = (f32[4,512,128]{2,1,0:T(8,128)S(1)}, f32[4,512,128]{2,1,0:T(8,128)}, u32[]{:S(2)}) copy-start(f32[4,512,128]{2,1,0:T(8,128)} %mom_ref.1) | copy-start | bytes 3145732
  98.1 22.4 %copy-start.27 = (s32[16,1]{0,1:T(1,128)S(1)}, s32[16,1]{0,1:T(1,128)}, u32[]{:S(2)}) copy-start(s32[16,1]{0,1:T(1,128)} %param.11) | copy-start | bytes 196
  98.1 22.4 %copy-start.29 = (s32[16,1]{0,1:T(1,128)S(1)}, s32[16,1]{0,1:T(1,128)}, u32[]{:S(2)}) copy-start(s32[16,1]{0,1:T(1,128)} %param.12) | copy-start | bytes 196
  125.5 54.0 %all-to-all-start.1 = ((bf16[16,128,512]{2,1,0:T(8,128)(2,1)}), bf16[16,128,512]{2,1,0:T(8,128)(2,1)}, u32[]{:S(2)}, u32[]{:S(2)}) async-start(bf16[16,128,512]{2,1,0:T(8,128)(2,1)} %copy-done.2), calls=%async_computation.1 | async-start | bytes 4194304 | tf_op jit(solution)/shard_map/all_to_all | solution.py:332
  (18 other events, 20.4 us)

commit v5 on v4

--- a/solution.py
+++ b/solution.py
@@ -85,12 +85,28 @@
 
 
 def slot_grad_kernel(groups, keep, place_ref, hidden_ref, *refs):
-    piece_refs = refs[: 4 * len(groups)]
+    count = 4 * len(groups)
+    piece_refs = refs[:count]
+    second_half = ()
+    if keep:
+        second_half, piece_refs = refs[2:3], refs[:2] + refs[3 : count + 1]
     held, stage, in_sems, sems, keep_sems = refs[-5:]
     out_ref = refs[-7] if keep else refs[-6]
-    loads = fetch(piece_refs, held, in_sems)
-    copies, kept = [], []
     _, size, rows = held.shape
+    loads, copies, kept = [], [], []
+    for n, ref in enumerate(piece_refs):
+        loads.append(
+            pltpu.make_async_copy(ref, held.at[n, pl.ds(0, ref.shape[0])], in_sems.at[n])
+        )
+    for ref in second_half:
+        half = ref.shape[0]
+        loads.append(
+            pltpu.make_async_copy(ref, held.at[1, pl.ds(size - half, half)], in_sems.at[count])
+        )
+    for load in loads:
+        load.start()
+    for load in loads[count:]:
+        load.wait()
     for i, group in enumerate(groups):
         for n in range(4 * i, 4 * i + 4):
             loads[n].wait()
@@ -117,10 +133,11 @@
 def slot_grad(place, hidden, pieces, groups, into, keep=False):
     size, rows = pieces[0].shape
     width = hidden.shape[1]
+    blocks = 4 * len(groups)
     extra = () if into is None else (into,)
     shapes = [jax.ShapeDtypeStruct((16, size, width), jnp.bfloat16)]
     if keep:
-        shapes.append(jax.ShapeDtypeStruct((len(pieces), size, rows), jnp.bfloat16))
+        shapes.append(jax.ShapeDtypeStruct((blocks, size, rows), jnp.bfloat16))
     return pl.pallas_call(
         functools.partial(slot_grad_kernel, groups, keep),
         out_shape=shapes,
@@ -128,8 +145,8 @@
         out_specs=[HBM] * len(shapes),
         input_output_aliases={2 + len(pieces): 0} if extra else {},
         scratch_shapes=[
-            pltpu.VMEM((len(pieces), size, rows), jnp.bfloat16),
-            pltpu.VMEM((len(pieces), size, width), jnp.bfloat16),
+            pltpu.VMEM((blocks, size, rows), jnp.bfloat16),
+            pltpu.VMEM((blocks, size, width), jnp.bfloat16),
             pltpu.SemaphoreType.DMA((len(pieces),)),
             pltpu.SemaphoreType.DMA((len(pieces),)),
             pltpu.SemaphoreType.DMA((len(pieces),)),
@@ -306,8 +323,9 @@
     line = [own, behind, ahead, across]
     below += [lax.ppermute(p, BOTH, up) for p in line[1:]]
     above += [lax.ppermute(p, BOTH, down) for p in line[1:]]
-    far = [lax.ppermute(p, BOTH, up) for p in below[:2]]
-    far += [lax.ppermute(p, BOTH, down) for p in above[2:]]
+    half = own.shape[0] // 2
+    far = [lax.ppermute(below[0], BOTH, up), lax.ppermute(below[1][:half], BOTH, up)]
+    far += [lax.ppermute(p, BOTH, down) for p in (above[1][half:], above[2], above[3])]
     return line, below, above, far
 
 

time: 184 us -> 184 us (level)
  starting transfers between devices: 36.7 us -> 42 us
  waiting for transfers between devices: 87.5 us -> 82.8 us
    ppermute x4 -> x5, waiting for transfers between devices: 5.72 us -> 0.55 us  [the longest x1 0.54 us: gather_hid(): lax.ppermute(below[1][:half], BOTH, up)]
    ppermute x3, waiting for transfers between devices: 0.01 us -> 5.06 us  [gather_hid(): above += [lax.ppermute(p, BOTH, down) for p in line[1:]]]
    ppermute x3, waiting for transfers between devices: 9.38 us -> 5.52 us  [gather_hid(): below += [lax.ppermute(p, BOTH, up) for p in line[1:]]]
    all_to_all x1, starting transfers between devices: 10 us -> 13 us  [local(): got = lax.all_to_all(grads, 'slot', 0, 0, tiled=True)]
    ppermute x3, starting transfers between devices: 0.5 us -> 3.46 us  [gather_hid(): below += [lax.ppermute(p, BOTH, up) for p in line[1:]]]
    ppermute x3, starting transfers between devices: 9.58 us -> 7.5 us  [gather_hid(): above += [lax.ppermute(p, BOTH, down) for p in line[1:]]]
    unnamed x66 -> x64, local copies, waits for them, and re-layouts: 22 us -> 21.3 us
    ppermute x4 -> x5, starting transfers between devices: 5.33 us -> 5.64 us  [the longest x3 4.9 us: gather_hid(): lax.ppermute(p, BOTH, down)]
  transfers between devices with their start and end apart: 17 -> 18, of which waited for: 10 -> 10; matrix products, arithmetic and copies ran while one was open for 4% -> 4% of each run, Pallas kernels for 11% -> 11%
where the time goes in v5:
time: 184 us; the launch traced here: 183 us
  waiting for transfers between devices  82.8 us (45%)
  starting transfers between devices  42 us (23%)
  Pallas kernels  28.9 us (16%)
  local copies, waits for them, and re-layouts  25.3 us (14%)
  other arithmetic  2.84 us (2%)
    all_to_all x1, waiting for transfers between devices, local(): lax.all_to_all(next_weights(now, following, got, base), 'slot', 0, 0, til...  44.2 us
    unnamed x64, local copies, waits for them, and re-layouts  21.3 us
    all_to_all x1, waiting for transfers between devices, local(): got = lax.all_to_all(grads, 'slot', 0, 0, tiled=True)  19.6 us
    all_to_all x1, starting transfers between devices, local(): got = lax.all_to_all(grads, 'slot', 0, 0, tiled=True)  13 us
    pallas_call x3, Pallas kernels, slot_grad(): pl.pallas_call(functools.partial(slot_grad_kernel, groups, keep), out_sha...  9.85 us
    pallas_call x1, Pallas kernels, input_gradient(): pl.pallas_call(input_grad_kernel, grid=(rows // tile,), out_shape=jax.Sha...  9 us
    ppermute x3, starting transfers between devices, gather_hid(): above += [lax.ppermute(p, BOTH, down) for p in line[1:]]  7.5 us
    ppermute x3, waiting for transfers between devices, gather_hid(): below += [lax.ppermute(p, BOTH, up) for p in line[1:]]  5.52 us
  transfers between devices with their start and end apart: 18, of which 10 were waited for; matrix products, arithmetic and copies ran while one was open for 4% of the time, Pallas kernels for 11%

profile of v5, /device:TPU:1, one launch (start us, length us, event | category | flops | bytes accessed | tf_op | source)
XLA Modules:
  0.0 182.9 jit_solution(4810585862281139996)
XLA Ops:
  3.3 2.2 %collective-permute-start = (bf16[128,2048]{1,0:T(8,128)(2,1)S(1)}, bf16[128,2048]{1,0:T(8,128)(2,1)S(1)}, u32[]{:S(2)}, u32[]{:S(2)}) collective-permute-start(bf16[128,2048]{1,0:T(8,128)(2,1)S(1)} %mask_turn.1.refs_0_), channel_id=1, source_target_pairs={{0,1},{16,20},{1,2},{17,21},{2,3},{18,22},{3,0},{19,23},{4,5},{20,... | collective-permute-start | bytes 1572872 | tf_op jit(solution)/shard_map/ppermute | solution.py:318
  5.5 1.5 collective-permute-start.1
  7.0 2.5 %collective-permute-start.7 = (bf16[128,2048]{1,0:T(8,128)(2,1)S(1)}, bf16[128,2048]{1,0:T(8,128)(2,1)S(1)}, u32[]{:S(2)}, u32[]{:S(2)}) collective-permute-start(bf16[128,2048]{1,0:T(8,128)(2,1)S(1)} %mask_turn.1.refs_0_), channel_id=1, source_target_pairs={{0,12},{16,19},{1,13},{17,16},{2,14},{18,17},{3,15},{19,18},{4,0},... | collective-permute-start | bytes 1572872 | tf_op jit(solution)/shard_map/ppermute | solution.py:321
  9.5 4.3 %collective-permute-done.refs_1_ = bf16[128,2048]{1,0:T(8,128)(2,1)S(1)} collective-permute-done((bf16[128,2048]{1,0:T(8,128)(2,1)S(1)}, bf16[128,2048]{1,0:T(8,128)(2,1)S(1)}, u32[]{:S(2)}, u32[]{:S(2)}) %collective-permute-start) | collective-permute-done | bytes 524320 | tf_op jit(solution)/shard_map/ppermute | solution.py:318
  15.1 4.8 %collective-permute-start.9 = (bf16[128,2048]{1,0:T(8,128)(2,1)S(1)}, bf16[128,2048]{1,0:T(8,128)(2,1)S(1)}, u32[]{:S(2)}, u32[]{:S(2)}) collective-permute-start(bf16[128,2048]{1,0:T(8,128)(2,1)S(1)} %collective-permute-done.1.refs_2_), channel_id=1, source_target_pairs={{0,12},{16,19},{1,13},{17,16},{2,14},{18,17},{3,15},{19,18},{4,0},... | collective-permute-start | bytes 1572872 | tf_op jit(solution)/shard_map/ppermute | solution.py:325
  22.0 3.2 %collective-permute-done.2.refs_3_ = bf16[128,2048]{1,0:T(8,128)(2,1)S(1)} collective-permute-done((bf16[128,2048]{1,0:T(8,128)(2,1)S(1)}, bf16[128,2048]{1,0:T(8,128)(2,1)S(1)}, u32[]{:S(2)}, u32[]{:S(2)}) %collective-permute-start.2) | collective-permute-done | bytes 524320 | tf_op jit(solution)/shard_map/ppermute | solution.py:322
  25.2 2.0 %collective-permute-start.10 = (bf16[128,2048]{1,0:T(8,128)(2,1)S(1)}, bf16[128,2048]{1,0:T(8,128)(2,1)S(1)}, u32[]{:S(2)}, u32[]{:S(2)}) collective-permute-start(bf16[128,2048]{1,0:T(8,128)(2,1)S(1)} %collective-permute-done.2.refs_3_), channel_id=1, source_target_pairs={{0,12},{16,19},{1,13},{17,16},{2,14},{18,17},{3,15},{19,18},{4,0},... | collective-permute-start | bytes 1572872 | tf_op jit(solution)/shard_map/ppermute | solution.py:325
  27.4 2.2 %collective-permute-start.6 = (bf16[128,2048]{1,0:T(8,128)(2,1)S(1)}, bf16[128,2048]{1,0:T(8,128)(2,1)S(1)}, u32[]{:S(2)}, u32[]{:S(2)}) collective-permute-start(bf16[128,2048]{1,0:T(8,128)(2,1)S(1)} %collective-permute-done.2.refs_3_), channel_id=1, source_target_pairs={{0,4},{16,17},{1,5},{17,18},{2,6},{18,19},{3,7},{19,16},{4,8},{20,... | collective-permute-start | bytes 1572872 | tf_op jit(solution)/shard_map/ppermute | solution.py:324
  29.6 2.9 %collective-permute-done.8.refs_5_.refs_9_ = bf16[128,2048]{1,0:T(8,128)(2,1)S(1)} collective-permute-done((bf16[128,2048]{1,0:T(8,128)(2,1)S(1)}, bf16[128,2048]{1,0:T(8,128)(2,1)S(1)}, u32[]{:S(2)}, u32[]{:S(2)}) %collective-permute-start.8) | collective-permute-done | bytes 524320 | tf_op jit(solution)/shard_map/ppermute | solution.py:325
  33.2 1.4 collective-permute-done.4.refs_1_.refs_5_
  34.6 1.4 collective-permute-start.14
  36.0 2.1 %collective-permute-done.10.refs_7_.refs_11_ = bf16[128,2048]{1,0:T(8,128)(2,1)S(1)} collective-permute-done((bf16[128,2048]{1,0:T(8,128)(2,1)S(1)}, bf16[128,2048]{1,0:T(8,128)(2,1)S(1)}, u32[]{:S(2)}, u32[]{:S(2)}) %collective-permute-start.10) | collective-permute-done | bytes 524320 | tf_op jit(solution)/shard_map/ppermute | solution.py:325
  38.1 3.4 %collective-permute-start.15 = (bf16[128,2048]{1,0:T(8,128)(2,1)S(1)}, bf16[128,2048]{1,0:T(8,128)(2,1)S(1)}, u32[]{:S(2)}, u32[]{:S(2)}) collective-permute-start(bf16[128,2048]{1,0:T(8,128)(2,1)S(1)} %collective-permute-done.10.refs_7_.refs_11_), channel_id=1, source_target_pairs={{0,12},{16,19},{1,13},{17,16},{2,14},{18,17},{3,15},{19,18},{4,0},... | collective-permute-start | bytes 1572872 | tf_op jit(solution)/shard_map/ppermute | solution.py:328
  41.7 4.2 %collective-permute-done.6.refs_3_.refs_7_ = bf16[128,2048]{1,0:T(8,128)(2,1)S(1)} collective-permute-done((bf16[128,2048]{1,0:T(8,128)(2,1)S(1)}, bf16[128,2048]{1,0:T(8,128)(2,1)S(1)}, u32[]{:S(2)}, u32[]{:S(2)}) %collective-permute-start.6) | collective-permute-done | bytes 524320 | tf_op jit(solution)/shard_map/ppermute | solution.py:324
  45.9 2.7 %slot_grad.3.refs_8_ = bf16[16,128,512]{2,1,0:T(8,128)(2,1)} custom-call(s32[4]{0:T(128)S(1)} %pad_add_fusion.place_ref, bf16[2048,512]{1,0:T(8,128)(2,1)S(1)} %copy-done, bf16[128,2048]{1,0:T(8,128)(2,1)S(1)} %mask_turn.1.refs_0_, bf16[128,2048]{1,0:T(8,128)(2,1)S(1)} %collective-permute-done.refs_1_, bf16[128,2048]{1,0:T(8,128)(2,1)S(1)} %collective-permute-done.1.refs_2_, ...), custom_call_target="tpu_custom_call" | custom-call | flops 1073741824 | bytes 6291456 | tf_op jit(solution)/shard_map/slot_grad/pallas_call | solution.py:141
  49.5 4.2 %slot_grad.4.refs_5_ = bf16[16,128,512]{2,1,0:T(8,128)(2,1)} custom-call(s32[4]{0:T(128)S(1)} %pad_add_fusion.place_ref, bf16[2048,512]{1,0:T(8,128)(2,1)S(1)} %copy-done, bf16[128,2048]{1,0:T(8,128)(2,1)S(1)} %collective-permute-done.3.refs_0_.refs_4_, ...), custom_call_target="tpu_custom_call", output_to_operand_aliasing={{}: (10, {})} | custom-call | flops 2147483648 | bytes 6291456 | tf_op jit(solution)/shard_map/slot_grad/pallas_call | solution.py:141
  54.3 2.9 %slot_grad.5 = (bf16[16,128,512]{2,1,0:T(8,128)(2,1)}, bf16[4,128,2048]{2,1,0:T(8,128)(2,1)S(1)}) custom-call(s32[4]{0:T(128)S(1)} %pad_add_fusion.place_ref, bf16[2048,512]{1,0:T(8,128)(2,1)S(1)} %copy-done, bf16[128,2048]{1,0:T(8,128)(2,1)S(1)} %collective-permute-done.11.refs_0_, ...), custom_call_target="tpu_custom_call", output_to_operand_aliasing={{0}: (7, {})} | custom-call | flops 1342177280 | bytes 6291456 | tf_op jit(solution)/shard_map/slot_grad/pallas_call | solution.py:141
  57.2 1.3 copy-done.30
  58.5 13.0 %all-to-all-start = ((bf16[16,128,512]{2,1,0:T(8,128)(2,1)}), bf16[16,128,512]{2,1,0:T(8,128)(2,1)S(1)}, u32[]{:S(2)}, u32[]{:S(2)}) async-start(bf16[16,128,512]{2,1,0:T(8,128)(2,1)} %get-tuple-element.13), calls=%async_computation | async-start | bytes 4194304 | tf_op jit(solution)/shard_map/all_to_all | solution.py:346
  82.0 1.6 copy-done.29
  83.5 1.6 copy-done.31
  85.1 9.0 %input_grad.1 = bf16[2048,512]{1,0:T(8,128)(2,1)} custom-call(s32[4]{0:T(128)S(1)} %pad_add_fusion.place_ref, bf16[512,2048]{1,0:T(8,128)(2,1)S(1)} %bitcast.13, bf16[128,2048]{1,0:T(8,128)(2,1)S(1)} %mask_turn.1.refs_0_, bf16[128,2048]{1,0:T(8,128)(2,1)S(1)} %copy-done.8, bf16[128,2048]{1,0:T(8,128)(2,1)S(1)} %copy-done.10, ...), custom_call_target="tpu_custom_call" | custom-call | flops 4294967296 | bytes 12582912 | tf_op jit(solution)/shard_map/input_grad/pallas_call | solution.py:267
  94.2 2.6 %copy.15 = f32[4,512,128]{1,2,0:T(8,128)} copy(f32[4,512,128]{2,1,0:T(8,128)} %mas_ref.1) | data formatting | bytes 2097152 | tf_op jit(solution)/shard_map/optimization_barrier | solution.py:348
  96.8 1.3 copy.14
  98.1 2.8 %subtract_bitcast_fusion.base_ref = f32[4,128,512]{2,1,0:T(8,128)} fusion(f32[4,512,128]{1,2,0:T(8,128)} %copy.15, f32[4,512,128]{1,2,0:T(8,128)} %copy.14), kind=kLoop, calls=%fused_computation | loop fusion | flops 524288 | bytes 3145728 | tf_op jit(solution)/shard_map/transpose | solution.py:349
  100.8 19.6 %all-to-all-done.got_ref = bf16[16,128,512]{2,1,0:T(8,128)(2,1)S(1)} async-done(((bf16[16,128,512]{2,1,0:T(8,128)(2,1)}), bf16[16,128,512]{2,1,0:T(8,128)(2,1)S(1)}, u32[]{:S(2)}, u32[]{:S(2)}) %all-to-all-start) | async-done | bytes 2097184 | tf_op jit(solution)/shard_map/all_to_all | solution.py:346
  121.7 2.4 %next_weights.1 = bf16[16,128,512]{2,1,0:T(8,128)(2,1)S(1)} custom-call(s32[16]{0:T(128)S(1)} %bitcast.10, s32[16]{0:T(128)S(1)} %bitcast.12, bf16[16,128,512]{2,1,0:T(8,128)(2,1)S(1)} %all-to-all-done.got_ref, f32[4,128,512]{2,1,0:T(8,128)S(1)} %copy-done.4), custom_call_target="tpu_custom_call" | custom-call | bytes 6291456 | tf_op jit(solution)/shard_map/next_weights/pallas_call | solution.py:185
  124.1 1.3 copy-done.1
  125.5 5.0 %all-to-all-start.1 = ((bf16[16,128,512]{2,1,0:T(8,128)(2,1)}), bf16[16,128,512]{2,1,0:T(8,128)(2,1)}, u32[]{:S(2)}, u32[]{:S(2)}) async-start(bf16[16,128,512]{2,1,0:T(8,128)(2,1)} %copy-done.1), calls=%async_computation.1 | async-start | bytes 4194304 | tf_op jit(solution)/shard_map/all_to_all | solution.py:350
  131.7 3.6 %momentum_step.1 = (f32[4,512,128]{2,1,0:T(8,128)}, f32[4,512,128]{2,1,0:T(8,128)}) custom-call(s32[16]{0:T(128)S(1)} %bitcast.11, f32[4,512,128]{2,1,0:T(8,128)S(1)} %copy-done.2, f32[4,512,128]{2,1,0:T(8,128)S(1)} %copy-done.3, bf16[16,128,512]{2,1,0:T(8,128)(2,1)S(1)} %all-to-all-done.got_ref), custom_call_target="tpu_custom_call" | custom-call | bytes 8388608 | tf_op jit(solution)/shard_map/momentum_step/pallas_call | solution.py:209
  135.3 44.2 %all-to-all-done.1.got_ref = bf16[16,128,512]{2,1,0:T(8,128)(2,1)} async-done(((bf16[16,128,512]{2,1,0:T(8,128)(2,1)}), bf16[16,128,512]{2,1,0:T(8,128)(2,1)}, u32[]{:S(2)}, u32[]{:S(2)}) %all-to-all-start.1) | async-done | bytes 2097184 | tf_op jit(solution)/shard_map/all_to_all | solution.py:350
  179.5 3.3 %placed_turn.1 = bf16[512,2048]{1,0:T(8,128)(2,1)} custom-call(bf16[16,128,512]{2,1,0:T(8,128)(2,1)} %all-to-all-done.1.got_ref), custom_call_target="tpu_custom_call" | custom-call | bytes 4194304 | tf_op jit(solution)/shard_map/placed_turn/pallas_call | solution.py:299
  (82 shorter events, 21.3 us)
Async XLA Ops:
  0.6 45.2 %copy-start = (bf16[2048,512]{1,0:T(8,128)(2,1)S(1)}, bf16[2048,512]{1,0:T(8,128)(2,1)}, u32[]{:S(2)}) copy-start(bf16[2048,512]{1,0:T(8,128)(2,1)} %hidden_ref.5) | copy-start | bytes 6291460
  3.3 10.5 %collective-permute-start = (bf16[128,2048]{1,0:T(8,128)(2,1)S(1)}, bf16[128,2048]{1,0:T(8,128)(2,1)S(1)}, u32[]{:S(2)}, u32[]{:S(2)}) collective-permute-start(bf16[128,2048]{1,0:T(8,128)(2,1)S(1)} %mask_turn.1.refs_0_), channel_id=1, source_target_pairs={{0,1},{16,20},{1,2},{17,21},{2,3},{18,22},{3,0},{19,23},{4,5},{20,... | collective-permute-start | bytes 1572872 | tf_op jit(solution)/shard_map/ppermute | solution.py:318
  5.5 9.5 %collective-permute-start.1 = (bf16[128,2048]{1,0:T(8,128)(2,1)S(1)}, bf16[128,2048]{1,0:T(8,128)(2,1)S(1)}, u32[]{:S(2)}, u32[]{:S(2)}) collective-permute-start(bf16[128,2048]{1,0:T(8,128)(2,1)S(1)} %mask_turn.1.refs_0_), channel_id=1, source_target_pairs={{0,3},{16,28},{1,0},{17,29},{2,1},{18,30},{3,2},{19,31},{4,7},{20,... | collective-permute-start | bytes 1572872 | tf_op jit(solution)/shard_map/ppermute | solution.py:319
  7.0 13.8 %collective-permute-start.7 = (bf16[128,2048]{1,0:T(8,128)(2,1)S(1)}, bf16[128,2048]{1,0:T(8,128)(2,1)S(1)}, u32[]{:S(2)}, u32[]{:S(2)}) collective-permute-start(bf16[128,2048]{1,0:T(8,128)(2,1)S(1)} %mask_turn.1.refs_0_), channel_id=1, source_target_pairs={{0,12},{16,19},{1,13},{17,16},{2,14},{18,17},{3,15},{19,18},{4,0},... | collective-permute-start | bytes 1572872 | tf_op jit(solution)/shard_map/ppermute | solution.py:321
  13.8 32.0 %copy-start.7 = (bf16[128,2048]{1,0:T(8,128)(2,1)}, bf16[128,2048]{1,0:T(8,128)(2,1)S(1)}, u32[]{:S(2)}) copy-start(bf16[128,2048]{1,0:T(8,128)(2,1)S(1)} %collective-permute-done.refs_1_) | copy-start | bytes 1572868
  13.8 11.4 %collective-permute-start.2 = (bf16[128,2048]{1,0:T(8,128)(2,1)S(1)}, bf16[128,2048]{1,0:T(8,128)(2,1)S(1)}, u32[]{:S(2)}, u32[]{:S(2)}) collective-permute-start(bf16[128,2048]{1,0:T(8,128)(2,1)S(1)} %collective-permute-done.refs_1_), channel_id=1, source_target_pairs={{0,1},{16,20},{1,2},{17,21},{2,3},{18,22},{3,0},{19,23},{4,5},{20,... | collective-permute-start | bytes 1572872 | tf_op jit(solution)/shard_map/ppermute | solution.py:322
  13.8 13.4 %collective-permute-start.3 = (bf16[128,2048]{1,0:T(8,128)(2,1)S(1)}, bf16[128,2048]{1,0:T(8,128)(2,1)S(1)}, u32[]{:S(2)}, u32[]{:S(2)}) collective-permute-start(bf16[128,2048]{1,0:T(8,128)(2,1)S(1)} %mask_turn.1.refs_0_), channel_id=1, source_target_pairs={{0,4},{16,17},{1,5},{17,18},{2,6},{18,19},{3,7},{19,16},{4,8},{20,... | collective-permute-start | bytes 1572872 | tf_op jit(solution)/shard_map/ppermute | solution.py:320
  15.1 33.6 %copy-start.9 = (bf16[128,2048]{1,0:T(8,128)(2,1)}, bf16[128,2048]{1,0:T(8,128)(2,1)S(1)}, u32[]{:S(2)}) copy-start(bf16[128,2048]{1,0:T(8,128)(2,1)S(1)} %collective-permute-done.1.refs_2_) | copy-start | bytes 1572868
  15.1 12.4 %collective-permute-start.9 = (bf16[128,2048]{1,0:T(8,128)(2,1)S(1)}, bf16[128,2048]{1,0:T(8,128)(2,1)S(1)}, u32[]{:S(2)}, u32[]{:S(2)}) collective-permute-start(bf16[128,2048]{1,0:T(8,128)(2,1)S(1)} %collective-permute-done.1.refs_2_), channel_id=1, source_target_pairs={{0,12},{16,19},{1,13},{17,16},{2,14},{18,17},{3,15},{19,18},{4,0},... | collective-permute-start | bytes 1572872 | tf_op jit(solution)/shard_map/ppermute | solution.py:325
  19.8 12.7 %collective-permute-start.8 = (bf16[128,2048]{1,0:T(8,128)(2,1)S(1)}, bf16[128,2048]{1,0:T(8,128)(2,1)S(1)}, u32[]{:S(2)}, u32[]{:S(2)}) collective-permute-start(bf16[128,2048]{1,0:T(8,128)(2,1)S(1)} %collective-permute-done.refs_1_), channel_id=1, source_target_pairs={{0,12},{16,19},{1,13},{17,16},{2,14},{18,17},{3,15},{19,18},{4,0},... | collective-permute-start | bytes 1572872 | tf_op jit(solution)/shard_map/ppermute | solution.py:325
  20.8 27.8 %copy-start.14 = (bf16[128,2048]{1,0:T(8,128)(2,1)}, bf16[128,2048]{1,0:T(8,128)(2,1)S(1)}, u32[]{:S(2)}) copy-start(bf16[128,2048]{1,0:T(8,128)(2,1)S(1)} %collective-permute-done.7.refs_4_.refs_8_) | copy-start | bytes 1572868
  20.9 13.7 %collective-permute-start.4 = (bf16[128,2048]{1,0:T(8,128)(2,1)S(1)}, bf16[128,2048]{1,0:T(8,128)(2,1)S(1)}, u32[]{:S(2)}, u32[]{:S(2)}) collective-permute-start(bf16[128,2048]{1,0:T(8,128)(2,1)S(1)} %collective-permute-done.refs_1_), channel_id=1, source_target_pairs={{0,4},{16,17},{1,5},{17,18},{2,6},{18,19},{3,7},{19,16},{4,8},{20,... | collective-permute-start | bytes 1572872 | tf_op jit(solution)/shard_map/ppermute | solution.py:324
  25.2 12.9 %collective-permute-start.10 = (bf16[128,2048]{1,0:T(8,128)(2,1)S(1)}, bf16[128,2048]{1,0:T(8,128)(2,1)S(1)}, u32[]{:S(2)}, u32[]{:S(2)}) collective-permute-start(bf16[128,2048]{1,0:T(8,128)(2,1)S(1)} %collective-permute-done.2.refs_3_), channel_id=1, source_target_pairs={{0,12},{16,19},{1,13},{17,16},{2,14},{18,17},{3,15},{19,18},{4,0},... | collective-permute-start | bytes 1572872 | tf_op jit(solution)/shard_map/ppermute | solution.py:325
  27.2 21.4 %copy-start.16 = (bf16[128,2048]{1,0:T(8,128)(2,1)}, bf16[128,2048]{1,0:T(8,128)(2,1)S(1)}, u32[]{:S(2)}) copy-start(bf16[128,2048]{1,0:T(8,128)(2,1)S(1)} %collective-permute-done.3.refs_0_.refs_4_) | copy-start | bytes 1572868
  27.3 14.3 %collective-permute-start.5 = (bf16[128,2048]{1,0:T(8,128)(2,1)S(1)}, bf16[128,2048]{1,0:T(8,128)(2,1)S(1)}, u32[]{:S(2)}, u32[]{:S(2)}) collective-permute-start(bf16[128,2048]{1,0:T(8,128)(2,1)S(1)} %collective-permute-done.1.refs_2_), channel_id=1, source_target_pairs={{0,4},{16,17},{1,5},{17,18},{2,6},{18,19},{3,7},{19,16},{4,8},{20,... | collective-permute-start | bytes 1572872 | tf_op jit(solution)/shard_map/ppermute | solution.py:324
  27.4 21.2 %copy-start.18 = (bf16[128,2048]{1,0:T(8,128)(2,1)}, bf16[128,2048]{1,0:T(8,128)(2,1)S(1)}, u32[]{:S(2)}) copy-start(bf16[128,2048]{1,0:T(8,128)(2,1)S(1)} %collective-permute-done.9.refs_6_.refs_10_) | copy-start | bytes 1572868
  27.4 18.4 %collective-permute-start.6 = (bf16[128,2048]{1,0:T(8,128)(2,1)S(1)}, bf16[128,2048]{1,0:T(8,128)(2,1)S(1)}, u32[]{:S(2)}, u32[]{:S(2)}) collective-permute-start(bf16[128,2048]{1,0:T(8,128)(2,1)S(1)} %collective-permute-done.2.refs_3_), channel_id=1, source_target_pairs={{0,4},{16,17},{1,5},{17,18},{2,6},{18,19},{3,7},{19,16},{4,8},{20,... | collective-permute-start | bytes 1572872 | tf_op jit(solution)/shard_map/ppermute | solution.py:324
  32.5 21.2 %collective-permute-start.11 = (bf16[128,2048]{1,0:T(8,128)(2,1)S(1)}, bf16[128,2048]{1,0:T(8,128)(2,1)S(1)}, u32[]{:S(2)}, u32[]{:S(2)}) collective-permute-start(bf16[128,2048]{1,0:T(8,128)(2,1)S(1)} %collective-permute-done.3.refs_0_.refs_4_), channel_id=1, source_target_pairs={{0,4},{16,17},{1,5},{17,18},{2,6},{18,19},{3,7},{19,16},{4,8},{20,... | collective-permute-start | bytes 1572872 | tf_op jit(solution)/shard_map/ppermute | solution.py:327
  34.6 14.1 %copy-start.5 = (bf16[128,2048]{1,0:T(8,128)(2,1)}, bf16[128,2048]{1,0:T(8,128)(2,1)S(1)}, u32[]{:S(2)}) copy-start(bf16[128,2048]{1,0:T(8,128)(2,1)S(1)} %collective-permute-done.4.refs_1_.refs_5_) | copy-start | bytes 1572868
  34.6 19.7 %collective-permute-start.14 = (bf16[128,2048]{1,0:T(8,128)(2,1)S(1)}, bf16[128,2048]{1,0:T(8,128)(2,1)S(1)}, u32[]{:S(2)}, u32[]{:S(2)}) collective-permute-start(bf16[128,2048]{1,0:T(8,128)(2,1)S(1)} %collective-permute-done.9.refs_6_.refs_10_), channel_id=1, source_target_pairs={{0,12},{16,19},{1,13},{17,16},{2,14},{18,17},{3,15},{19,18},{4,0},... | collective-permute-start | bytes 1572872 | tf_op jit(solution)/shard_map/ppermute | solution.py:328
  38.1 10.5 %copy-start.20 = (bf16[128,2048]{1,0:T(8,128)(2,1)}, bf16[128,2048]{1,0:T(8,128)(2,1)S(1)}, u32[]{:S(2)}) copy-start(bf16[128,2048]{1,0:T(8,128)(2,1)S(1)} %collective-permute-done.10.refs_7_.refs_11_) | copy-start | bytes 1572868
  38.1 16.2 %collective-permute-start.15 = (bf16[128,2048]{1,0:T(8,128)(2,1)S(1)}, bf16[128,2048]{1,0:T(8,128)(2,1)S(1)}, u32[]{:S(2)}, u32[]{:S(2)}) collective-permute-start(bf16[128,2048]{1,0:T(8,128)(2,1)S(1)} %collective-permute-done.10.refs_7_.refs_11_), channel_id=1, source_target_pairs={{0,12},{16,19},{1,13},{17,16},{2,14},{18,17},{3,15},{19,18},{4,0},... | collective-permute-start | bytes 1572872 | tf_op jit(solution)/shard_map/ppermute | solution.py:328
  41.6 7.1 %copy-start.22 = (bf16[128,2048]{1,0:T(8,128)(2,1)}, bf16[128,2048]{1,0:T(8,128)(2,1)S(1)}, u32[]{:S(2)}) copy-start(bf16[128,2048]{1,0:T(8,128)(2,1)S(1)} %collective-permute-done.5.refs_2_.refs_6_) | copy-start | bytes 1572868
  41.6 12.1 %collective-permute-start.13 = (bf16[64,2048]{1,0:T(8,128)(2,1)S(1)}, bf16[64,2048]{1,0:T(8,128)(2,1)S(1)}, u32[]{:S(2)}, u32[]{:S(2)}) collective-permute-start(bf16[64,2048]{1,0:T(8,128)(2,1)S(1)} %slice.9), channel_id=1, source_target_pairs={{0,12},{16,19},{1,13},{17,16},{2,14},{18,17},{3,15},{19,18},{4,0},... | collective-permute-start | bytes 786440 | tf_op jit(solution)/shard_map/ppermute | solution.py:328
  45.9 2.8 %copy-start.24 = (bf16[128,2048]{1,0:T(8,128)(2,1)}, bf16[128,2048]{1,0:T(8,128)(2,1)S(1)}, u32[]{:S(2)}) copy-start(bf16[128,2048]{1,0:T(8,128)(2,1)S(1)} %collective-permute-done.6.refs_3_.refs_7_) | copy-start | bytes 1572868
  45.9 8.4 %collective-permute-start.12 = (bf16[64,2048]{1,0:T(8,128)(2,1)S(1)}, bf16[64,2048]{1,0:T(8,128)(2,1)S(1)}, u32[]{:S(2)}, u32[]{:S(2)}) collective-permute-start(bf16[64,2048]{1,0:T(8,128)(2,1)S(1)} %slice.8), channel_id=1, source_target_pairs={{0,4},{16,17},{1,5},{17,18},{2,6},{18,19},{3,7},{19,16},{4,8},{20,... | collective-permute-start | bytes 786440 | tf_op jit(solution)/shard_map/ppermute | solution.py:327
  58.5 62.0 %all-to-all-start = ((bf16[16,128,512]{2,1,0:T(8,128)(2,1)}), bf16[16,128,512]{2,1,0:T(8,128)(2,1)S(1)}, u32[]{:S(2)}, u32[]{:S(2)}) async-start(bf16[16,128,512]{2,1,0:T(8,128)(2,1)} %get-tuple-element.13), calls=%async_computation | async-start | bytes 4194304 | tf_op jit(solution)/shard_map/all_to_all | solution.py:346
  82.0 1.6 copy-start.29
  94.1 2.6 %copy-start.2 = (f32[4,512,128]{2,1,0:T(8,128)S(1)}, f32[4,512,128]{2,1,0:T(8,128)}, u32[]{:S(2)}) copy-start(f32[4,512,128]{2,1,0:T(8,128)} %mom_ref.1) | copy-start | bytes 3145732
  98.1 22.4 %copy-start.26 = (s32[16,1]{0,1:T(1,128)S(1)}, s32[16,1]{0,1:T(1,128)}, u32[]{:S(2)}) copy-start(s32[16,1]{0,1:T(1,128)} %param.11) | copy-start | bytes 196
  98.1 22.4 %copy-start.28 = (s32[16,1]{0,1:T(1,128)S(1)}, s32[16,1]{0,1:T(1,128)}, u32[]{:S(2)}) copy-start(s32[16,1]{0,1:T(1,128)} %param.12) | copy-start | bytes 196
  125.5 54.0 %all-to-all-start.1 = ((bf16[16,128,512]{2,1,0:T(8,128)(2,1)}), bf16[16,128,512]{2,1,0:T(8,128)(2,1)}, u32[]{:S(2)}, u32[]{:S(2)}) async-start(bf16[16,128,512]{2,1,0:T(8,128)(2,1)} %copy-done.1), calls=%async_computation.1 | async-start | bytes 4194304 | tf_op jit(solution)/shard_map/all_to_all | solution.py:350
  (18 other events, 19.7 us)

commit v6 on v5

--- a/solution.py
+++ b/solution.py
@@ -48,17 +48,28 @@
     return pairs
 
 
-def mask_kernel(place_ref, counts_ref, cot_ref, out_ref):
-    live = lax.broadcasted_iota(jnp.int32, cot_ref.shape, 0) < counts_ref[place_ref[3]]
-    out_ref[...] = jnp.where(live, cot_ref[...], jnp.zeros_like(cot_ref)).T
+def mask_kernel(place_ref, counts_ref, cot_ref, out_ref, held, sems):
+    parts, step, _ = held.shape
+    loads = fetch([cot_ref.at[pl.ds(n * step, step)] for n in range(parts)], held, sems)
+    for n in range(parts):
+        loads[n].wait()
+        rows = held[n]
+        live = lax.broadcasted_iota(jnp.int32, rows.shape, 0) + n * step < counts_ref[place_ref[3]]
+        out_ref[:, n * step : (n + 1) * step] = jnp.where(live, rows, jnp.zeros_like(rows)).T
 
 
 def masked_block(place, counts, cotangent):
+    rows, columns = cotangent.shape
+    parts = 4
     return pl.pallas_call(
         mask_kernel,
-        out_shape=jax.ShapeDtypeStruct(cotangent.shape[::-1], jnp.bfloat16),
-        in_specs=[SM, SM, VM],
+        out_shape=jax.ShapeDtypeStruct((columns, rows), jnp.bfloat16),
+        in_specs=[SM, SM, HBM],
         out_specs=VM,
+        scratch_shapes=[
+            pltpu.VMEM((parts, rows // parts, columns), jnp.bfloat16),
+            pltpu.SemaphoreType.DMA((parts,)),
+        ],
         compiler_params=params(16),
         cost_estimate=cost(0, 1 * MIB),
         name="mask_turn",

time: 184 us -> 185 us (level)
  no operation moved by 1% of the time
where the time goes in v6:
time: 185 us; the launch traced here: 184 us
  waiting for transfers between devices  82.8 us (45%)
  starting transfers between devices  42 us (23%)
  Pallas kernels  29.8 us (16%)
  local copies, waits for them, and re-layouts  25.3 us (14%)
  other arithmetic  2.84 us (2%)
    all_to_all x1, waiting for transfers between devices, local(): lax.all_to_all(next_weights(now, following, got, base), 'slot', 0, 0, til...  44.2 us
    unnamed x64, local copies, waits for them, and re-layouts  21.3 us
    all_to_all x1, waiting for transfers between devices, local(): got = lax.all_to_all(grads, 'slot', 0, 0, tiled=True)  19.6 us
    all_to_all x1, starting transfers between devices, local(): got = lax.all_to_all(grads, 'slot', 0, 0, tiled=True)  13 us
    pallas_call x3, Pallas kernels, slot_grad(): pl.pallas_call(functools.partial(slot_grad_kernel, groups, keep), out_sha...  9.85 us
    pallas_call x1, Pallas kernels, input_gradient(): pl.pallas_call(input_grad_kernel, grid=(rows // tile,), out_shape=jax.Sha...  9 us
    ppermute x3, starting transfers between devices, gather_hid(): above += [lax.ppermute(p, BOTH, down) for p in line[1:]]  7.5 us
    ppermute x3, waiting for transfers between devices, gather_hid(): below += [lax.ppermute(p, BOTH, up) for p in line[1:]]  5.52 us
  transfers between devices with their start and end apart: 18, of which 10 were waited for; matrix products, arithmetic and copies ran while one was open for 4% of the time, Pallas kernels for 11%

profile of v6, /device:TPU:1, one launch (start us, length us, event | category | flops | bytes accessed | tf_op | source)
XLA Modules:
  0.0 183.8 jit_solution(9477919523989466478)
XLA Ops:
  2.6 1.6 mask_turn.1.refs_0_
  4.2 2.2 %collective-permute-start = (bf16[128,2048]{1,0:T(8,128)(2,1)S(1)}, bf16[128,2048]{1,0:T(8,128)(2,1)S(1)}, u32[]{:S(2)}, u32[]{:S(2)}) collective-permute-start(bf16[128,2048]{1,0:T(8,128)(2,1)S(1)} %mask_turn.1.refs_0_), channel_id=1, source_target_pairs={{0,1},{16,20},{1,2},{17,21},{2,3},{18,22},{3,0},{19,23},{4,5},{20,... | collective-permute-start | bytes 1572872 | tf_op jit(solution)/shard_map/ppermute | solution.py:329
  6.4 1.5 collective-permute-start.1
  7.9 2.5 %collective-permute-start.7 = (bf16[128,2048]{1,0:T(8,128)(2,1)S(1)}, bf16[128,2048]{1,0:T(8,128)(2,1)S(1)}, u32[]{:S(2)}, u32[]{:S(2)}) collective-permute-start(bf16[128,2048]{1,0:T(8,128)(2,1)S(1)} %mask_turn.1.refs_0_), channel_id=1, source_target_pairs={{0,12},{16,19},{1,13},{17,16},{2,14},{18,17},{3,15},{19,18},{4,0},... | collective-permute-start | bytes 1572872 | tf_op jit(solution)/shard_map/ppermute | solution.py:332
  10.4 4.3 %collective-permute-done.refs_1_ = bf16[128,2048]{1,0:T(8,128)(2,1)S(1)} collective-permute-done((bf16[128,2048]{1,0:T(8,128)(2,1)S(1)}, bf16[128,2048]{1,0:T(8,128)(2,1)S(1)}, u32[]{:S(2)}, u32[]{:S(2)}) %collective-permute-start) | collective-permute-done | bytes 524320 | tf_op jit(solution)/shard_map/ppermute | solution.py:329
  16.0 4.8 %collective-permute-start.9 = (bf16[128,2048]{1,0:T(8,128)(2,1)S(1)}, bf16[128,2048]{1,0:T(8,128)(2,1)S(1)}, u32[]{:S(2)}, u32[]{:S(2)}) collective-permute-start(bf16[128,2048]{1,0:T(8,128)(2,1)S(1)} %collective-permute-done.1.refs_2_), channel_id=1, source_target_pairs={{0,12},{16,19},{1,13},{17,16},{2,14},{18,17},{3,15},{19,18},{4,0},... | collective-permute-start | bytes 1572872 | tf_op jit(solution)/shard_map/ppermute | solution.py:336
  22.9 3.2 %collective-permute-done.2.refs_3_ = bf16[128,2048]{1,0:T(8,128)(2,1)S(1)} collective-permute-done((bf16[128,2048]{1,0:T(8,128)(2,1)S(1)}, bf16[128,2048]{1,0:T(8,128)(2,1)S(1)}, u32[]{:S(2)}, u32[]{:S(2)}) %collective-permute-start.2) | collective-permute-done | bytes 524320 | tf_op jit(solution)/shard_map/ppermute | solution.py:333
  26.1 2.0 %collective-permute-start.10 = (bf16[128,2048]{1,0:T(8,128)(2,1)S(1)}, bf16[128,2048]{1,0:T(8,128)(2,1)S(1)}, u32[]{:S(2)}, u32[]{:S(2)}) collective-permute-start(bf16[128,2048]{1,0:T(8,128)(2,1)S(1)} %collective-permute-done.2.refs_3_), channel_id=1, source_target_pairs={{0,12},{16,19},{1,13},{17,16},{2,14},{18,17},{3,15},{19,18},{4,0},... | collective-permute-start | bytes 1572872 | tf_op jit(solution)/shard_map/ppermute | solution.py:336
  28.3 2.2 %collective-permute-start.6 = (bf16[128,2048]{1,0:T(8,128)(2,1)S(1)}, bf16[128,2048]{1,0:T(8,128)(2,1)S(1)}, u32[]{:S(2)}, u32[]{:S(2)}) collective-permute-start(bf16[128,2048]{1,0:T(8,128)(2,1)S(1)} %collective-permute-done.2.refs_3_), channel_id=1, source_target_pairs={{0,4},{16,17},{1,5},{17,18},{2,6},{18,19},{3,7},{19,16},{4,8},{20,... | collective-permute-start | bytes 1572872 | tf_op jit(solution)/shard_map/ppermute | solution.py:335
  30.5 2.9 %collective-permute-done.8.refs_5_.refs_9_ = bf16[128,2048]{1,0:T(8,128)(2,1)S(1)} collective-permute-done((bf16[128,2048]{1,0:T(8,128)(2,1)S(1)}, bf16[128,2048]{1,0:T(8,128)(2,1)S(1)}, u32[]{:S(2)}, u32[]{:S(2)}) %collective-permute-start.8) | collective-permute-done | bytes 524320 | tf_op jit(solution)/shard_map/ppermute | solution.py:336
  34.1 1.4 collective-permute-done.4.refs_1_.refs_5_
  35.5 1.4 collective-permute-start.14
  36.9 2.1 %collective-permute-done.10.refs_7_.refs_11_ = bf16[128,2048]{1,0:T(8,128)(2,1)S(1)} collective-permute-done((bf16[128,2048]{1,0:T(8,128)(2,1)S(1)}, bf16[128,2048]{1,0:T(8,128)(2,1)S(1)}, u32[]{:S(2)}, u32[]{:S(2)}) %collective-permute-start.10) | collective-permute-done | bytes 524320 | tf_op jit(solution)/shard_map/ppermute | solution.py:336
  39.0 3.4 %collective-permute-start.15 = (bf16[128,2048]{1,0:T(8,128)(2,1)S(1)}, bf16[128,2048]{1,0:T(8,128)(2,1)S(1)}, u32[]{:S(2)}, u32[]{:S(2)}) collective-permute-start(bf16[128,2048]{1,0:T(8,128)(2,1)S(1)} %collective-permute-done.10.refs_7_.refs_11_), channel_id=1, source_target_pairs={{0,12},{16,19},{1,13},{17,16},{2,14},{18,17},{3,15},{19,18},{4,0},... | collective-permute-start | bytes 1572872 | tf_op jit(solution)/shard_map/ppermute | solution.py:339
  42.6 4.2 %collective-permute-done.6.refs_3_.refs_7_ = bf16[128,2048]{1,0:T(8,128)(2,1)S(1)} collective-permute-done((bf16[128,2048]{1,0:T(8,128)(2,1)S(1)}, bf16[128,2048]{1,0:T(8,128)(2,1)S(1)}, u32[]{:S(2)}, u32[]{:S(2)}) %collective-permute-start.6) | collective-permute-done | bytes 524320 | tf_op jit(solution)/shard_map/ppermute | solution.py:335
  46.8 2.7 %slot_grad.3.refs_8_ = bf16[16,128,512]{2,1,0:T(8,128)(2,1)} custom-call(s32[4]{0:T(128)S(1)} %pad_add_fusion.place_ref, bf16[2048,512]{1,0:T(8,128)(2,1)S(1)} %copy-done, bf16[128,2048]{1,0:T(8,128)(2,1)S(1)} %mask_turn.1.refs_0_, bf16[128,2048]{1,0:T(8,128)(2,1)S(1)} %collective-permute-done.refs_1_, bf16[128,2048]{1,0:T(8,128)(2,1)S(1)} %collective-permute-done.1.refs_2_, ...), custom_call_target="tpu_custom_call" | custom-call | flops 1073741824 | bytes 6291456 | tf_op jit(solution)/shard_map/slot_grad/pallas_call | solution.py:152
  50.4 4.2 %slot_grad.4.refs_5_ = bf16[16,128,512]{2,1,0:T(8,128)(2,1)} custom-call(s32[4]{0:T(128)S(1)} %pad_add_fusion.place_ref, bf16[2048,512]{1,0:T(8,128)(2,1)S(1)} %copy-done, bf16[128,2048]{1,0:T(8,128)(2,1)S(1)} %collective-permute-done.3.refs_0_.refs_4_, ...), custom_call_target="tpu_custom_call", output_to_operand_aliasing={{}: (10, {})} | custom-call | flops 2147483648 | bytes 6291456 | tf_op jit(solution)/shard_map/slot_grad/pallas_call | solution.py:152
  55.2 2.9 %slot_grad.5 = (bf16[16,128,512]{2,1,0:T(8,128)(2,1)}, bf16[4,128,2048]{2,1,0:T(8,128)(2,1)S(1)}) custom-call(s32[4]{0:T(128)S(1)} %pad_add_fusion.place_ref, bf16[2048,512]{1,0:T(8,128)(2,1)S(1)} %copy-done, bf16[128,2048]{1,0:T(8,128)(2,1)S(1)} %collective-permute-done.11.refs_0_, ...), custom_call_target="tpu_custom_call", output_to_operand_aliasing={{0}: (7, {})} | custom-call | flops 1342177280 | bytes 6291456 | tf_op jit(solution)/shard_map/slot_grad/pallas_call | solution.py:152
  58.1 1.3 copy-done.30
  59.4 13.0 %all-to-all-start = ((bf16[16,128,512]{2,1,0:T(8,128)(2,1)}), bf16[16,128,512]{2,1,0:T(8,128)(2,1)S(1)}, u32[]{:S(2)}, u32[]{:S(2)}) async-start(bf16[16,128,512]{2,1,0:T(8,128)(2,1)} %get-tuple-element.13), calls=%async_computation | async-start | bytes 4194304 | tf_op jit(solution)/shard_map/all_to_all | solution.py:357
  82.8 1.6 copy-done.29
  84.4 1.6 copy-done.31
  86.0 9.0 %input_grad.1 = bf16[2048,512]{1,0:T(8,128)(2,1)} custom-call(s32[4]{0:T(128)S(1)} %pad_add_fusion.place_ref, bf16[512,2048]{1,0:T(8,128)(2,1)S(1)} %bitcast.13, bf16[128,2048]{1,0:T(8,128)(2,1)S(1)} %mask_turn.1.refs_0_, bf16[128,2048]{1,0:T(8,128)(2,1)S(1)} %copy-done.8, bf16[128,2048]{1,0:T(8,128)(2,1)S(1)} %copy-done.10, ...), custom_call_target="tpu_custom_call" | custom-call | flops 4294967296 | bytes 12582912 | tf_op jit(solution)/shard_map/input_grad/pallas_call | solution.py:278
  95.1 2.6 %copy.15 = f32[4,512,128]{1,2,0:T(8,128)} copy(f32[4,512,128]{2,1,0:T(8,128)} %mas_ref.1) | data formatting | bytes 2097152 | tf_op jit(solution)/shard_map/optimization_barrier | solution.py:359
  99.0 2.8 %subtract_bitcast_fusion.base_ref = f32[4,128,512]{2,1,0:T(8,128)} fusion(f32[4,512,128]{1,2,0:T(8,128)} %copy.15, f32[4,512,128]{1,2,0:T(8,128)} %copy.14), kind=kLoop, calls=%fused_computation | loop fusion | flops 524288 | bytes 3145728 | tf_op jit(solution)/shard_map/transpose | solution.py:360
  101.7 19.6 %all-to-all-done.got_ref = bf16[16,128,512]{2,1,0:T(8,128)(2,1)S(1)} async-done(((bf16[16,128,512]{2,1,0:T(8,128)(2,1)}), bf16[16,128,512]{2,1,0:T(8,128)(2,1)S(1)}, u32[]{:S(2)}, u32[]{:S(2)}) %all-to-all-start) | async-done | bytes 2097184 | tf_op jit(solution)/shard_map/all_to_all | solution.py:357
  122.6 2.4 %next_weights.1 = bf16[16,128,512]{2,1,0:T(8,128)(2,1)S(1)} custom-call(s32[16]{0:T(128)S(1)} %bitcast.10, s32[16]{0:T(128)S(1)} %bitcast.12, bf16[16,128,512]{2,1,0:T(8,128)(2,1)S(1)} %all-to-all-done.got_ref, f32[4,128,512]{2,1,0:T(8,128)S(1)} %copy-done.4), custom_call_target="tpu_custom_call" | custom-call | bytes 6291456 | tf_op jit(solution)/shard_map/next_weights/pallas_call | solution.py:196
  125.0 1.3 copy-done.1
  126.4 5.0 %all-to-all-start.1 = ((bf16[16,128,512]{2,1,0:T(8,128)(2,1)}), bf16[16,128,512]{2,1,0:T(8,128)(2,1)}, u32[]{:S(2)}, u32[]{:S(2)}) async-start(bf16[16,128,512]{2,1,0:T(8,128)(2,1)} %copy-done.1), calls=%async_computation.1 | async-start | bytes 4194304 | tf_op jit(solution)/shard_map/all_to_all | solution.py:361
  132.6 3.6 %momentum_step.1 = (f32[4,512,128]{2,1,0:T(8,128)}, f32[4,512,128]{2,1,0:T(8,128)}) custom-call(s32[16]{0:T(128)S(1)} %bitcast.11, f32[4,512,128]{2,1,0:T(8,128)S(1)} %copy-done.2, f32[4,512,128]{2,1,0:T(8,128)S(1)} %copy-done.3, bf16[16,128,512]{2,1,0:T(8,128)(2,1)S(1)} %all-to-all-done.got_ref), custom_call_target="tpu_custom_call" | custom-call | bytes 8388608 | tf_op jit(solution)/shard_map/momentum_step/pallas_call | solution.py:220
  136.2 44.2 %all-to-all-done.1.got_ref = bf16[16,128,512]{2,1,0:T(8,128)(2,1)} async-done(((bf16[16,128,512]{2,1,0:T(8,128)(2,1)}), bf16[16,128,512]{2,1,0:T(8,128)(2,1)}, u32[]{:S(2)}, u32[]{:S(2)}) %all-to-all-start.1) | async-done | bytes 2097184 | tf_op jit(solution)/shard_map/all_to_all | solution.py:361
  180.4 3.3 %placed_turn.1 = bf16[512,2048]{1,0:T(8,128)(2,1)} custom-call(bf16[16,128,512]{2,1,0:T(8,128)(2,1)} %all-to-all-done.1.got_ref), custom_call_target="tpu_custom_call" | custom-call | bytes 4194304 | tf_op jit(solution)/shard_map/placed_turn/pallas_call | solution.py:310
  (82 shorter events, 21.9 us)
Async XLA Ops:
  0.6 46.1 %copy-start = (bf16[2048,512]{1,0:T(8,128)(2,1)S(1)}, bf16[2048,512]{1,0:T(8,128)(2,1)}, u32[]{:S(2)}) copy-start(bf16[2048,512]{1,0:T(8,128)(2,1)} %hidden_ref.5) | copy-start | bytes 6291460
  4.2 10.5 %collective-permute-start = (bf16[128,2048]{1,0:T(8,128)(2,1)S(1)}, bf16[128,2048]{1,0:T(8,128)(2,1)S(1)}, u32[]{:S(2)}, u32[]{:S(2)}) collective-permute-start(bf16[128,2048]{1,0:T(8,128)(2,1)S(1)} %mask_turn.1.refs_0_), channel_id=1, source_target_pairs={{0,1},{16,20},{1,2},{17,21},{2,3},{18,22},{3,0},{19,23},{4,5},{20,... | collective-permute-start | bytes 1572872 | tf_op jit(solution)/shard_map/ppermute | solution.py:329
  6.4 9.5 %collective-permute-start.1 = (bf16[128,2048]{1,0:T(8,128)(2,1)S(1)}, bf16[128,2048]{1,0:T(8,128)(2,1)S(1)}, u32[]{:S(2)}, u32[]{:S(2)}) collective-permute-start(bf16[128,2048]{1,0:T(8,128)(2,1)S(1)} %mask_turn.1.refs_0_), channel_id=1, source_target_pairs={{0,3},{16,28},{1,0},{17,29},{2,1},{18,30},{3,2},{19,31},{4,7},{20,... | collective-permute-start | bytes 1572872 | tf_op jit(solution)/shard_map/ppermute | solution.py:330
  7.9 13.8 %collective-permute-start.7 = (bf16[128,2048]{1,0:T(8,128)(2,1)S(1)}, bf16[128,2048]{1,0:T(8,128)(2,1)S(1)}, u32[]{:S(2)}, u32[]{:S(2)}) collective-permute-start(bf16[128,2048]{1,0:T(8,128)(2,1)S(1)} %mask_turn.1.refs_0_), channel_id=1, source_target_pairs={{0,12},{16,19},{1,13},{17,16},{2,14},{18,17},{3,15},{19,18},{4,0},... | collective-permute-start | bytes 1572872 | tf_op jit(solution)/shard_map/ppermute | solution.py:332
  14.7 32.0 %copy-start.7 = (bf16[128,2048]{1,0:T(8,128)(2,1)}, bf16[128,2048]{1,0:T(8,128)(2,1)S(1)}, u32[]{:S(2)}) copy-start(bf16[128,2048]{1,0:T(8,128)(2,1)S(1)} %collective-permute-done.refs_1_) | copy-start | bytes 1572868
  14.7 11.4 %collective-permute-start.2 = (bf16[128,2048]{1,0:T(8,128)(2,1)S(1)}, bf16[128,2048]{1,0:T(8,128)(2,1)S(1)}, u32[]{:S(2)}, u32[]{:S(2)}) collective-permute-start(bf16[128,2048]{1,0:T(8,128)(2,1)S(1)} %collective-permute-done.refs_1_), channel_id=1, source_target_pairs={{0,1},{16,20},{1,2},{17,21},{2,3},{18,22},{3,0},{19,23},{4,5},{20,... | collective-permute-start | bytes 1572872 | tf_op jit(solution)/shard_map/ppermute | solution.py:333
  14.7 13.4 %collective-permute-start.3 = (bf16[128,2048]{1,0:T(8,128)(2,1)S(1)}, bf16[128,2048]{1,0:T(8,128)(2,1)S(1)}, u32[]{:S(2)}, u32[]{:S(2)}) collective-permute-start(bf16[128,2048]{1,0:T(8,128)(2,1)S(1)} %mask_turn.1.refs_0_), channel_id=1, source_target_pairs={{0,4},{16,17},{1,5},{17,18},{2,6},{18,19},{3,7},{19,16},{4,8},{20,... | collective-permute-start | bytes 1572872 | tf_op jit(solution)/shard_map/ppermute | solution.py:331
  16.0 33.5 %copy-start.9 = (bf16[128,2048]{1,0:T(8,128)(2,1)}, bf16[128,2048]{1,0:T(8,128)(2,1)S(1)}, u32[]{:S(2)}) copy-start(bf16[128,2048]{1,0:T(8,128)(2,1)S(1)} %collective-permute-done.1.refs_2_) | copy-start | bytes 1572868
  16.0 12.4 %collective-permute-start.9 = (bf16[128,2048]{1,0:T(8,128)(2,1)S(1)}, bf16[128,2048]{1,0:T(8,128)(2,1)S(1)}, u32[]{:S(2)}, u32[]{:S(2)}) collective-permute-start(bf16[128,2048]{1,0:T(8,128)(2,1)S(1)} %collective-permute-done.1.refs_2_), channel_id=1, source_target_pairs={{0,12},{16,19},{1,13},{17,16},{2,14},{18,17},{3,15},{19,18},{4,0},... | collective-permute-start | bytes 1572872 | tf_op jit(solution)/shard_map/ppermute | solution.py:336
  20.7 12.7 %collective-permute-start.8 = (bf16[128,2048]{1,0:T(8,128)(2,1)S(1)}, bf16[128,2048]{1,0:T(8,128)(2,1)S(1)}, u32[]{:S(2)}, u32[]{:S(2)}) collective-permute-start(bf16[128,2048]{1,0:T(8,128)(2,1)S(1)} %collective-permute-done.refs_1_), channel_id=1, source_target_pairs={{0,12},{16,19},{1,13},{17,16},{2,14},{18,17},{3,15},{19,18},{4,0},... | collective-permute-start | bytes 1572872 | tf_op jit(solution)/shard_map/ppermute | solution.py:336
  21.7 27.8 %copy-start.14 = (bf16[128,2048]{1,0:T(8,128)(2,1)}, bf16[128,2048]{1,0:T(8,128)(2,1)S(1)}, u32[]{:S(2)}) copy-start(bf16[128,2048]{1,0:T(8,128)(2,1)S(1)} %collective-permute-done.7.refs_4_.refs_8_) | copy-start | bytes 1572868
  21.7 13.7 %collective-permute-start.4 = (bf16[128,2048]{1,0:T(8,128)(2,1)S(1)}, bf16[128,2048]{1,0:T(8,128)(2,1)S(1)}, u32[]{:S(2)}, u32[]{:S(2)}) collective-permute-start(bf16[128,2048]{1,0:T(8,128)(2,1)S(1)} %collective-permute-done.refs_1_), channel_id=1, source_target_pairs={{0,4},{16,17},{1,5},{17,18},{2,6},{18,19},{3,7},{19,16},{4,8},{20,... | collective-permute-start | bytes 1572872 | tf_op jit(solution)/shard_map/ppermute | solution.py:335
  26.1 12.9 %collective-permute-start.10 = (bf16[128,2048]{1,0:T(8,128)(2,1)S(1)}, bf16[128,2048]{1,0:T(8,128)(2,1)S(1)}, u32[]{:S(2)}, u32[]{:S(2)}) collective-permute-start(bf16[128,2048]{1,0:T(8,128)(2,1)S(1)} %collective-permute-done.2.refs_3_), channel_id=1, source_target_pairs={{0,12},{16,19},{1,13},{17,16},{2,14},{18,17},{3,15},{19,18},{4,0},... | collective-permute-start | bytes 1572872 | tf_op jit(solution)/shard_map/ppermute | solution.py:336
  28.1 21.4 %copy-start.16 = (bf16[128,2048]{1,0:T(8,128)(2,1)}, bf16[128,2048]{1,0:T(8,128)(2,1)S(1)}, u32[]{:S(2)}) copy-start(bf16[128,2048]{1,0:T(8,128)(2,1)S(1)} %collective-permute-done.3.refs_0_.refs_4_) | copy-start | bytes 1572868
  28.1 14.3 %collective-permute-start.5 = (bf16[128,2048]{1,0:T(8,128)(2,1)S(1)}, bf16[128,2048]{1,0:T(8,128)(2,1)S(1)}, u32[]{:S(2)}, u32[]{:S(2)}) collective-permute-start(bf16[128,2048]{1,0:T(8,128)(2,1)S(1)} %collective-permute-done.1.refs_2_), channel_id=1, source_target_pairs={{0,4},{16,17},{1,5},{17,18},{2,6},{18,19},{3,7},{19,16},{4,8},{20,... | collective-permute-start | bytes 1572872 | tf_op jit(solution)/shard_map/ppermute | solution.py:335
  28.3 21.2 %copy-start.18 = (bf16[128,2048]{1,0:T(8,128)(2,1)}, bf16[128,2048]{1,0:T(8,128)(2,1)S(1)}, u32[]{:S(2)}) copy-start(bf16[128,2048]{1,0:T(8,128)(2,1)S(1)} %collective-permute-done.9.refs_6_.refs_10_) | copy-start | bytes 1572868
  28.3 18.4 %collective-permute-start.6 = (bf16[128,2048]{1,0:T(8,128)(2,1)S(1)}, bf16[128,2048]{1,0:T(8,128)(2,1)S(1)}, u32[]{:S(2)}, u32[]{:S(2)}) collective-permute-start(bf16[128,2048]{1,0:T(8,128)(2,1)S(1)} %collective-permute-done.2.refs_3_), channel_id=1, source_target_pairs={{0,4},{16,17},{1,5},{17,18},{2,6},{18,19},{3,7},{19,16},{4,8},{20,... | collective-permute-start | bytes 1572872 | tf_op jit(solution)/shard_map/ppermute | solution.py:335
  33.4 21.2 %collective-permute-start.11 = (bf16[128,2048]{1,0:T(8,128)(2,1)S(1)}, bf16[128,2048]{1,0:T(8,128)(2,1)S(1)}, u32[]{:S(2)}, u32[]{:S(2)}) collective-permute-start(bf16[128,2048]{1,0:T(8,128)(2,1)S(1)} %collective-permute-done.3.refs_0_.refs_4_), channel_id=1, source_target_pairs={{0,4},{16,17},{1,5},{17,18},{2,6},{18,19},{3,7},{19,16},{4,8},{20,... | collective-permute-start | bytes 1572872 | tf_op jit(solution)/shard_map/ppermute | solution.py:338
  35.5 14.1 %copy-start.5 = (bf16[128,2048]{1,0:T(8,128)(2,1)}, bf16[128,2048]{1,0:T(8,128)(2,1)S(1)}, u32[]{:S(2)}) copy-start(bf16[128,2048]{1,0:T(8,128)(2,1)S(1)} %collective-permute-done.4.refs_1_.refs_5_) | copy-start | bytes 1572868
  35.5 19.7 %collective-permute-start.14 = (bf16[128,2048]{1,0:T(8,128)(2,1)S(1)}, bf16[128,2048]{1,0:T(8,128)(2,1)S(1)}, u32[]{:S(2)}, u32[]{:S(2)}) collective-permute-start(bf16[128,2048]{1,0:T(8,128)(2,1)S(1)} %collective-permute-done.9.refs_6_.refs_10_), channel_id=1, source_target_pairs={{0,12},{16,19},{1,13},{17,16},{2,14},{18,17},{3,15},{19,18},{4,0},... | collective-permute-start | bytes 1572872 | tf_op jit(solution)/shard_map/ppermute | solution.py:339
  39.0 10.5 %copy-start.20 = (bf16[128,2048]{1,0:T(8,128)(2,1)}, bf16[128,2048]{1,0:T(8,128)(2,1)S(1)}, u32[]{:S(2)}) copy-start(bf16[128,2048]{1,0:T(8,128)(2,1)S(1)} %collective-permute-done.10.refs_7_.refs_11_) | copy-start | bytes 1572868
  39.0 16.2 %collective-permute-start.15 = (bf16[128,2048]{1,0:T(8,128)(2,1)S(1)}, bf16[128,2048]{1,0:T(8,128)(2,1)S(1)}, u32[]{:S(2)}, u32[]{:S(2)}) collective-permute-start(bf16[128,2048]{1,0:T(8,128)(2,1)S(1)} %collective-permute-done.10.refs_7_.refs_11_), channel_id=1, source_target_pairs={{0,12},{16,19},{1,13},{17,16},{2,14},{18,17},{3,15},{19,18},{4,0},... | collective-permute-start | bytes 1572872 | tf_op jit(solution)/shard_map/ppermute | solution.py:339
  42.5 7.1 %copy-start.22 = (bf16[128,2048]{1,0:T(8,128)(2,1)}, bf16[128,2048]{1,0:T(8,128)(2,1)S(1)}, u32[]{:S(2)}) copy-start(bf16[128,2048]{1,0:T(8,128)(2,1)S(1)} %collective-permute-done.5.refs_2_.refs_6_) | copy-start | bytes 1572868
  42.5 12.1 %collective-permute-start.13 = (bf16[64,2048]{1,0:T(8,128)(2,1)S(1)}, bf16[64,2048]{1,0:T(8,128)(2,1)S(1)}, u32[]{:S(2)}, u32[]{:S(2)}) collective-permute-start(bf16[64,2048]{1,0:T(8,128)(2,1)S(1)} %slice.9), channel_id=1, source_target_pairs={{0,12},{16,19},{1,13},{17,16},{2,14},{18,17},{3,15},{19,18},{4,0},... | collective-permute-start | bytes 786440 | tf_op jit(solution)/shard_map/ppermute | solution.py:339
  46.7 2.8 %copy-start.24 = (bf16[128,2048]{1,0:T(8,128)(2,1)}, bf16[128,2048]{1,0:T(8,128)(2,1)S(1)}, u32[]{:S(2)}) copy-start(bf16[128,2048]{1,0:T(8,128)(2,1)S(1)} %collective-permute-done.6.refs_3_.refs_7_) | copy-start | bytes 1572868
  46.7 8.4 %collective-permute-start.12 = (bf16[64,2048]{1,0:T(8,128)(2,1)S(1)}, bf16[64,2048]{1,0:T(8,128)(2,1)S(1)}, u32[]{:S(2)}, u32[]{:S(2)}) collective-permute-start(bf16[64,2048]{1,0:T(8,128)(2,1)S(1)} %slice.8), channel_id=1, source_target_pairs={{0,4},{16,17},{1,5},{17,18},{2,6},{18,19},{3,7},{19,16},{4,8},{20,... | collective-permute-start | bytes 786440 | tf_op jit(solution)/shard_map/ppermute | solution.py:338
  59.4 62.0 %all-to-all-start = ((bf16[16,128,512]{2,1,0:T(8,128)(2,1)}), bf16[16,128,512]{2,1,0:T(8,128)(2,1)S(1)}, u32[]{:S(2)}, u32[]{:S(2)}) async-start(bf16[16,128,512]{2,1,0:T(8,128)(2,1)} %get-tuple-element.13), calls=%async_computation | async-start | bytes 4194304 | tf_op jit(solution)/shard_map/all_to_all | solution.py:357
  82.8 1.6 copy-start.29
  95.0 2.6 %copy-start.2 = (f32[4,512,128]{2,1,0:T(8,128)S(1)}, f32[4,512,128]{2,1,0:T(8,128)}, u32[]{:S(2)}) copy-start(f32[4,512,128]{2,1,0:T(8,128)} %mom_ref.1) | copy-start | bytes 3145732
  99.0 22.4 %copy-start.26 = (s32[16,1]{0,1:T(1,128)S(1)}, s32[16,1]{0,1:T(1,128)}, u32[]{:S(2)}) copy-start(s32[16,1]{0,1:T(1,128)} %param.11) | copy-start | bytes 196
  99.0 22.4 %copy-start.28 = (s32[16,1]{0,1:T(1,128)S(1)}, s32[16,1]{0,1:T(1,128)}, u32[]{:S(2)}) copy-start(s32[16,1]{0,1:T(1,128)} %param.12) | copy-start | bytes 196
  126.4 54.0 %all-to-all-start.1 = ((bf16[16,128,512]{2,1,0:T(8,128)(2,1)}), bf16[16,128,512]{2,1,0:T(8,128)(2,1)}, u32[]{:S(2)}, u32[]{:S(2)}) async-start(bf16[16,128,512]{2,1,0:T(8,128)(2,1)} %copy-done.1), calls=%async_computation.1 | async-start | bytes 4194304 | tf_op jit(solution)/shard_map/all_to_all | solution.py:361
  (18 other events, 19.7 us)
